TPU v7x, 128 devices: a whole 4x4x4 slice. The times are simulated.
128 devices in a mesh: grp: 16 (over z, y_lo, core), dp: 8 (over x, y_hi).
Axes of the slice: x: 4, y: 4 (y_hi: 2, y_lo: 2; y = y_hi * 2 + y_lo), z: 4, core: 2. Of those that a mesh axis runs over, the one named last changes fastest.
Arguments:
- w_qkv: bfloat16 [8192, 768], P('dp'), may hold values from -0.0625 to 0.0625
- qkv_bias: float32 [768], replicated, may hold values from -3 to 3
- w_out: bfloat16 [512, 8192], P('dp'), may hold values from -0.25 to 0.25
- video_x: bfloat16 [8, 2048, 8192], P('dp', 'grp'), may hold values from -30 to 30
- video_pos: int32 [3, 8, 2048], P(None, 'dp', 'grp'), may hold values from 0 to 511
- short_x: bfloat16 [128, 256, 8192], P(('dp', 'grp')), may hold values from -30 to 30
- short_pos: int32 [3, 128, 256], P(None, ('dp', 'grp')), may hold values from 0 to 511
- short_seg: int32 [128, 256], P(('dp', 'grp')), may hold values from 0 to 31, never falling along the last dimension, each value on 1 to 128 neighbouring positions
- video_cot: bfloat16 [8, 2048, 8192], P('dp', 'grp'), may hold values from -0.0390625 to 0.0390625
- short_cot: bfloat16 [128, 256, 8192], P(('dp', 'grp')), may hold values from -0.109375 to 0.109375
Outputs:
- video_y: bfloat16 [8, 2048, 8192], P('dp', 'grp')
- short_y: bfloat16 [128, 256, 8192], P(('dp', 'grp'))
- grad_qkv: float32 [8192, 768], P(('grp', 'dp'))
- grad_out: float32 [512, 8192], P(None, ('grp', 'dp'))
- grad_bias: float32 [768], replicated
Inputs may be any that keep to these rules, and one draw needn't show every extreme that they name: `short_seg`: within each block of 256 rows the sample numbers never fall, and each sample holds 1 to 128 rows.
All inputs are finite; a program needn't handle non-finite values.
Results may differ from a plain program's by a relative error of at most 0.035.
Values may be sent and summed in bfloat16 or wider, within the bound.
No kernel may reach another device: no remote copies, remote signals or barrier semaphores. Data moves between devices by JAX's collectives and lax.ppermute only.
A program may use at most 128 MiB of HBM per device.

v0:
```python
import jax
import jax.numpy as jnp
from jax import lax
from jax.sharding import PartitionSpec as P

HEAD = 128
QH = 4


theta_log = 13.815510557964274


def rope_angles(positions):
    half_dim = HEAD // 2
    freq_index = jnp.arange(half_dim, dtype=jnp.int32)
    inv_freq = jnp.exp(freq_index.astype(jnp.float32) * (-2.0 * theta_log / HEAD))
    first_cut = HEAD // 8
    second_cut = first_cut + 3 * HEAD // 16
    pos_float = positions.astype(jnp.float32)
    chosen_pos = jnp.where(
        (freq_index < first_cut)[None, :],
        pos_float[0][:, None],
        jnp.where((freq_index < second_cut)[None, :], pos_float[1][:, None], pos_float[2][:, None]),
    )
    angles = chosen_pos * inv_freq[None, :]
    return (jnp.cos(angles), jnp.sin(angles))


def rotate(tensor, cosines, sine_vals, direction):
    half_dim = HEAD // 2
    wide_cos = cosines[:, None, :]
    wide_sin = sine_vals[:, None, :] * direction
    front_half = tensor[..., :half_dim]
    back_half = tensor[..., half_dim:]
    return jnp.concatenate(
        [
            front_half * wide_cos - back_half * wide_sin,
            back_half * wide_cos + front_half * wide_sin,
        ],
        axis=-1,
    )


def attend(queries, keys_in, values_in, allowed):
    scores = jnp.einsum(
        "rhe,ke->rhk", queries, keys_in, preferred_element_type=jnp.float32
    ) * HEAD ** (-0.5)
    scores = jnp.where(allowed, scores, -1e30)
    peak_score = jnp.max(scores, axis=-1, keepdims=True)
    weights = jnp.where(allowed, jnp.exp(scores - peak_score), 0.0)
    weight_sum = jnp.sum(weights, axis=-1, keepdims=True)
    probs = weights / weight_sum
    probs_half = probs.astype(jnp.bfloat16)
    attended = jnp.einsum(
        "rhk,ke->rhe", probs_half, values_in, preferred_element_type=jnp.float32
    ).astype(jnp.bfloat16)
    return (attended, probs, probs_half, peak_score, weight_sum)


def per_device(
    w_qkv, qkv_bias, w_out, video_x, video_pos, short_x, short_pos, short_seg, video_cot, short_cot
):
    qkv_whole, out_whole = (
        lax.all_gather(w_qkv, "dp", axis=0, tiled=True),
        lax.all_gather(w_out, "dp", axis=0, tiled=True),
    )
    long_count = video_x.shape[1]
    short_count = short_x.shape[1]
    row_count = long_count + short_count
    att_width = QH * HEAD
    score_scale = HEAD ** (-0.5)
    tokens = jnp.concatenate([video_x[0], short_x[0]], axis=0)
    places = jnp.concatenate([video_pos[:, 0, :], short_pos[:, 0, :]], axis=1)
    cotangent = jnp.concatenate([video_cot[0], short_cot[0]], axis=0)
    projected = jnp.dot(tokens, qkv_whole, preferred_element_type=jnp.float32) + qkv_bias[None, :]
    cosines, sine_vals = rope_angles(places)
    queries = rotate(
        projected[:, :att_width].reshape(row_count, QH, HEAD), cosines, sine_vals, 1.0
    ).astype(jnp.bfloat16)
    key_local = rotate(
        projected[:, att_width : att_width + HEAD].reshape(row_count, 1, HEAD),
        cosines,
        sine_vals,
        1.0,
    )[:, 0].astype(jnp.bfloat16)
    value_local = projected[:, att_width + HEAD :].astype(jnp.bfloat16)
    keys_group, values_group = (
        lax.all_gather(key_local[:long_count], "grp", axis=0, tiled=True),
        lax.all_gather(value_local[:long_count], "grp", axis=0, tiled=True),
    )
    first_row = lax.axis_index("grp") * long_count
    key_count = keys_group.shape[0]
    query_at = first_row + jnp.arange(long_count, dtype=jnp.int32)
    video_allowed = (jnp.arange(key_count, dtype=jnp.int32)[None, :] <= query_at[:, None])[
        :, None, :
    ]
    position = jnp.arange(short_count, dtype=jnp.int32)
    segment = short_seg[0]
    short_allowed = (
        (segment[None, :] == segment[:, None]) & (position[None, :] <= position[:, None])
    )[:, None, :]
    video_queries = queries[:long_count]
    short_queries = queries[long_count:]
    short_keys = key_local[long_count:]
    short_values = value_local[long_count:]
    video_att, video_probs, video_half, video_peak, video_total = attend(
        video_queries, keys_group, values_group, video_allowed
    )
    short_att, short_probs, short_half, short_peak, short_total = attend(
        short_queries, short_keys, short_values, short_allowed
    )
    attended = jnp.concatenate([video_att, short_att], axis=0)
    flat_out = attended.reshape(row_count, att_width)
    layer_out = jnp.dot(flat_out, out_whole, preferred_element_type=jnp.float32).astype(
        jnp.bfloat16
    )
    grad_attended = lax.dot_general(
        cotangent, out_whole, (((1,), (1,)), ((), ())), preferred_element_type=jnp.float32
    ).astype(jnp.bfloat16)
    term_output = lax.dot_general(
        flat_out, cotangent, (((0,), (0,)), ((), ())), preferred_element_type=jnp.float32
    )
    grad_heads = grad_attended.reshape(row_count, QH, HEAD)
    deltas = jnp.sum(grad_heads.astype(jnp.float32) * attended.astype(jnp.float32), axis=-1)
    video_grad = grad_heads[:long_count]
    video_delta = deltas[:long_count]
    video_dprob = jnp.einsum(
        "rhe,ke->rhk", video_grad, values_group, preferred_element_type=jnp.float32
    )
    video_dscore = (video_probs * (video_dprob - video_delta[..., None]) * score_scale).astype(
        jnp.bfloat16
    )
    video_dquery = jnp.einsum(
        "rhk,ke->rhe", video_dscore, keys_group, preferred_element_type=jnp.float32
    )
    grad_keys = jnp.einsum(
        "rhk,rhe->ke", video_dscore, video_queries, preferred_element_type=jnp.float32
    )
    grad_values = jnp.einsum(
        "rhk,rhe->ke", video_half, video_grad, preferred_element_type=jnp.float32
    )
    key_value_grads = lax.psum_scatter(
        jnp.concatenate([grad_keys, grad_values], axis=1), "grp", scatter_dimension=0, tiled=True
    )
    video_dkey = key_value_grads[:, :HEAD]
    video_dvalue = key_value_grads[:, HEAD:]
    short_grad = grad_heads[long_count:]
    short_delta = deltas[long_count:]
    short_dprob = jnp.einsum(
        "rhe,ke->rhk", short_grad, short_values, preferred_element_type=jnp.float32
    )
    short_dscore = (short_probs * (short_dprob - short_delta[..., None]) * score_scale).astype(
        jnp.bfloat16
    )
    short_dquery = jnp.einsum(
        "rhk,ke->rhe", short_dscore, short_keys, preferred_element_type=jnp.float32
    )
    short_dkey = jnp.einsum(
        "rhk,rhe->ke", short_dscore, short_queries, preferred_element_type=jnp.float32
    )
    short_dvalue = jnp.einsum(
        "rhk,rhe->ke", short_half, short_grad, preferred_element_type=jnp.float32
    )
    grad_queries = rotate(
        jnp.concatenate([video_dquery, short_dquery], axis=0), cosines, sine_vals, -1.0
    )
    grad_keys_all = rotate(
        jnp.concatenate([video_dkey, short_dkey], axis=0)[:, None, :], cosines, sine_vals, -1.0
    )[:, 0]
    grad_values_all = jnp.concatenate([video_dvalue, short_dvalue], axis=0)
    grad_projected = jnp.concatenate(
        [grad_queries.reshape(row_count, att_width), grad_keys_all, grad_values_all], axis=1
    )
    bias_term = jnp.sum(grad_projected, axis=0)
    grad_rows = grad_projected.astype(jnp.bfloat16)
    term_proj = lax.dot_general(
        tokens, grad_rows, (((0,), (0,)), ((), ())), preferred_element_type=jnp.float32
    )
    grad_bias = lax.psum(bias_term, ("grp", "dp"))
    proj_part, output_part = (
        lax.psum_scatter(
            term_proj.astype(jnp.bfloat16), "grp", scatter_dimension=0, tiled=True
        ).astype(jnp.float32),
        lax.psum_scatter(
            term_output.astype(jnp.bfloat16), "grp", scatter_dimension=1, tiled=True
        ).astype(jnp.float32),
    )
    grad_qkv, grad_out = (
        lax.psum_scatter(proj_part, "dp", scatter_dimension=0, tiled=True),
        lax.psum_scatter(output_part, "dp", scatter_dimension=1, tiled=True),
    )
    return (
        layer_out[:long_count][None],
        layer_out[long_count:][None],
        grad_qkv,
        grad_out,
        grad_bias,
    )


def solution(mesh):
    return jax.shard_map(
        per_device,
        mesh=mesh,
        in_specs=(
            P("dp", None),
            P(),
            P("dp", None),
            P("dp", "grp", None),
            P(None, "dp", "grp"),
            P(("dp", "grp"), None, None),
            P(None, ("dp", "grp"), None),
            P(("dp", "grp"), None),
            P("dp", "grp", None),
            P(("dp", "grp"), None, None),
        ),
        out_specs=(
            P("dp", "grp", None),
            P(("dp", "grp"), None, None),
            P(("grp", "dp"), None),
            P(None, ("grp", "dp")),
            P(),
        ),
        check_vma=False,
    )
```

profile of v0, /device:TPU:0, one launch (start us, length us, event | category | flops | bytes accessed | tf_op | source)
XLA Modules:
  0.0 803.5 jit_solution(12445562711263912727)
XLA Ops:
  7.2 0.7 all-gather.6.cloned.1.call-update
  7.9 0.7 all-gather.4.cloned.1.call-update
  8.7 0.7 copy.96
  9.4 0.7 copy.97
  10.2 0.9 fusion.36
  11.0 1.8 broadcast_multiply_fusion
  12.8 0.9 iota_compare_fusion
  13.7 108.0 %all-gather.6.cloned.1.call-done = bf16[512,8192]{1,0:T(8,128)(2,1)} async-done(((bf16[64,8192]{1,0:T(8,128)(2,1)}), bf16[512,8192]{1,0:T(8,128)(2,1)}) %all-gather.6.cloned.1.call-update) | async-done | bytes 8388624 | tf_op jit(solution)/shard_map/all_gather | solution.py:65
  121.7 8.7 %fusion.17 = bf16[384,512]{1,0:T(8,128)(2,1)S(1)} fusion(bf16[512,8192]{1,0:T(8,128)(2,1)} %all-gather.6.cloned.1.call-done, bf16[256,8192]{1,0:T(8,128)(2,1)} %bitcast.103, bf16[128,8192]{1,0:T(8,128)(2,1)} %bitcast.107), kind=kOutput, calls=%fused_computation.33 | convolution fusion | flops 3234004992 | bytes 15073280 | tf_op jit(solution)/shard_map/dot_general | solution.py:117
  130.6 0.5 copy-done.9
  131.4 0.8 copy.80
  132.2 137.2 %all-gather.4.cloned.1.call-done = bf16[8192,768]{1,0:T(8,128)(2,1)} async-done(((bf16[1024,768]{1,0:T(8,128)(2,1)}), bf16[8192,768]{1,0:T(8,128)(2,1)}) %all-gather.4.cloned.1.call-update) | async-done | bytes 12582928 | tf_op jit(solution)/shard_map/all_gather | solution.py:64
  269.4 12.3 %fusion.60 = (bf16[384,768]{1,0:T(8,128)(2,1)}, f32[384,768]{1,0:T(8,128)S(1)}) fusion(f32[768]{0:T(1024)S(1)} %copy-done.25, bf16[8192,768]{1,0:T(8,128)(2,1)} %all-gather.4.cloned.1.call-done, bf16[256,8192]{1,0:T(8,128)(2,1)} %bitcast.105, bf16[128,8192]{1,0:T(8,128)(2,1)} %bitcast.109), kind=kOutput, calls=%fused_computation.114 | convolution fusion | flops 4845010944 | bytes 20646912 | tf_op jit(solution)/shard_map/dot_general | solution.py:75
  282.1 0.5 fusion.57
  283.1 1.1 subtract_convert_fusion.1
  284.4 21.2 %all-gather = bf16[2048,1,128]{2,0,1:T(8,128)(2,1)S(1)} all-gather(bf16[128,1,128]{2,0,1:T(8,128)(2,1)S(1)} %pad_maximum_fusion.19), channel_id=2, replica_groups=mesh['grp'=16,'dp'=8] {'grp'}, dimensions={0}, use_global_device_ids=true | all-gather | bytes 557056 | tf_op jit(solution)/shard_map/all_gather | solution.py:88
  305.6 0.8 slice.134
  306.4 18.7 %all_gather.14 = bf16[2048,128]{1,0:T(8,128)(2,1)S(1)} all-gather(bf16[128,128]{1,0:T(8,128)(2,1)S(1)} %slice.134), channel_id=1, replica_groups=mesh['grp'=16,'dp'=8] {'grp'}, dimensions={0}, use_global_device_ids=true | all-gather | bytes 557056 | tf_op jit(solution)/shard_map/all_gather | solution.py:89
  325.1 1.5 fusion.59
  326.6 1.3 fusion.33
  328.0 1.2 convolution_convert_fusion.3
  329.2 4.0 fusion.61
  333.2 0.6 copy-done.23
  333.7 2.8 fusion.8
  336.6 0.7 convolution_convert_fusion.4
  337.6 0.6 copy-done.16
  338.2 0.7 convolution_bitcast_fusion
  338.9 1.1 multiply_convert_fusion
  340.0 0.7 convolution_bitcast_fusion.1
  340.8 1.5 pad_maximum_fusion.6
  342.3 0.9 copy.50
  343.3 10.8 %convolution_convert_fusion.1 = bf16[512,8192]{1,0:T(8,128)(2,1)} fusion(bf16[384,512]{0,1:T(8,128)(2,1)} %bitcast.96, bf16[256,8192]{1,0:T(8,128)(2,1)} %bitcast.104, bf16[128,8192]{1,0:T(8,128)(2,1)} %bitcast.108), kind=kOutput, calls=%fused_computation.3 | convolution fusion | flops 3238002688 | bytes 15073280 | tf_op jit(solution)/shard_map/dot_general | solution.py:120
  354.8 1.7 fusion.16
  356.8 0.7 fusion.27
  358.8 1.2 convolution_bitcast_fusion.2
  360.1 43.8 %reduce-scatter.8.cloned.1.call-done = f32[128,256]{1,0:T(8,128)} async-done(((f32[2048,256]{1,0:T(8,128)}), f32[128,256]{1,0:T(8,128)}) %reduce-scatter.8.cloned.1.call-update) | async-done | bytes 131088 | tf_op jit(solution)/shard_map/reduce_scatter | solution.py:142
  403.8 0.9 fusion.58
  404.8 1.1 multiply_subtract_fusion.1
  406.3 12.5 %convolution_convert_fusion = bf16[8192,768]{1,0:T(8,128)(2,1)} fusion(bf16[256,8192]{1,0:T(8,128)(2,1)} %bitcast.106, bf16[128,8192]{1,0:T(8,128)(2,1)} %bitcast.110, f32[384,128]{0,1:T(8,128)S(1)} %copy.64, f32[384,128]{0,1:T(8,128)S(1)} %copy.63, f32[384,512]{0,1:T(8,128)S(1)} %bitcast.93), kind=kOutput, calls=%fused_computation.2 | convolution fusion | flops 4852482048 | bytes 20054016 | tf_op jit(solution)/shard_map/dot_general | solution.py:176
  418.9 84.0 %reduce-scatter.14.cloned.1.call-done = bf16[512,512]{1,0:T(8,128)(2,1)} async-done(((bf16[512,8192]{1,0:T(8,128)(2,1)}), bf16[512,512]{1,0:T(8,128)(2,1)}) %reduce-scatter.14.cloned.1.call-update) | async-done | bytes 524304 | tf_op jit(solution)/shard_map/reduce_scatter | solution.py:184
  502.8 2.2 copy.74
  505.1 9.5 %convolution_convert_fusion.2 = bf16[384,8192]{1,0:T(8,128)(2,1)} fusion(bf16[384,512]{0,1:T(8,128)(2,1)S(1)} %bitcast.97, bf16[512,8192]{1,0:T(8,128)(2,1)} %all-gather.6.cloned.1.call-done), kind=kOutput, calls=%fused_computation.4 | convolution fusion | flops 3224371200 | bytes 15073280 | tf_op jit(solution)/shard_map/dot_general | solution.py:114
  514.6 129.3 %reduce-scatter.10.cloned.1.call-done = bf16[512,768]{1,0:T(8,128)(2,1)} async-done(((bf16[8192,768]{1,0:T(8,128)(2,1)}), bf16[512,768]{1,0:T(8,128)(2,1)}) %reduce-scatter.10.cloned.1.call-update) | async-done | bytes 786448 | tf_op jit(solution)/shard_map/reduce_scatter | solution.py:181
  644.0 2.4 convert_element_type.79
  646.4 3.1 slice_bitcast_fusion.1
  649.5 4.6 slice_bitcast_fusion
  654.3 65.3 %psum.7 = f32[768]{0:T(1024)} all-reduce(f32[768]{0:T(1024)S(1)} %fusion.18), channel_id=1, replica_groups=mesh['grp'=16,'dp'=8] {'grp','dp'}, use_global_device_ids=true, to_apply=%region_11.12 | all-reduce | flops 768 | bytes 6144 | tf_op jit(solution)/shard_map/psum | solution.py:179
  719.6 77.1 %reduce-scatter.12.cloned.1.call-done = f32[64,768]{1,0:T(8,128)} async-done(((f32[512,768]{1,0:T(8,128)}), f32[64,768]{1,0:T(8,128)}) %reduce-scatter.12.cloned.1.call-update) | async-done | bytes 196624 | tf_op jit(solution)/shard_map/reduce_scatter | solution.py:189
  (93 shorter events, 5.0 us)
Async XLA Ops:
  7.2 114.5 %all-gather.6.cloned.1.call-start = ((), (), s32[]{:S(2)}) async-start(), calls=%async_computation.6 | async-start | bytes 9437184 | tf_op jit(solution)/shard_map/all_gather | solution.py:65
  7.9 261.5 %all-gather.4.cloned.1.call-start = ((), (), s32[]{:S(2)}) async-start(), calls=%async_computation.5 | async-start | bytes 14155776 | tf_op jit(solution)/shard_map/all_gather | solution.py:64
  8.6 395.2 %reduce-scatter.8.cloned.1.call-start = ((), (), s32[]{:S(2)}) async-start(), calls=%async_computation.7 | async-start | bytes 2228224 | tf_op jit(solution)/shard_map/reduce_scatter | solution.py:142
  10.1 272.9 %copy-start.17 = (pred[64]{0:T(512)(128)(4,1)}, pred[64]{0:T(512)(128)(4,1)S(1)}, u32[]{:S(2)}) copy-start(pred[64]{0:T(512)(128)(4,1)S(1)} %get-tuple-element.44) | copy-start | bytes 196
  10.1 272.9 %copy-start.19 = (pred[64]{0:T(512)(128)(4,1)}, pred[64]{0:T(512)(128)(4,1)S(1)}, u32[]{:S(2)}) copy-start(pred[64]{0:T(512)(128)(4,1)S(1)} %get-tuple-element.45) | copy-start | bytes 196
  12.8 269.8 %copy-start.3 = (f32[384,64]{1,0:T(8,128)}, f32[384,64]{1,0:T(8,128)S(1)}, u32[]{:S(2)}) copy-start(f32[384,64]{1,0:T(8,128)S(1)} %get-tuple-element.37) | copy-start | bytes 294916
  121.7 147.7 %copy-start.25 = (f32[768]{0:T(1024)S(1)}, f32[768]{0:T(1024)}, u32[]{:S(2)}) copy-start(f32[768]{0:T(1024)} %param.11) | copy-start | bytes 9220
  130.4 0.7 copy-start.9
  282.9 50.3 %copy-start.10 = (bf16[128,4,128]{2,0,1:T(8,128)(2,1)}, bf16[128,4,128]{2,0,1:T(8,128)(2,1)S(1)}, u32[]{:S(2)}) copy-start(bf16[128,4,128]{2,0,1:T(8,128)(2,1)S(1)} %pad_maximum_fusion.17) | copy-start | bytes 393220
  282.9 46.3 %copy-start.13 = (pred[128,2048]{1,0:T(8,128)(4,1)S(1)}, pred[128,2048]{1,0:T(8,128)(4,1)}, u32[]{:S(2)}) copy-start(pred[128,2048]{1,0:T(8,128)(4,1)} %iota_compare_fusion) | copy-start | bytes 786436
  283.1 43.6 %copy-start.6 = (bf16[256,4,128]{2,0,1:T(8,128)(2,1)}, bf16[256,4,128]{2,0,1:T(8,128)(2,1)S(1)}, u32[]{:S(2)}) copy-start(bf16[256,4,128]{2,0,1:T(8,128)(2,1)S(1)} %pad_maximum_fusion.15) | copy-start | bytes 786436
  284.4 48.8 %copy-start.14 = (bf16[256,128,1]{1,0,2:T(8,128)(2,1)}, bf16[256,128,1]{1,0,2:T(8,128)(2,1)S(1)}, u32[]{:S(2)}) copy-start(bf16[256,128,1]{1,0,2:T(8,128)(2,1)S(1)} %fusion.44) | copy-start | bytes 196612
  305.6 27.5 %copy-start.1 = (bf16[2048,1,128]{2,0,1:T(8,128)(2,1)}, bf16[2048,1,128]{2,0,1:T(8,128)(2,1)S(1)}, u32[]{:S(2)}) copy-start(bf16[2048,1,128]{2,0,1:T(8,128)(2,1)S(1)} %all-gather) | copy-start | bytes 1572868
  326.6 6.5 copy-start.21
  333.1 0.6 copy-start.23
  333.7 4.5 copy-start.12
  336.6 2.4 copy-start
  336.6 2.4 copy-start.24
  337.6 0.6 copy-start.16
  338.9 1.1 copy-start.11
  342.3 160.6 %reduce-scatter.14.cloned.1.call-start = ((), (), s32[]{:S(2)}) async-start(), calls=%async_computation.10 | async-start | bytes 8912896 | tf_op jit(solution)/shard_map/reduce_scatter | solution.py:184
  354.1 0.7 slice-start
  354.1 0.7 copy-start.22
  354.1 2.4 copy-start.15
  354.1 289.9 %reduce-scatter.10.cloned.1.call-start = ((), (), s32[]{:S(2)}) async-start(), calls=%async_computation.8 | async-start | bytes 13369344 | tf_op jit(solution)/shard_map/reduce_scatter | solution.py:181
  354.4 2.5 copy-start.2
  354.8 2.8 copy-start.4
  354.8 2.8 copy-start.8
  357.6 1.0 copy-start.7
  357.6 47.1 %copy-start.18 = (pred[64]{0:T(512)(128)(4,1)S(1)}, pred[64]{0:T(512)(128)(4,1)}, u32[]{:S(2)}) copy-start(pred[64]{0:T(512)(128)(4,1)} %copy-done.17) | copy-start | bytes 196
  357.6 47.1 %copy-start.20 = (pred[64]{0:T(512)(128)(4,1)S(1)}, pred[64]{0:T(512)(128)(4,1)}, u32[]{:S(2)}) copy-start(pred[64]{0:T(512)(128)(4,1)} %copy-done.19) | copy-start | bytes 196
  418.8 86.3 %copy-start.5 = (bf16[384,4,128]{0,2,1:T(8,128)(2,1)S(1)}, bf16[384,4,128]{0,2,1:T(8,128)(2,1)}, u32[]{:S(2)}) copy-start(bf16[384,4,128]{0,2,1:T(8,128)(2,1)} %copy.50) | copy-start | bytes 1179652
  418.8 300.8 %reduce-scatter.16.cloned.1.call-start = ((), (), s32[]{:S(2)}) async-start(), calls=%async_computation.11 | async-start | bytes 1179648
  505.1 291.6 %reduce-scatter.12.cloned.1.call-start = ((), (), s32[]{:S(2)}) async-start(), calls=%async_computation.9 | async-start | bytes 1769472 | tf_op jit(solution)/shard_map/reduce_scatter | solution.py:189
Sparse Core Ops, SparseCore 0:
  10.3 111.3 all-gather.5
  124.0 145.3 all-gather.3
  342.4 61.4 reduce-scatter.7
  406.1 96.6 reduce-scatter.13
  505.1 138.8 reduce-scatter.9
  648.0 70.6 reduce-scatter.15
  723.5 73.1 reduce-scatter.11
where the time goes:
time: 804 us
  waiting for transfers between devices  581 us (72%)
  blocking collectives  105 us (13%)
  matrix products  68 us (8%)
  local copies, waits for them, and re-layouts  18.6 us (2%)
  other arithmetic  15.7 us (2%)
  between operations  14.7 us (2%)
    all_gather x1, waiting for transfers between devices, per_device(): lax.all_gather(w_qkv, 'dp', axis=0, tiled=True)  137 us
    reduce_scatter x1, waiting for transfers between devices, per_device(): lax.psum_scatter(term_proj.astype(jnp.bfloat16), 'grp', scatter_dimension...  129 us
    all_gather x1, waiting for transfers between devices, per_device(): lax.all_gather(w_out, 'dp', axis=0, tiled=True)  108 us
    reduce_scatter x1, waiting for transfers between devices, per_device(): lax.psum_scatter(term_output.astype(jnp.bfloat16), 'grp', scatter_dimensi...  84 us
    reduce_scatter x1, waiting for transfers between devices, per_device(): lax.psum_scatter(proj_part, 'dp', scatter_dimension=0, tiled=True)  77.1 us
    psum x1, blocking collectives, per_device(): grad_bias = lax.psum(bias_term, ('grp', 'dp'))  65.3 us
    reduce_scatter x1, waiting for transfers between devices, per_device(): lax.psum_scatter(jnp.concatenate([grad_keys, grad_values], axis=1), 'grp'...  43.8 us
    all_gather x1, blocking collectives, per_device(): lax.all_gather(key_local[:long_count], 'grp', axis=0, tiled=True)  21.2 us
  transfers between devices with their start and end apart: 7, of which 6 were waited for; matrix products, arithmetic and copies ran while one was open for 9% of the time, Pallas kernels for 0%

commit v1 on v0

v1 whole, which is shorter than its diff:
```python
import functools

import jax
import jax.numpy as jnp
from jax import lax
from jax.experimental import pallas as pl
from jax.experimental.pallas import tpu as pltpu
from jax.sharding import Mesh
from jax.sharding import PartitionSpec as P

HEAD = 128
QH = 4
ATT = QH * HEAD
AXES = ("z", "yl", "c", "x", "yh")
SIZES = (4, 2, 2, 4, 2)
GRP = ("z", "yl", "c")
DP = ("x", "yh")
BF = jnp.bfloat16
F32 = jnp.float32
THETA_LOG = 13.815510557964274


def device_index(z, y, c, x):
    z, y, c, x = z % 4, y % 4, c % 2, x % 4
    return (((z * 2 + y % 2) * 2 + c) * 4 + x) * 2 + y // 2


def pairs(target):
    result = []
    for z in range(4):
        for y in range(4):
            for c in range(2):
                for x in range(4):
                    result.append((device_index(z, y, c, x), device_index(*target(z, y, c, x))))
    return result


def move(value, target):
    return lax.ppermute(value, AXES, pairs(target))


def other_core(value):
    return move(value, lambda z, y, c, x: (z, y, c + 1, x))


def to_x(value, step):
    return move(value, lambda z, y, c, x: (z, y, c, x + step))


def to_z(value, step):
    return move(value, lambda z, y, c, x: (z + step, y, c, x))


def to_y(value, step):
    return move(value, lambda z, y, c, x: (z, y + step, c, x))


def across(value):
    return move(value, lambda z, y, c, x: (z, 3 - y, c, x))


def to_first(value, step):
    return move(
        value, lambda z, y, c, x: (z + step, y, c, x) if c == 0 else (z, y, c, x + step)
    )


def to_second(value, step):
    return move(
        value, lambda z, y, c, x: (z, y, c, x + step) if c == 0 else (z + step, y, c, x)
    )


def params(limit=48):
    return pltpu.CompilerParams(vmem_limit_bytes=limit * 1024 * 1024)


def halves_kernel(core_ref, a0, b0, a1, b1, mine, theirs):
    n = a0.shape[0]
    first = core_ref[0] == 0

    @pl.when(first)
    def _():
        mine[:n] = a0[...]
        mine[n:] = b0[...]
        theirs[:n] = a1[...]
        theirs[n:] = b1[...]

    @pl.when(jnp.logical_not(first))
    def _():
        mine[:n] = a1[...]
        mine[n:] = b1[...]
        theirs[:n] = a0[...]
        theirs[n:] = b0[...]


def column_halves(core, video, short):
    rows = video.shape[0] + short.shape[0]
    spec = lambda n, k: pl.BlockSpec((n, 512), lambda j, s: (0, 2 * j + k))
    out = pl.BlockSpec((rows, 512), lambda j, s: (0, j))
    shape = jax.ShapeDtypeStruct((rows, 4096), BF)
    nv, ns = video.shape[0], short.shape[0]
    return pl.pallas_call(
        halves_kernel,
        grid_spec=pltpu.PrefetchScalarGridSpec(
            num_scalar_prefetch=1,
            grid=(8,),
            in_specs=[spec(nv, 0), spec(ns, 0), spec(nv, 1), spec(ns, 1)],
            out_specs=[out, out],
        ),
        out_shape=[shape, shape],
        compiler_params=params(),
        name="column_halves",
    )(core, video, short, video, short)


def weight_half_kernel(core_ref, block, result):
    result[0] = block[...]


def weight_half(core, w):
    return pl.pallas_call(
        weight_half_kernel,
        grid_spec=pltpu.PrefetchScalarGridSpec(
            num_scalar_prefetch=1,
            grid=(8,),
            in_specs=[pl.BlockSpec((64, 512), lambda j, s: (0, 2 * j + s[0]))],
            out_specs=pl.BlockSpec((1, 64, 512), lambda j, s: (j, 0, 0)),
        ),
        out_shape=jax.ShapeDtypeStruct((8, 64, 512), BF),
        compiler_params=params(),
        name="weight_half",
    )(core, w)


def put(buffer, piece, *index):
    index = tuple(index) + (0,) * (buffer.ndim - len(index))
    return lax.dynamic_update_slice(buffer, piece, index)


def ring(pair, mover, position):
    got = [(position, pair)]
    for step in (1, 3, 2):
        got.append(((position + 4 - step) % 4, mover(pair, step)))
    return got


def gather(lower, upper, at):
    m, n = lower.shape[1:]
    x, yh, z = at["x"], at["yh"], at["z"]
    whole = jnp.zeros((4, 2, 8, m, n), BF)
    quarter = lax.dynamic_slice(upper, (z, 0, 0), (1, m, n))
    pair_q = jnp.stack([quarter, across(quarter)])
    pair_l = jnp.stack([lower, across(lower)])
    block = jnp.zeros((4, 2, 1, m, n), BF)
    for place, pair in ring(pair_q, to_x, x):
        block = put(block, pair[0][None, None], place, yh)
        block = put(block, pair[1][None, None], place, 1 - yh)
    for place, pair in ring(pair_l, to_x, x):
        whole = put(whole, pair[0][None, None], place, yh)
        whole = put(whole, pair[1][None, None], place, 1 - yh)
    for place, got in ring(block, to_z, z):
        whole = put(whole, got, 0, 0, 4 + place)
    return whole.reshape(8, 8, m, n)


def grad_attended_kernel(cot, w, total):
    @pl.when(pl.program_id(0) == 0)
    def _():
        total[...] = jnp.zeros_like(total)

    total[...] += lax.dot_general(
        cot[...], w[0], (((1,), (1,)), ((), ())), preferred_element_type=F32
    )


def grad_attended_part(cot, w):
    rows = cot.shape[0]
    return pl.pallas_call(
        grad_attended_kernel,
        grid=(8,),
        in_specs=[
            pl.BlockSpec((rows, 512), lambda j: (0, j)),
            pl.BlockSpec((1, 512, 512), lambda j: (j, 0, 0)),
        ],
        out_specs=pl.BlockSpec((rows, 512), lambda j: (0, 0)),
        out_shape=jax.ShapeDtypeStruct((rows, 512), F32),
        compiler_params=params(),
        cost_estimate=pl.CostEstimate(
            flops=2 * rows * 4096 * 512, bytes_accessed=rows * 8192 + 4096 * 1024, transcendentals=0
        ),
        name="grad_attended",
    )(cot, w)


def layer_out_kernel(core_ref, att, mine, theirs, video, short):
    n = video.shape[0]
    own = jnp.dot(att[...], mine[0], preferred_element_type=F32).astype(BF)
    other = jnp.dot(att[...], theirs[0], preferred_element_type=F32).astype(BF)
    first = core_ref[0] == 0

    @pl.when(first)
    def _():
        video[:, :512] = own[:n]
        short[:, :512] = own[n:]
        video[:, 512:] = other[:n]
        short[:, 512:] = other[n:]

    @pl.when(jnp.logical_not(first))
    def _():
        video[:, :512] = other[:n]
        short[:, :512] = other[n:]
        video[:, 512:] = own[:n]
        short[:, 512:] = own[n:]


def layer_out(core, att, mine, theirs, nv, ns):
    w = pl.BlockSpec((1, 512, 512), lambda j, s: (j, 0, 0))
    return pl.pallas_call(
        layer_out_kernel,
        grid_spec=pltpu.PrefetchScalarGridSpec(
            num_scalar_prefetch=1,
            grid=(8,),
            in_specs=[pl.BlockSpec((nv + ns, 512), lambda j, s: (0, 0)), w, w],
            out_specs=[
                pl.BlockSpec((nv, 1024), lambda j, s: (0, j)),
                pl.BlockSpec((ns, 1024), lambda j, s: (0, j)),
            ],
        ),
        out_shape=[jax.ShapeDtypeStruct((nv, 8192), BF), jax.ShapeDtypeStruct((ns, 8192), BF)],
        compiler_params=params(),
        cost_estimate=pl.CostEstimate(
            flops=2 * 384 * 8192 * 512, bytes_accessed=16 * 1024 * 1024, transcendentals=0
        ),
        name="layer_out",
    )(core, att, mine, theirs)


TAIL = 16


def term_kernel(tab, *refs, received, bias):
    xa, xb = refs[0:2], refs[2:4]
    ga, gb = refs[4:6]
    got = refs[6 : 6 + received]
    out = refs[-1]
    step = pl.program_id(0)
    n = ga.shape[1]
    dims = (((0,), (0,)), ((), ()))
    left = jnp.concatenate([xa[0][...], xa[1][...]], axis=1)
    total = lax.dot_general(left, ga[...], dims, preferred_element_type=F32)
    left = jnp.concatenate([xb[0][...], xb[1][...]], axis=1)
    total += lax.dot_general(left, gb[...], dims, preferred_element_type=F32)
    for k in range(4):
        where = pl.ds(pl.multiple_of(step * 256 + tab[9 + k] * 64, 64), 64)
        piece = total[k * 64 : (k + 1) * 64]
        for ref in got:
            piece += ref[where, :].astype(F32)
        out[where, :] = piece.astype(BF)

    @pl.when(step == 0)
    def _():
        if bias:
            row = jnp.sum(ga[...].astype(F32), axis=0, keepdims=True)
            row += jnp.sum(gb[...].astype(F32), axis=0, keepdims=True)
            for ref in got:
                row += jnp.sum(ref[1024:, :].astype(F32), axis=0, keepdims=True)
            high = row.astype(BF).astype(F32)
            index = lax.broadcasted_iota(jnp.int32, (TAIL, n), 0)
            out[1024:, :] = jnp.where(
                index == 0, high, jnp.where(index == 1, row - high, 0.0)
            ).astype(BF)
        else:
            out[1024:, :] = jnp.zeros((TAIL, n), BF)


def term_chunk(tab, x_own, x_other, g_own, g_other, got, bias, name):
    rows, n = g_own.shape
    x_spec = lambda k: pl.BlockSpec((rows, 128), lambda j, s: (0, s[2 * j + k]))
    whole = lambda shape: pl.BlockSpec(shape, lambda j, s: (0, 0))
    return pl.pallas_call(
        functools.partial(term_kernel, received=len(got), bias=bias),
        grid_spec=pltpu.PrefetchScalarGridSpec(
            num_scalar_prefetch=1,
            grid=(4,),
            in_specs=[x_spec(0), x_spec(1), x_spec(0), x_spec(1), whole((rows, n)), whole((rows, n))]
            + [whole((1024 + TAIL, n))] * len(got),
            out_specs=whole((1024 + TAIL, n)),
        ),
        out_shape=jax.ShapeDtypeStruct((1024 + TAIL, n), BF),
        compiler_params=params(),
        cost_estimate=pl.CostEstimate(
            flops=2 * 2 * rows * 1024 * n, bytes_accessed=4 * rows * 1024 + 4 * rows * n + 2048 * n,
            transcendentals=0,
        ),
        name=name,
    )(tab, x_own, x_own, x_other, x_other, g_own, g_other, *got)


def tables(at):
    core, z, x = at["c"], at["z"], at["x"]
    y = at["yh"] * 2 + at["yl"]
    result = []
    for far in range(4):
        entries = []
        for step in range(4):
            for yl in range(2):
                zero = (((z + far) % 4) * 2 + yl) * 4 + (x + step) % 4
                one = (((z + step) % 4) * 2 + yl) * 4 + (x + far) % 4
                entries.append(jnp.where(core == 0, zero, one))
        entries.append(jnp.int32(0))
        for yl in range(2):
            for yh in range(2):
                entries.append((yh * 2 + yl - y + 4) % 4)
        result.append(jnp.stack([jnp.asarray(e, jnp.int32) for e in entries]))
    return result


def split_tail(rows):
    high = lax.reduce_precision(rows, 8, 7)
    n = rows.shape[1]
    return jnp.concatenate(
        [high.astype(BF), (rows - high).astype(BF), jnp.zeros((TAIL - 2, n), BF)], axis=0
    )


def fold(parts, chunk, tail):
    total = sum(p[:chunk].astype(F32) for p in parts)
    bias = sum(jnp.sum(p[chunk:].astype(F32), axis=0, keepdims=True) for p in parts) if tail else None
    return total, bias


def scatter(tabs, x_own, x_other, g_own, g_other, bias, name):
    term = lambda far, got: term_chunk(tabs[far], x_own, x_other, g_own, g_other, got, bias, name)
    got = [to_first(term(far, []), far) for far in (2, 1, 3)]
    first = term(0, got)
    tail = [first[1024:]] if bias else []
    chunk = lambda k: jnp.concatenate([first[k * 256 : (k + 1) * 256]] + tail, axis=0)
    got = [to_second(chunk(far), far) for far in (2, 1, 3)]
    total, row = fold([chunk(0)] + got, 256, bias)
    total = total.astype(BF)
    tail = [split_tail(row)] if bias else []
    chunk = lambda k: jnp.concatenate([total[k * 64 : (k + 1) * 64]] + tail, axis=0)
    got = [to_y(chunk(far), far) for far in (2, 1, 3)]
    return fold([chunk(0)] + got, 64, bias)


def rope_angles(positions):
    half_dim = HEAD // 2
    freq_index = jnp.arange(half_dim, dtype=jnp.int32)
    inv_freq = jnp.exp(freq_index.astype(F32) * (-2.0 * THETA_LOG / HEAD))
    first_cut = HEAD // 8
    second_cut = first_cut + 3 * HEAD // 16
    pos_float = positions.astype(F32)
    chosen_pos = jnp.where(
        (freq_index < first_cut)[None, :],
        pos_float[0][:, None],
        jnp.where((freq_index < second_cut)[None, :], pos_float[1][:, None], pos_float[2][:, None]),
    )
    angles = chosen_pos * inv_freq[None, :]
    return (jnp.cos(angles), jnp.sin(angles))


def rotate(tensor, cosines, sine_vals, direction):
    half_dim = HEAD // 2
    wide_cos = cosines[:, None, :]
    wide_sin = sine_vals[:, None, :] * direction
    front_half = tensor[..., :half_dim]
    back_half = tensor[..., half_dim:]
    return jnp.concatenate(
        [
            front_half * wide_cos - back_half * wide_sin,
            back_half * wide_cos + front_half * wide_sin,
        ],
        axis=-1,
    )


def attend(queries, keys_in, values_in, allowed):
    scores = jnp.einsum(
        "rhe,ke->rhk", queries, keys_in, preferred_element_type=F32
    ) * HEAD ** (-0.5)
    scores = jnp.where(allowed, scores, -1e30)
    peak_score = jnp.max(scores, axis=-1, keepdims=True)
    weights = jnp.where(allowed, jnp.exp(scores - peak_score), 0.0)
    weight_sum = jnp.sum(weights, axis=-1, keepdims=True)
    probs = weights / weight_sum
    probs_half = probs.astype(BF)
    attended = jnp.einsum(
        "rhk,ke->rhe", probs_half, values_in, preferred_element_type=F32
    ).astype(BF)
    return (attended, probs, probs_half)


def attend_back(queries, keys_in, values_in, probs, probs_half, grad, delta):
    dprob = jnp.einsum("rhe,ke->rhk", grad, values_in, preferred_element_type=F32)
    dscore = (probs * (dprob - delta[..., None]) * HEAD ** (-0.5)).astype(BF)
    dquery = jnp.einsum("rhk,ke->rhe", dscore, keys_in, preferred_element_type=F32)
    dkey = jnp.einsum("rhk,rhe->ke", dscore, queries, preferred_element_type=F32)
    dvalue = jnp.einsum("rhk,rhe->ke", probs_half, grad, preferred_element_type=F32)
    return dquery, dkey, dvalue


def per_device(
    w_qkv, qkv_bias, w_out, video_x, video_pos, short_x, short_pos, short_seg, video_cot, short_cot
):
    at = {name: lax.axis_index(name) for name in AXES}
    core = at["c"].astype(jnp.int32)[None]
    tabs = tables(at)
    nv, ns = video_x.shape[1], short_x.shape[1]
    rows = nv + ns

    w_half = lax.dynamic_slice(w_qkv, (at["c"] * 512, 0), (512, 768)).reshape(8, 64, 768)
    qkv_whole = gather(w_half[:4], w_half[4:], at).reshape(4096, 768)
    wo_half = weight_half(core, w_out)
    wo = gather(wo_half[:4], wo_half[4:], at)
    wo = wo.transpose(1, 0, 2, 3).reshape(8, 512, 512)
    wo_other = other_core(wo)

    x_own, x_send = column_halves(core, video_x[0], short_x[0])
    x_other = other_core(x_send)
    c_own, c_send = column_halves(core, video_cot[0], short_cot[0])
    c_other = other_core(c_send)

    places = jnp.concatenate([video_pos[:, 0, :], short_pos[:, 0, :]], axis=1)
    cosines, sine_vals = rope_angles(places)

    part = other_core(jnp.dot(x_other, qkv_whole, preferred_element_type=F32))
    projected = (
        jnp.dot(x_own, qkv_whole, preferred_element_type=F32) + part + qkv_bias[None, :]
    )
    key_local = rotate(
        projected[:, ATT : ATT + HEAD].reshape(rows, 1, HEAD), cosines, sine_vals, 1.0
    )[:, 0].astype(BF)
    value_local = projected[:, ATT + HEAD :].astype(BF)
    both_group = lax.all_gather(
        jnp.concatenate([key_local[:nv], value_local[:nv]], axis=1), GRP, axis=0, tiled=True
    )
    keys_group, values_group = both_group[:, :HEAD], both_group[:, HEAD:]
    queries = rotate(
        projected[:, :ATT].reshape(rows, QH, HEAD), cosines, sine_vals, 1.0
    ).astype(BF)

    grad_att_part = other_core(grad_attended_part(c_other, wo))
    grad_attended = (grad_attended_part(c_own, wo) + grad_att_part).astype(BF)

    position = jnp.arange(ns, dtype=jnp.int32)
    segment = short_seg[0]
    short_allowed = (
        (segment[None, :] == segment[:, None]) & (position[None, :] <= position[:, None])
    )[:, None, :]
    short_att, short_probs, short_half = attend(
        queries[nv:], key_local[nv:], value_local[nv:], short_allowed
    )

    first_row = ((at["z"] * 2 + at["yl"]) * 2 + at["c"]) * nv
    key_count = keys_group.shape[0]
    query_at = first_row + jnp.arange(nv, dtype=jnp.int32)
    video_allowed = (jnp.arange(key_count, dtype=jnp.int32)[None, :] <= query_at[:, None])[
        :, None, :
    ]
    video_att, video_probs, video_half = attend(
        queries[:nv], keys_group, values_group, video_allowed
    )
    attended = jnp.concatenate([video_att, short_att], axis=0)
    flat = attended.reshape(rows, ATT)
    flat_other = other_core(flat)

    grad_heads = grad_attended.reshape(rows, QH, HEAD)
    deltas = jnp.sum(grad_heads.astype(F32) * attended.astype(F32), axis=-1)
    video_dq, video_dk, video_dv = attend_back(
        queries[:nv], keys_group, values_group, video_probs, video_half, grad_heads[:nv], deltas[:nv]
    )
    to_owner = jnp.concatenate([video_dk, video_dv], axis=1).astype(BF)
    from_all = lax.all_to_all(to_owner, GRP, 0, 0, tiled=True)
    key_value = jnp.sum(from_all.reshape(16, nv, 2 * HEAD).astype(F32), axis=0)
    short_dq, short_dk, short_dv = attend_back(
        queries[nv:], key_local[nv:], value_local[nv:], short_probs, short_half, grad_heads[nv:], deltas[nv:]
    )

    grad_out, _ = scatter(tabs, c_own, c_other, flat, flat_other, False, "term_out")
    video_y, short_y = layer_out(core, flat, wo, wo_other, nv, ns)

    grad_queries = rotate(
        jnp.concatenate([video_dq, short_dq], axis=0), cosines, sine_vals, -1.0
    ).reshape(rows, ATT).astype(BF)
    grad_q, bias_q = scatter(
        tabs, x_own, x_other, grad_queries, other_core(grad_queries), True, "term_q"
    )
    grad_keys = rotate(
        jnp.concatenate([key_value[:, :HEAD], short_dk], axis=0)[:, None, :], cosines, sine_vals, -1.0
    )[:, 0]
    grad_values = jnp.concatenate([key_value[:, HEAD:], short_dv], axis=0)
    grad_kv_rows = jnp.concatenate([grad_keys, grad_values], axis=1).astype(BF)
    grad_kv, bias_kv = scatter(
        tabs, x_own, x_other, grad_kv_rows, other_core(grad_kv_rows), True, "term_kv"
    )
    return (
        video_y[None],
        short_y[None],
        jnp.concatenate([grad_q, grad_kv], axis=1),
        grad_out.T,
        jnp.concatenate([bias_q, bias_kv], axis=1)[0],
    )


def solution(mesh):
    fine = Mesh(mesh.devices.reshape(SIZES), AXES)
    return jax.shard_map(
        per_device,
        mesh=fine,
        in_specs=(
            P(DP, None),
            P(),
            P(DP, None),
            P(DP, GRP, None),
            P(None, DP, GRP),
            P(DP + GRP, None, None),
            P(None, DP + GRP, None),
            P(DP + GRP, None),
            P(DP, GRP, None),
            P(DP + GRP, None, None),
        ),
        out_specs=(
            P(DP, GRP, None),
            P(DP + GRP, None, None),
            P(GRP + DP, None),
            P(None, GRP + DP),
            P(),
        ),
        check_vma=False,
    )
```

time: 804 us -> 434 us (0.54)
  waiting for transfers between devices: 581 us -> 104 us
  blocking collectives: 105 us -> 0 us
  Pallas kernels: 0 us -> 96.4 us
  starting transfers between devices: 0.5 us -> 96.8 us
  matrix products: 68 us -> 28.6 us
  local copies, waits for them, and re-layouts: 18.6 us -> 53.7 us
  other arithmetic: 15.7 us -> 30.6 us
    reduce_scatter x4 -> x0, waiting for transfers between devices: 334 us -> none  [the longest x1 129 us: per_device(): lax.psum_scatter(term_proj.astype(jnp.bfloat16), 'grp', scatter_dimension...]
    all_gather x2 -> x1, waiting for transfers between devices: 245 us -> 22 us  [per_device(): lax.all_gather(jnp.concatenate([key_local[:nv], value_local[:nv]], axis=1...]
    pallas_call x0 -> x18, Pallas kernels: none -> 96.4 us  [the longest x12 58.4 us: term_chunk(): pl.pallas_call(functools.partial(term_kernel, received=len(got), bias=bia...]
    ppermute x0 -> x57, starting transfers between devices: none -> 92 us  [move(): return lax.ppermute(value, AXES, pairs(target))]
    ppermute x0 -> x57, waiting for transfers between devices: none -> 82.4 us  [move(): return lax.ppermute(value, AXES, pairs(target))]
    psum x1 -> x0, blocking collectives: 65.3 us -> none  [per_device(): grad_bias = lax.psum(bias_term, ('grp', 'dp'))]
    all_gather x2 -> x0, blocking collectives: 40 us -> none  [the longest x1 21.2 us: per_device(): lax.all_gather(key_local[:long_count], 'grp', axis=0, tiled=True)]
    dot_general x15 -> x13, matrix products: 62.5 us -> 25.4 us  [the longest x2 4.81 us: attend_back(): jnp.einsum('rhk,rhe->ke', probs_half, grad, preferred_element_type=F32)]
  transfers between devices with their start and end apart: 7 -> 59, of which waited for: 6 -> 21; matrix products, arithmetic and copies ran while one was open for 9% -> 23% of each run, Pallas kernels for 0% -> 23%
where the time goes in v1:
time: 434 us; the launch traced here: 426 us
  waiting for transfers between devices  104 us (24%)
  starting transfers between devices  96.8 us (22%)
  Pallas kernels  96.4 us (22%)
  local copies, waits for them, and re-layouts  53.7 us (12%)
  other arithmetic  30.6 us (7%)
  matrix products  28.6 us (7%)
  between operations  15.6 us (4%)
    ppermute x57, starting transfers between devices, move(): return lax.ppermute(value, AXES, pairs(target))  92 us
    ppermute x57, waiting for transfers between devices, move(): return lax.ppermute(value, AXES, pairs(target))  82.4 us
    pallas_call x12, Pallas kernels, term_chunk(): pl.pallas_call(functools.partial(term_kernel, received=len(got), bias=bia...  58.4 us
    all_gather x1, waiting for transfers between devices, per_device(): lax.all_gather(jnp.concatenate([key_local[:nv], value_local[:nv]], axis=1...  22 us
    dynamic_update_slice x41, local copies, waits for them, and re-layouts, put(): return lax.dynamic_update_slice(buffer, piece, index)  19.6 us
    unnamed x130, local copies, waits for them, and re-layouts  16.4 us
    pallas_call x2, Pallas kernels, grad_attended_part(): pl.pallas_call(grad_attended_kernel, grid=(8,), in_specs=[pl.BlockSpec((r...  14.4 us
    pallas_call x2, Pallas kernels, column_halves(): pl.pallas_call(halves_kernel, grid_spec=pltpu.PrefetchScalarGridSpec(num_...  13.2 us
  transfers between devices with their start and end apart: 59, of which 21 were waited for; matrix products, arithmetic and copies ran while one was open for 23% of the time, Pallas kernels for 23%

profile of v1, /device:TPU:0, one launch (start us, length us, event | category | flops | bytes accessed | tf_op | source)
XLA Modules:
  0.0 426.0 jit_solution(12738689923377345122)
XLA Ops:
  9.7 3.1 collective-permute-start.13
  14.4 6.6 %column_halves.3 = (bf16[384,4096]{1,0:T(8,128)(2,1)S(1)}, bf16[384,4096]{1,0:T(8,128)(2,1)}) custom-call(s32[1]{0:T(128)} %bitcast.core_ref, bf16[128,8192]{1,0:T(8,128)(2,1)S(1)} %bitcast.307, bf16[256,8192]{1,0:T(8,128)(2,1)} %bitcast.311, bf16[128,8192]{1,0:T(8,128)(2,1)S(1)} %bitcast.308, bf16[256,8192]{1,0:T(8,128)(2,1)} %bitcast.312), custom_call_target="tpu_custom_call" | custom-call | tf_op jit(solution)/shard_map/column_halves/pallas_call | solution.py:103
  23.8 2.5 collective-permute-start
  30.9 2.5 broadcast_in_dim.190
  37.0 6.6 %column_halves.2 = (bf16[384,4096]{1,0:T(8,128)(2,1)S(1)}, bf16[384,4096]{1,0:T(8,128)(2,1)}) custom-call(s32[1]{0:T(128)} %bitcast.core_ref, bf16[128,8192]{1,0:T(8,128)(2,1)S(1)} %bitcast.309, bf16[256,8192]{1,0:T(8,128)(2,1)} %bitcast.313, bf16[128,8192]{1,0:T(8,128)(2,1)S(1)} %bitcast.310, bf16[256,8192]{1,0:T(8,128)(2,1)} %bitcast.314), custom_call_target="tpu_custom_call" | custom-call | tf_op jit(solution)/shard_map/column_halves/pallas_call | solution.py:103
  43.7 2.5 broadcast_multiply_fusion
  53.7 3.7 collective-permute-done.18
  59.0 3.5 collective-permute-done.19
  64.3 4.6 %collective-permute-done.20 = bf16[2,1,64,512]{3,2,1,0:T(8,128)(2,1)S(1)} collective-permute-done((bf16[2,1,64,512]{3,2,1,0:T(8,128)(2,1)S(1)}, bf16[2,1,64,512]{3,2,1,0:T(8,128)(2,1)S(1)}, u32[]{:S(2)}, u32[]{:S(2)}) %collective-permute-start.20) | collective-permute-done | bytes 131104 | tf_op jit(solution)/shard_map/ppermute | solution.py:39
  69.3 3.0 collective-permute-start.6
  78.9 6.2 %collective-permute-done.7 = bf16[2,1,64,768]{3,2,1,0:T(8,128)(2,1)S(1)} collective-permute-done((bf16[2,1,64,768]{3,2,1,0:T(8,128)(2,1)S(1)}, bf16[2,1,64,768]{3,2,1,0:T(8,128)(2,1)S(1)}, u32[]{:S(2)}, u32[]{:S(2)}) %collective-permute-start.7) | collective-permute-done | bytes 196640 | tf_op jit(solution)/shard_map/ppermute | solution.py:39
  98.2 11.5 %collective-permute-done.1 = bf16[2,4,64,768]{3,2,1,0:T(8,128)(2,1)S(1)} collective-permute-done((bf16[2,4,64,768]{3,2,1,0:T(8,128)(2,1)S(1)}, bf16[2,4,64,768]{3,2,1,0:T(8,128)(2,1)S(1)}, u32[]{:S(2)}, u32[]{:S(2)}) %collective-permute-start.1) | collective-permute-done | bytes 786464 | tf_op jit(solution)/shard_map/ppermute | solution.py:39
  109.8 5.8 %collective-permute-done.2 = bf16[2,4,64,768]{3,2,1,0:T(8,128)(2,1)S(1)} collective-permute-done((bf16[2,4,64,768]{3,2,1,0:T(8,128)(2,1)S(1)}, bf16[2,4,64,768]{3,2,1,0:T(8,128)(2,1)S(1)}, u32[]{:S(2)}, u32[]{:S(2)}) %collective-permute-start.2) | collective-permute-done | bytes 786464 | tf_op jit(solution)/shard_map/ppermute | solution.py:39
  115.6 4.0 collective-permute-start.9
  119.7 7.0 %collective-permute-done.3 = bf16[2,4,64,768]{3,2,1,0:T(8,128)(2,1)S(1)} collective-permute-done((bf16[2,4,64,768]{3,2,1,0:T(8,128)(2,1)S(1)}, bf16[2,4,64,768]{3,2,1,0:T(8,128)(2,1)S(1)}, u32[]{:S(2)}, u32[]{:S(2)}) %collective-permute-start.3) | collective-permute-done | bytes 786464 | tf_op jit(solution)/shard_map/ppermute | solution.py:39
  126.7 3.9 collective-permute-start.10
  131.9 15.4 %collective-permute-done.9 = bf16[4,2,1,64,768]{4,3,2,1,0:T(8,128)(2,1)S(1)} collective-permute-done((bf16[4,2,1,64,768]{4,3,2,1,0:T(8,128)(2,1)S(1)}, bf16[4,2,1,64,768]{4,3,2,1,0:T(8,128)(2,1)S(1)}, u32[]{:S(2)}, u32[]{:S(2)}) %collective-permute-start.9) | collective-permute-done | bytes 786464 | tf_op jit(solution)/shard_map/ppermute | solution.py:39
  147.3 4.2 collective-permute-start.22
  151.5 12.8 %collective-permute-start.23 = (bf16[4,2,1,64,512]{4,3,1,0,2:T(8,128)(2,1)S(1)}, bf16[4,2,1,64,512]{4,3,1,0,2:T(8,128)(2,1)S(1)}, u32[]{:S(2)}, u32[]{:S(2)}) collective-permute-start(bf16[4,2,1,64,512]{4,3,1,0,2:T(8,128)(2,1)S(1)} %fusion.67), channel_id=1, source_target_pairs={{0,64},{2,66},{4,68},{6,70},{8,72},{10,74},{12,76},{14,78},{16,80}... | collective-permute-start | bytes 1572872 | tf_op jit(solution)/shard_map/ppermute | solution.py:39
  165.4 3.6 fusion.94
  169.0 6.2 %collective-permute-done.16 = bf16[2,4,64,512]{3,2,1,0:T(8,128)(2,1)S(1)} collective-permute-done((bf16[2,4,64,512]{3,2,1,0:T(8,128)(2,1)S(1)}, bf16[2,4,64,512]{3,2,1,0:T(8,128)(2,1)S(1)}, u32[]{:S(2)}, u32[]{:S(2)}) %collective-permute-start.16) | collective-permute-done | bytes 524320 | tf_op jit(solution)/shard_map/ppermute | solution.py:39
  175.9 4.7 %copy.38 = bf16[4,2,8,64,512]{4,3,1,0,2:T(8,128)(2,1)} copy(bf16[4,2,8,64,512]{4,3,2,1,0:T(8,128)(2,1)} %fusion.47) | data formatting | bytes 8388608 | tf_op jit(solution)/shard_map/dynamic_update_slice | solution.py:138
  185.3 6.5 %grad_attended.2 = f32[384,512]{1,0:T(8,128)S(1)} custom-call(bf16[384,4096]{1,0:T(8,128)(2,1)S(1)} %copy-done.3, bf16[8,512,512]{2,1,0:T(8,128)(2,1)} %bitcast.59.mine.w), custom_call_target="tpu_custom_call" | custom-call | flops 1610612736 | bytes 7340032 | tf_op jit(solution)/shard_map/grad_attended/pallas_call | solution.py:179
  192.8 7.8 %grad_attended.3 = f32[384,512]{1,0:T(8,128)} custom-call(bf16[384,4096]{1,0:T(8,128)(2,1)} %collective-permute-done.25.cot.refs_2_.refs_3_, bf16[8,512,512]{2,1,0:T(8,128)(2,1)} %bitcast.59.mine.w), custom_call_target="tpu_custom_call" | custom-call | flops 1610612736 | bytes 7340032 | tf_op jit(solution)/shard_map/grad_attended/pallas_call | solution.py:179
  200.7 3.9 fusion.93
  219.7 3.1 fusion.92
  226.9 22.0 %all-gather.2.cloned.1.call-done = bf16[2048,256]{1,0:T(8,128)(2,1)} async-done(((bf16[128,256]{1,0:T(8,128)(2,1)}), bf16[2048,256]{1,0:T(8,128)(2,1)}) %all-gather.2.cloned.1.call-update) | async-done | bytes 1048592 | tf_op jit(solution)/shard_map/all_gather | solution.py:436
  261.9 3.9 fusion.25
  266.9 4.7 %all-to-all-start = ((bf16[16,128,256]{1,2,0:T(8,128)(2,1)}), bf16[16,128,256]{1,2,0:T(8,128)(2,1)}, u32[]{:S(2)}, u32[]{:S(2)}) async-start(bf16[16,128,256]{1,2,0:T(8,128)(2,1)} %pad_maximum_fusion), calls=%async_computation | async-start | bytes 2097152 | tf_op jit(solution)/shard_map/all_to_all | solution.py:475
  277.8 5.2 %term_q.6 = bf16[1040,512]{1,0:T(8,128)(2,1)} custom-call(s32[13]{0:T(128)S(1)} %stack.219.tab, bf16[384,4096]{1,0:T(8,128)(2,1)S(1)} %get-tuple-element.11.refs_0_.refs_1_, bf16[384,4096]{1,0:T(8,128)(2,1)S(1)} %get-tuple-element.11.refs_0_.refs_1_, bf16[384,4096]{1,0:T(8,128)(2,1)} %copy-done.17, bf16[384,4096]{1,0:T(8,128)(2,1)} %copy-done.17, ...), custom_call_target="tpu_custom_call" | custom-call | flops 805306368 | bytes 3407872 | tf_op jit(solution)/shard_map/term_q/pallas_call | solution.py:281
  283.0 3.2 collective-permute-start.30
  286.2 5.3 %term_q.5 = bf16[1040,512]{1,0:T(8,128)(2,1)} custom-call(s32[13]{0:T(128)S(1)} %stack.210.tab, bf16[384,4096]{1,0:T(8,128)(2,1)S(1)} %get-tuple-element.11.refs_0_.refs_1_, bf16[384,4096]{1,0:T(8,128)(2,1)S(1)} %get-tuple-element.11.refs_0_.refs_1_, bf16[384,4096]{1,0:T(8,128)(2,1)} %copy-done.17, bf16[384,4096]{1,0:T(8,128)(2,1)} %copy-done.17, ...), custom_call_target="tpu_custom_call" | custom-call | flops 805306368 | bytes 3407872 | tf_op jit(solution)/shard_map/term_q/pallas_call | solution.py:281
  291.4 5.2 %term_q.4 = bf16[1040,512]{1,0:T(8,128)(2,1)} custom-call(s32[13]{0:T(128)S(1)} %stack.201.tab, bf16[384,4096]{1,0:T(8,128)(2,1)S(1)} %get-tuple-element.11.refs_0_.refs_1_, bf16[384,4096]{1,0:T(8,128)(2,1)S(1)} %get-tuple-element.11.refs_0_.refs_1_, bf16[384,4096]{1,0:T(8,128)(2,1)} %copy-done.17, bf16[384,4096]{1,0:T(8,128)(2,1)} %copy-done.17, ...), custom_call_target="tpu_custom_call" | custom-call | flops 805306368 | bytes 3407872 | tf_op jit(solution)/shard_map/term_q/pallas_call | solution.py:281
  312.6 5.3 %term_out.6 = bf16[1040,512]{1,0:T(8,128)(2,1)} custom-call(s32[13]{0:T(128)S(1)} %stack.219.tab, bf16[384,4096]{1,0:T(8,128)(2,1)S(1)} %copy-done.4, bf16[384,4096]{1,0:T(8,128)(2,1)S(1)} %copy-done.4, bf16[384,4096]{1,0:T(8,128)(2,1)} %collective-permute-done.25.cot.refs_2_.refs_3_, bf16[384,4096]{1,0:T(8,128)(2,1)} %collective-permute-done.25.cot.refs_2_.refs_3_, ...), custom_call_target="tpu_custom_call" | custom-call | flops 805306368 | bytes 3407872 | tf_op jit(solution)/shard_map/term_out/pallas_call | solution.py:281
  320.0 5.3 %term_out.5 = bf16[1040,512]{1,0:T(8,128)(2,1)} custom-call(s32[13]{0:T(128)S(1)} %stack.210.tab, bf16[384,4096]{1,0:T(8,128)(2,1)S(1)} %copy-done.4, bf16[384,4096]{1,0:T(8,128)(2,1)S(1)} %copy-done.4, bf16[384,4096]{1,0:T(8,128)(2,1)} %collective-permute-done.25.cot.refs_2_.refs_3_, bf16[384,4096]{1,0:T(8,128)(2,1)} %collective-permute-done.25.cot.refs_2_.refs_3_, ...), custom_call_target="tpu_custom_call" | custom-call | flops 805306368 | bytes 3407872 | tf_op jit(solution)/shard_map/term_out/pallas_call | solution.py:281
  325.3 5.3 %term_out.4 = bf16[1040,512]{1,0:T(8,128)(2,1)} custom-call(s32[13]{0:T(128)S(1)} %stack.201.tab, bf16[384,4096]{1,0:T(8,128)(2,1)S(1)} %copy-done.4, bf16[384,4096]{1,0:T(8,128)(2,1)S(1)} %copy-done.4, bf16[384,4096]{1,0:T(8,128)(2,1)} %collective-permute-done.25.cot.refs_2_.refs_3_, bf16[384,4096]{1,0:T(8,128)(2,1)} %collective-permute-done.25.cot.refs_2_.refs_3_, ...), custom_call_target="tpu_custom_call" | custom-call | flops 805306368 | bytes 3407872 | tf_op jit(solution)/shard_map/term_out/pallas_call | solution.py:281
  333.1 10.1 %layer_out.1 = (bf16[128,8192]{1,0:T(8,128)(2,1)}, bf16[256,8192]{1,0:T(8,128)(2,1)}) custom-call(s32[1]{0:T(128)} %bitcast.core_ref, bf16[384,512]{1,0:T(8,128)(2,1)S(1)} %copy_bitcast_fusion.1.att.refs_4_, bf16[8,512,512]{2,1,0:T(8,128)(2,1)} %bitcast.59.mine.w, bf16[8,512,512]{2,1,0:T(8,128)(2,1)} %collective-permute-done.24.theirs), custom_call_target="tpu_custom_call" | custom-call | flops 3221225472 | bytes 16777216 | tf_op jit(solution)/shard_map/layer_out/pallas_call | solution.py:219
  343.2 3.9 term_kv.6
  347.1 3.9 term_kv.5
  351.0 3.9 term_kv.4
  357.2 5.7 %term_q.7 = bf16[1040,512]{1,0:T(8,128)(2,1)S(1)} custom-call(s32[13]{0:T(128)S(1)} %stack.192.tab, bf16[384,4096]{1,0:T(8,128)(2,1)} %copy-done, bf16[384,4096]{1,0:T(8,128)(2,1)} %copy-done, bf16[384,4096]{1,0:T(8,128)(2,1)} %copy-done.17, bf16[384,4096]{1,0:T(8,128)(2,1)} %copy-done.17, bf16[384,512]{1,0:T(8,128)(2,1)S(1)} %copy-done.6, ...), custom_call_target="tpu_custom_call" | custom-call | flops 805306368 | bytes 3407872 | tf_op jit(solution)/shard_map/term_q/pallas_call | solution.py:281
  368.9 5.5 %term_out.7 = bf16[1040,512]{1,0:T(8,128)(2,1)S(1)} custom-call(s32[13]{0:T(128)S(1)} %stack.192.tab, bf16[384,4096]{1,0:T(8,128)(2,1)} %copy-done.2, bf16[384,4096]{1,0:T(8,128)(2,1)} %copy-done.2, bf16[384,4096]{1,0:T(8,128)(2,1)} %collective-permute-done.25.cot.refs_2_.refs_3_, bf16[384,4096]{1,0:T(8,128)(2,1)} %collective-permute-done.25.cot.refs_2_.refs_3_, ...), custom_call_target="tpu_custom_call" | custom-call | flops 805306368 | bytes 3407872 | tf_op jit(solution)/shard_map/term_out/pallas_call | solution.py:281
  377.0 2.7 collective-permute-done.38.refs_6_
  379.7 2.6 collective-permute-start.53
  382.3 3.9 term_kv.7
  389.7 2.8 collective-permute-start.54
  405.7 3.0 collective-permute-done.34
  409.5 4.2 collective-permute-start.44
  (374 shorter events, 147.3 us)
Async XLA Ops:
  7.2 241.8 %all-gather.2.cloned.1.call-start = ((), (), s32[]{:S(2)}) async-start(), calls=%async_computation.1 | async-start | bytes 1114112 | tf_op jit(solution)/shard_map/all_gather | solution.py:436
  9.7 59.5 %collective-permute-start.13 = (bf16[4,64,512]{2,1,0:T(8,128)(2,1)}, bf16[4,64,512]{2,1,0:T(8,128)(2,1)}, u32[]{:S(2)}, u32[]{:S(2)}) collective-permute-start(bf16[4,64,512]{2,1,0:T(8,128)(2,1)} %get-tuple-element.43), channel_id=1, source_target_pairs={{0,17},{2,19},{4,21},{6,23},{8,25},{10,27},{12,29},{14,31},{16,1},... | collective-permute-start | bytes 786440 | tf_op jit(solution)/shard_map/ppermute | solution.py:39
  13.5 33.9 %collective-permute-start.17 = (bf16[1,64,512]{2,1,0:T(8,128)(2,1)}, bf16[1,64,512]{2,1,0:T(8,128)(2,1)}, u32[]{:S(2)}, u32[]{:S(2)}) collective-permute-start(bf16[1,64,512]{2,1,0:T(8,128)(2,1)} %get-tuple-element.23), channel_id=1, source_target_pairs={{0,17},{2,19},{4,21},{6,23},{8,25},{10,27},{12,29},{14,31},{16,1},... | collective-permute-start | bytes 196616 | tf_op jit(solution)/shard_map/ppermute | solution.py:39
  22.6 170.2 %collective-permute-start.25 = (bf16[384,4096]{1,0:T(8,128)(2,1)}, bf16[384,4096]{1,0:T(8,128)(2,1)}, u32[]{:S(2)}, u32[]{:S(2)}) collective-permute-start(bf16[384,4096]{1,0:T(8,128)(2,1)} %get-tuple-element.16), channel_id=1, source_target_pairs={{0,8},{2,10},{4,12},{6,14},{8,0},{10,2},{12,4},{14,6},{16,24},{18,... | collective-permute-start | bytes 9437192 | tf_op jit(solution)/shard_map/ppermute | solution.py:39
  23.8 61.9 %collective-permute-start = (bf16[4,64,768]{2,1,0:T(8,128)(2,1)S(1)}, bf16[4,64,768]{2,1,0:T(8,128)(2,1)}, u32[]{:S(2)}, u32[]{:S(2)}) collective-permute-start(bf16[4,64,768]{2,1,0:T(8,128)(2,1)S(1)} %bitcast.318), channel_id=1, source_target_pairs={{0,17},{2,19},{4,21},{6,23},{8,25},{10,27},{12,29},{14,31},{16,1},... | collective-permute-start | bytes 1179656 | tf_op jit(solution)/shard_map/ppermute | solution.py:39
  27.1 23.2 %collective-permute-start.4 = (bf16[1,64,768]{2,1,0:T(8,128)(2,1)}, bf16[1,64,768]{2,1,0:T(8,128)(2,1)}, u32[]{:S(2)}, u32[]{:S(2)}) collective-permute-start(bf16[1,64,768]{2,1,0:T(8,128)(2,1)} %get-tuple-element.25), channel_id=1, source_target_pairs={{0,17},{2,19},{4,21},{6,23},{8,25},{10,27},{12,29},{14,31},{16,1},... | collective-permute-start | bytes 294920 | tf_op jit(solution)/shard_map/ppermute | solution.py:39
  48.5 116.0 %collective-permute-start.11 = (bf16[384,4096]{1,0:T(8,128)(2,1)S(1)}, bf16[384,4096]{1,0:T(8,128)(2,1)S(1)}, u32[]{:S(2)}, u32[]{:S(2)}) collective-permute-start(bf16[384,4096]{1,0:T(8,128)(2,1)S(1)} %copy-done.61), channel_id=1, source_target_pairs={{0,8},{2,10},{4,12},{6,14},{8,0},{10,2},{12,4},{14,6},{16,24},{18,... | collective-permute-start | bytes 9437192 | tf_op jit(solution)/shard_map/ppermute | solution.py:39
  50.3 7.1 %collective-permute-start.18 = (bf16[2,1,64,512]{3,2,1,0:T(8,128)(2,1)S(1)}, bf16[2,1,64,512]{3,2,1,0:T(8,128)(2,1)S(1)}, u32[]{:S(2)}, u32[]{:S(2)}) collective-permute-start(bf16[2,1,64,512]{3,2,1,0:T(8,128)(2,1)S(1)} %pad_maximum_fusion.22), channel_id=1, source_target_pairs={{0,2},{2,4},{4,6},{6,0},{8,10},{10,12},{12,14},{14,8},{16,18},{18,... | collective-permute-start | bytes 393224 | tf_op jit(solution)/shard_map/ppermute | solution.py:39
  68.9 6.9 %collective-permute-start.5 = (bf16[2,1,64,768]{3,2,1,0:T(8,128)(2,1)S(1)}, bf16[2,1,64,768]{3,2,1,0:T(8,128)(2,1)S(1)}, u32[]{:S(2)}, u32[]{:S(2)}) collective-permute-start(bf16[2,1,64,768]{3,2,1,0:T(8,128)(2,1)S(1)} %pad_maximum_fusion.8), channel_id=1, source_target_pairs={{0,2},{2,4},{4,6},{6,0},{8,10},{10,12},{12,14},{14,8},{16,18},{18,... | collective-permute-start | bytes 589832 | tf_op jit(solution)/shard_map/ppermute | solution.py:39
  69.3 8.4 %collective-permute-start.6 = (bf16[2,1,64,768]{3,2,1,0:T(8,128)(2,1)S(1)}, bf16[2,1,64,768]{3,2,1,0:T(8,128)(2,1)S(1)}, u32[]{:S(2)}, u32[]{:S(2)}) collective-permute-start(bf16[2,1,64,768]{3,2,1,0:T(8,128)(2,1)S(1)} %pad_maximum_fusion.8), channel_id=1, source_target_pairs={{0,6},{2,0},{4,2},{6,4},{8,14},{10,8},{12,10},{14,12},{16,22},{18,... | collective-permute-start | bytes 589832 | tf_op jit(solution)/shard_map/ppermute | solution.py:39
  75.8 9.3 %collective-permute-start.7 = (bf16[2,1,64,768]{3,2,1,0:T(8,128)(2,1)S(1)}, bf16[2,1,64,768]{3,2,1,0:T(8,128)(2,1)S(1)}, u32[]{:S(2)}, u32[]{:S(2)}) collective-permute-start(bf16[2,1,64,768]{3,2,1,0:T(8,128)(2,1)S(1)} %pad_maximum_fusion.8), channel_id=1, source_target_pairs={{0,4},{2,6},{4,0},{6,2},{8,12},{10,14},{12,8},{14,10},{16,20},{18,... | collective-permute-start | bytes 589832 | tf_op jit(solution)/shard_map/ppermute | solution.py:39
  77.6 14.5 %collective-permute-start.14 = (bf16[2,4,64,512]{3,2,1,0:T(8,128)(2,1)S(1)}, bf16[2,4,64,512]{3,2,1,0:T(8,128)(2,1)S(1)}, u32[]{:S(2)}, u32[]{:S(2)}) collective-permute-start(bf16[2,4,64,512]{3,2,1,0:T(8,128)(2,1)S(1)} %pad_maximum_fusion.3), channel_id=1, source_target_pairs={{0,2},{2,4},{4,6},{6,0},{8,10},{10,12},{12,14},{14,8},{16,18},{18,... | collective-permute-start | bytes 1572872 | tf_op jit(solution)/shard_map/ppermute | solution.py:39
  85.2 10.3 %collective-permute-start.15 = (bf16[2,4,64,512]{3,2,1,0:T(8,128)(2,1)S(1)}, bf16[2,4,64,512]{3,2,1,0:T(8,128)(2,1)S(1)}, u32[]{:S(2)}, u32[]{:S(2)}) collective-permute-start(bf16[2,4,64,512]{3,2,1,0:T(8,128)(2,1)S(1)} %pad_maximum_fusion.3), channel_id=1, source_target_pairs={{0,6},{2,0},{4,2},{6,4},{8,14},{10,8},{12,10},{14,12},{16,22},{18,... | collective-permute-start | bytes 1572872 | tf_op jit(solution)/shard_map/ppermute | solution.py:39
  85.7 45.0 %collective-permute-start.8 = (bf16[4,2,1,64,768]{4,3,2,1,0:T(8,128)(2,1)S(1)}, bf16[4,2,1,64,768]{4,3,2,1,0:T(8,128)(2,1)S(1)}, u32[]{:S(2)}, u32[]{:S(2)}) collective-permute-start(bf16[4,2,1,64,768]{4,3,2,1,0:T(8,128)(2,1)S(1)} %fusion.61), channel_id=1, source_target_pairs={{0,32},{2,34},{4,36},{6,38},{8,40},{10,42},{12,44},{14,46},{16,48}... | collective-permute-start | bytes 2359304 | tf_op jit(solution)/shard_map/ppermute | solution.py:39
  92.1 17.6 %collective-permute-start.1 = (bf16[2,4,64,768]{3,2,1,0:T(8,128)(2,1)S(1)}, bf16[2,4,64,768]{3,2,1,0:T(8,128)(2,1)S(1)}, u32[]{:S(2)}, u32[]{:S(2)}) collective-permute-start(bf16[2,4,64,768]{3,2,1,0:T(8,128)(2,1)S(1)} %pad_maximum_fusion.2), channel_id=1, source_target_pairs={{0,2},{2,4},{4,6},{6,0},{8,10},{10,12},{12,14},{14,8},{16,18},{18,... | collective-permute-start | bytes 2359304 | tf_op jit(solution)/shard_map/ppermute | solution.py:39
  95.5 20.1 %collective-permute-start.2 = (bf16[2,4,64,768]{3,2,1,0:T(8,128)(2,1)S(1)}, bf16[2,4,64,768]{3,2,1,0:T(8,128)(2,1)S(1)}, u32[]{:S(2)}, u32[]{:S(2)}) collective-permute-start(bf16[2,4,64,768]{3,2,1,0:T(8,128)(2,1)S(1)} %pad_maximum_fusion.2), channel_id=1, source_target_pairs={{0,6},{2,0},{4,2},{6,4},{8,14},{10,8},{12,10},{14,12},{16,22},{18,... | collective-permute-start | bytes 2359304 | tf_op jit(solution)/shard_map/ppermute | solution.py:39
  109.7 17.0 %collective-permute-start.3 = (bf16[2,4,64,768]{3,2,1,0:T(8,128)(2,1)S(1)}, bf16[2,4,64,768]{3,2,1,0:T(8,128)(2,1)S(1)}, u32[]{:S(2)}, u32[]{:S(2)}) collective-permute-start(bf16[2,4,64,768]{3,2,1,0:T(8,128)(2,1)S(1)} %pad_maximum_fusion.2), channel_id=1, source_target_pairs={{0,4},{2,6},{4,0},{6,2},{8,12},{10,14},{12,8},{14,10},{16,20},{18,... | collective-permute-start | bytes 2359304 | tf_op jit(solution)/shard_map/ppermute | solution.py:39
  115.6 31.7 %collective-permute-start.9 = (bf16[4,2,1,64,768]{4,3,2,1,0:T(8,128)(2,1)S(1)}, bf16[4,2,1,64,768]{4,3,2,1,0:T(8,128)(2,1)S(1)}, u32[]{:S(2)}, u32[]{:S(2)}) collective-permute-start(bf16[4,2,1,64,768]{4,3,2,1,0:T(8,128)(2,1)S(1)} %fusion.61), channel_id=1, source_target_pairs={{0,96},{2,98},{4,100},{6,102},{8,104},{10,106},{12,108},{14,110},{... | collective-permute-start | bytes 2359304 | tf_op jit(solution)/shard_map/ppermute | solution.py:39
  126.7 24.8 %collective-permute-start.10 = (bf16[4,2,1,64,768]{4,3,2,1,0:T(8,128)(2,1)S(1)}, bf16[4,2,1,64,768]{4,3,2,1,0:T(8,128)(2,1)S(1)}, u32[]{:S(2)}, u32[]{:S(2)}) collective-permute-start(bf16[4,2,1,64,768]{4,3,2,1,0:T(8,128)(2,1)S(1)} %fusion.61), channel_id=1, source_target_pairs={{0,64},{2,66},{4,68},{6,70},{8,72},{10,74},{12,76},{14,78},{16,80}... | collective-permute-start | bytes 2359304 | tf_op jit(solution)/shard_map/ppermute | solution.py:39
  130.7 51.5 %collective-permute-start.21 = (bf16[4,2,1,64,512]{4,3,1,0,2:T(8,128)(2,1)S(1)}, bf16[4,2,1,64,512]{4,3,1,0,2:T(8,128)(2,1)S(1)}, u32[]{:S(2)}, u32[]{:S(2)}) collective-permute-start(bf16[4,2,1,64,512]{4,3,1,0,2:T(8,128)(2,1)S(1)} %fusion.67), channel_id=1, source_target_pairs={{0,32},{2,34},{4,36},{6,38},{8,40},{10,42},{12,44},{14,46},{16,48}... | collective-permute-start | bytes 1572872 | tf_op jit(solution)/shard_map/ppermute | solution.py:39
  147.3 35.8 %collective-permute-start.22 = (bf16[4,2,1,64,512]{4,3,1,0,2:T(8,128)(2,1)S(1)}, bf16[4,2,1,64,512]{4,3,1,0,2:T(8,128)(2,1)S(1)}, u32[]{:S(2)}, u32[]{:S(2)}) collective-permute-start(bf16[4,2,1,64,512]{4,3,1,0,2:T(8,128)(2,1)S(1)} %fusion.67), channel_id=1, source_target_pairs={{0,96},{2,98},{4,100},{6,102},{8,104},{10,106},{12,108},{14,110},{... | collective-permute-start | bytes 1572872 | tf_op jit(solution)/shard_map/ppermute | solution.py:39
  151.5 32.4 %collective-permute-start.23 = (bf16[4,2,1,64,512]{4,3,1,0,2:T(8,128)(2,1)S(1)}, bf16[4,2,1,64,512]{4,3,1,0,2:T(8,128)(2,1)S(1)}, u32[]{:S(2)}, u32[]{:S(2)}) collective-permute-start(bf16[4,2,1,64,512]{4,3,1,0,2:T(8,128)(2,1)S(1)} %fusion.67), channel_id=1, source_target_pairs={{0,64},{2,66},{4,68},{6,70},{8,72},{10,74},{12,76},{14,78},{16,80}... | collective-permute-start | bytes 1572872 | tf_op jit(solution)/shard_map/ppermute | solution.py:39
  164.4 10.8 %collective-permute-start.16 = (bf16[2,4,64,512]{3,2,1,0:T(8,128)(2,1)S(1)}, bf16[2,4,64,512]{3,2,1,0:T(8,128)(2,1)S(1)}, u32[]{:S(2)}, u32[]{:S(2)}) collective-permute-start(bf16[2,4,64,512]{3,2,1,0:T(8,128)(2,1)S(1)} %pad_maximum_fusion.3), channel_id=1, source_target_pairs={{0,4},{2,6},{4,0},{6,2},{8,12},{10,14},{12,8},{14,10},{16,20},{18,... | collective-permute-start | bytes 1572872 | tf_op jit(solution)/shard_map/ppermute | solution.py:39
  175.2 25.4 %collective-permute-start.12 = (f32[384,768]{1,0:T(8,128)}, f32[384,768]{1,0:T(8,128)}, u32[]{:S(2)}, u32[]{:S(2)}) collective-permute-start(f32[384,768]{1,0:T(8,128)} %fusion.94), channel_id=1, source_target_pairs={{0,8},{2,10},{4,12},{6,14},{8,0},{10,2},{12,4},{14,6},{16,24},{18,... | collective-permute-start | bytes 3538952 | tf_op jit(solution)/shard_map/ppermute | solution.py:39
  184.8 133.0 %collective-permute-start.24 = (bf16[8,512,512]{2,1,0:T(8,128)(2,1)}, bf16[8,512,512]{2,1,0:T(8,128)(2,1)}, u32[]{:S(2)}, u32[]{:S(2)}) collective-permute-start(bf16[8,512,512]{2,1,0:T(8,128)(2,1)} %bitcast.59.mine.w), channel_id=1, source_target_pairs={{0,8},{2,10},{4,12},{6,14},{8,0},{10,2},{12,4},{14,6},{16,24},{18,... | collective-permute-start | bytes 12582920 | tf_op jit(solution)/shard_map/ppermute | solution.py:39
  266.9 32.1 %all-to-all-start = ((bf16[16,128,256]{1,2,0:T(8,128)(2,1)}), bf16[16,128,256]{1,2,0:T(8,128)(2,1)}, u32[]{:S(2)}, u32[]{:S(2)}) async-start(bf16[16,128,256]{1,2,0:T(8,128)(2,1)} %pad_maximum_fusion), calls=%async_computation | async-start | bytes 2097152 | tf_op jit(solution)/shard_map/all_to_all | solution.py:475
  276.6 33.9 %collective-permute-start.47 = (bf16[384,512]{1,0:T(8,128)(2,1)S(1)}, bf16[384,512]{1,0:T(8,128)(2,1)}, u32[]{:S(2)}, u32[]{:S(2)}) collective-permute-start(bf16[384,512]{1,0:T(8,128)(2,1)S(1)} %copy_bitcast_fusion.1.att.refs_4_), channel_id=1, source_target_pairs={{0,8},{2,10},{4,12},{6,14},{8,0},{10,2},{12,4},{14,6},{16,24},{18,... | collective-permute-start | bytes 1179656 | tf_op jit(solution)/shard_map/ppermute | solution.py:39
  283.0 47.7 %collective-permute-start.30 = (bf16[1040,512]{1,0:T(8,128)(2,1)}, bf16[1040,512]{1,0:T(8,128)(2,1)}, u32[]{:S(2)}, u32[]{:S(2)}) collective-permute-start(bf16[1040,512]{1,0:T(8,128)(2,1)} %term_q.6), channel_id=1, source_target_pairs={{0,96},{2,98},{4,100},{6,102},{8,14},{10,8},{12,10},{14,12},{16,11... | collective-permute-start | bytes 3194888 | tf_op jit(solution)/shard_map/ppermute | solution.py:39
  291.4 63.5 %collective-permute-start.29 = (bf16[1040,512]{1,0:T(8,128)(2,1)}, bf16[1040,512]{1,0:T(8,128)(2,1)}, u32[]{:S(2)}, u32[]{:S(2)}) collective-permute-start(bf16[1040,512]{1,0:T(8,128)(2,1)} %term_q.5), channel_id=1, source_target_pairs={{0,32},{2,34},{4,36},{6,38},{8,10},{10,12},{12,14},{14,8},{16,48},... | collective-permute-start | bytes 3194888 | tf_op jit(solution)/shard_map/ppermute | solution.py:39
  296.7 60.5 %collective-permute-start.28 = (bf16[1040,512]{1,0:T(8,128)(2,1)}, bf16[1040,512]{1,0:T(8,128)(2,1)}, u32[]{:S(2)}, u32[]{:S(2)}) collective-permute-start(bf16[1040,512]{1,0:T(8,128)(2,1)} %term_q.4), channel_id=1, source_target_pairs={{0,64},{2,66},{4,68},{6,70},{8,12},{10,14},{12,8},{14,10},{16,80},... | collective-permute-start | bytes 3194888 | tf_op jit(solution)/shard_map/ppermute | solution.py:39
  310.6 14.7 %collective-permute-start.37 = (bf16[384,256]{1,0:T(8,128)(2,1)S(1)}, bf16[384,256]{1,0:T(8,128)(2,1)S(1)}, u32[]{:S(2)}, u32[]{:S(2)}) collective-permute-start(bf16[384,256]{1,0:T(8,128)(2,1)S(1)} %maximum_maximum_fusion.refs_4_), channel_id=1, source_target_pairs={{0,8},{2,10},{4,12},{6,14},{8,0},{10,2},{12,4},{14,6},{16,24},{18,... | collective-permute-start | bytes 589832 | tf_op jit(solution)/shard_map/ppermute | solution.py:39
  317.9 45.1 %collective-permute-start.50 = (bf16[1040,512]{1,0:T(8,128)(2,1)}, bf16[1040,512]{1,0:T(8,128)(2,1)}, u32[]{:S(2)}, u32[]{:S(2)}) collective-permute-start(bf16[1040,512]{1,0:T(8,128)(2,1)} %term_out.6), channel_id=1, source_target_pairs={{0,96},{2,98},{4,100},{6,102},{8,14},{10,8},{12,10},{14,12},{16,11... | collective-permute-start | bytes 3194888 | tf_op jit(solution)/shard_map/ppermute | solution.py:39
  325.2 39.6 %collective-permute-start.49 = (bf16[1040,512]{1,0:T(8,128)(2,1)}, bf16[1040,512]{1,0:T(8,128)(2,1)}, u32[]{:S(2)}, u32[]{:S(2)}) collective-permute-start(bf16[1040,512]{1,0:T(8,128)(2,1)} %term_out.5), channel_id=1, source_target_pairs={{0,32},{2,34},{4,36},{6,38},{8,10},{10,12},{12,14},{14,8},{16,48},... | collective-permute-start | bytes 3194888 | tf_op jit(solution)/shard_map/ppermute | solution.py:39
  330.6 36.0 %collective-permute-start.48 = (bf16[1040,512]{1,0:T(8,128)(2,1)}, bf16[1040,512]{1,0:T(8,128)(2,1)}, u32[]{:S(2)}, u32[]{:S(2)}) collective-permute-start(bf16[1040,512]{1,0:T(8,128)(2,1)} %term_out.4), channel_id=1, source_target_pairs={{0,64},{2,66},{4,68},{6,70},{8,12},{10,14},{12,8},{14,10},{16,80},... | collective-permute-start | bytes 3194888 | tf_op jit(solution)/shard_map/ppermute | solution.py:39
  354.9 19.7 %collective-permute-start.40 = (bf16[1040,256]{1,0:T(8,128)(2,1)S(1)}, bf16[1040,256]{1,0:T(8,128)(2,1)S(1)}, u32[]{:S(2)}, u32[]{:S(2)}) collective-permute-start(bf16[1040,256]{1,0:T(8,128)(2,1)S(1)} %term_kv.6), channel_id=1, source_target_pairs={{0,96},{2,98},{4,100},{6,102},{8,14},{10,8},{12,10},{14,12},{16,11... | collective-permute-start | bytes 1597448 | tf_op jit(solution)/shard_map/ppermute | solution.py:39
  357.2 18.8 %collective-permute-start.39 = (bf16[1040,256]{1,0:T(8,128)(2,1)S(1)}, bf16[1040,256]{1,0:T(8,128)(2,1)S(1)}, u32[]{:S(2)}, u32[]{:S(2)}) collective-permute-start(bf16[1040,256]{1,0:T(8,128)(2,1)S(1)} %term_kv.5), channel_id=1, source_target_pairs={{0,32},{2,34},{4,36},{6,38},{8,10},{10,12},{12,14},{14,8},{16,48},... | collective-permute-start | bytes 1597448 | tf_op jit(solution)/shard_map/ppermute | solution.py:39
  363.0 16.7 %collective-permute-start.38 = (bf16[1040,256]{1,0:T(8,128)(2,1)S(1)}, bf16[1040,256]{1,0:T(8,128)(2,1)S(1)}, u32[]{:S(2)}, u32[]{:S(2)}) collective-permute-start(bf16[1040,256]{1,0:T(8,128)(2,1)S(1)} %term_kv.4), channel_id=1, source_target_pairs={{0,64},{2,66},{4,68},{6,70},{8,12},{10,14},{12,8},{14,10},{16,80},... | collective-permute-start | bytes 1597448 | tf_op jit(solution)/shard_map/ppermute | solution.py:39
  364.8 24.8 %collective-permute-start.32 = (bf16[272,512]{1,0:T(8,128)(2,1)S(1)}, bf16[272,512]{1,0:T(8,128)(2,1)S(1)}, u32[]{:S(2)}, u32[]{:S(2)}) collective-permute-start(bf16[272,512]{1,0:T(8,128)(2,1)S(1)} %get-tuple-element.61), channel_id=1, source_target_pairs={{0,2},{2,4},{4,6},{6,0},{8,40},{10,42},{12,44},{14,46},{16,18},{18... | collective-permute-start | bytes 835592 | tf_op jit(solution)/shard_map/ppermute | solution.py:39
  366.7 25.8 %collective-permute-start.31 = (bf16[272,512]{1,0:T(8,128)(2,1)S(1)}, bf16[272,512]{1,0:T(8,128)(2,1)S(1)}, u32[]{:S(2)}, u32[]{:S(2)}) collective-permute-start(bf16[272,512]{1,0:T(8,128)(2,1)S(1)} %get-tuple-element.60), channel_id=1, source_target_pairs={{0,4},{2,6},{4,0},{6,2},{8,72},{10,74},{12,76},{14,78},{16,20},{18... | collective-permute-start | bytes 835592 | tf_op jit(solution)/shard_map/ppermute | solution.py:39
  374.6 11.8 %collective-permute-start.51 = (bf16[256,512]{1,0:T(8,128)(2,1)S(1)}, bf16[256,512]{1,0:T(8,128)(2,1)S(1)}, u32[]{:S(2)}, u32[]{:S(2)}) collective-permute-start(bf16[256,512]{1,0:T(8,128)(2,1)S(1)} %get-tuple-element.32), channel_id=1, source_target_pairs={{0,4},{2,6},{4,0},{6,2},{8,72},{10,74},{12,76},{14,78},{16,20},{18... | collective-permute-start | bytes 786440 | tf_op jit(solution)/shard_map/ppermute | solution.py:39
  375.9 11.5 %collective-permute-start.52 = (bf16[256,512]{1,0:T(8,128)(2,1)S(1)}, bf16[256,512]{1,0:T(8,128)(2,1)S(1)}, u32[]{:S(2)}, u32[]{:S(2)}) collective-permute-start(bf16[256,512]{1,0:T(8,128)(2,1)S(1)} %get-tuple-element.34), channel_id=1, source_target_pairs={{0,2},{2,4},{4,6},{6,0},{8,40},{10,42},{12,44},{14,46},{16,18},{18... | collective-permute-start | bytes 786440 | tf_op jit(solution)/shard_map/ppermute | solution.py:39
  379.7 8.8 %collective-permute-start.53 = (bf16[256,512]{1,0:T(8,128)(2,1)S(1)}, bf16[256,512]{1,0:T(8,128)(2,1)S(1)}, u32[]{:S(2)}, u32[]{:S(2)}) collective-permute-start(bf16[256,512]{1,0:T(8,128)(2,1)S(1)} %get-tuple-element.33), channel_id=1, source_target_pairs={{0,6},{2,0},{4,2},{6,4},{8,104},{10,106},{12,108},{14,110},{16,22}... | collective-permute-start | bytes 786440 | tf_op jit(solution)/shard_map/ppermute | solution.py:39
  386.3 7.2 %collective-permute-start.33 = (bf16[272,512]{1,0:T(8,128)(2,1)S(1)}, bf16[272,512]{1,0:T(8,128)(2,1)S(1)}, u32[]{:S(2)}, u32[]{:S(2)}) collective-permute-start(bf16[272,512]{1,0:T(8,128)(2,1)S(1)} %concatenate.129), channel_id=1, source_target_pairs={{0,6},{2,0},{4,2},{6,4},{8,104},{10,106},{12,108},{14,110},{16,22}... | collective-permute-start | bytes 835592 | tf_op jit(solution)/shard_map/ppermute | solution.py:39
  387.4 21.4 %collective-permute-start.42 = (bf16[272,256]{1,0:T(8,128)(2,1)S(1)}, bf16[272,256]{1,0:T(8,128)(2,1)S(1)}, u32[]{:S(2)}, u32[]{:S(2)}) collective-permute-start(bf16[272,256]{1,0:T(8,128)(2,1)S(1)} %get-tuple-element.66), channel_id=1, source_target_pairs={{0,2},{2,4},{4,6},{6,0},{8,40},{10,42},{12,44},{14,46},{16,18},{18... | collective-permute-start | bytes 417800 | tf_op jit(solution)/shard_map/ppermute | solution.py:39
  388.4 20.4 %collective-permute-start.41 = (bf16[272,256]{1,0:T(8,128)(2,1)S(1)}, bf16[272,256]{1,0:T(8,128)(2,1)S(1)}, u32[]{:S(2)}, u32[]{:S(2)}) collective-permute-start(bf16[272,256]{1,0:T(8,128)(2,1)S(1)} %get-tuple-element.65), channel_id=1, source_target_pairs={{0,4},{2,6},{4,0},{6,2},{8,72},{10,74},{12,76},{14,78},{16,20},{18... | collective-permute-start | bytes 417800 | tf_op jit(solution)/shard_map/ppermute | solution.py:39
  393.5 6.6 %collective-permute-start.56 = (bf16[64,512]{1,0:T(8,128)(2,1)S(1)}, bf16[64,512]{1,0:T(8,128)(2,1)S(1)}, u32[]{:S(2)}, u32[]{:S(2)}) collective-permute-start(bf16[64,512]{1,0:T(8,128)(2,1)S(1)} %get-tuple-element.45), channel_id=1, source_target_pairs={{0,17},{2,19},{4,21},{6,23},{8,25},{10,27},{12,29},{14,31},{16,0},... | collective-permute-start | bytes 196616 | tf_op jit(solution)/shard_map/ppermute | solution.py:39
  396.2 12.7 %collective-permute-start.43 = (bf16[272,256]{1,0:T(8,128)(2,1)S(1)}, bf16[272,256]{1,0:T(8,128)(2,1)S(1)}, u32[]{:S(2)}, u32[]{:S(2)}) collective-permute-start(bf16[272,256]{1,0:T(8,128)(2,1)S(1)} %concatenate.130), channel_id=1, source_target_pairs={{0,6},{2,0},{4,2},{6,4},{8,104},{10,106},{12,108},{14,110},{16,22}... | collective-permute-start | bytes 417800 | tf_op jit(solution)/shard_map/ppermute | solution.py:39
  409.5 6.6 %collective-permute-start.44 = (bf16[80,256]{1,0:T(8,128)(2,1)S(1)}, bf16[80,256]{1,0:T(8,128)(2,1)S(1)}, u32[]{:S(2)}, u32[]{:S(2)}) collective-permute-start(bf16[80,256]{1,0:T(8,128)(2,1)S(1)} %get-tuple-element.62), channel_id=1, source_target_pairs={{0,1},{2,3},{4,5},{6,7},{8,9},{10,11},{12,13},{14,15},{16,17},{18,... | collective-permute-start | bytes 122888 | tf_op jit(solution)/shard_map/ppermute | solution.py:39
  (74 other events, 692.6 us)
Sparse Core Ops, SparseCore 0:
  206.7 42.2 all-gather.1

commit v2 on v0

v2 whole, which is shorter than its diff:
```python
import functools

import jax
import jax.numpy as jnp
from jax import lax
from jax.experimental import pallas as pl
from jax.experimental.pallas import tpu as pltpu
from jax.sharding import Mesh
from jax.sharding import PartitionSpec as P

HEAD = 128
QH = 4
ATT = QH * HEAD
SCALE = HEAD ** (-0.5)
AXES = ("z", "yl", "c", "x", "yh")
SIZES = (4, 2, 2, 4, 2)
GRP = ("z", "yl", "c")
DP = ("x", "yh")
BF = jnp.bfloat16
F32 = jnp.float32
THETA_LOG = 13.815510557964274
STREAM = 52


def device_index(z, y, c, x):
    z, y, c, x = z % 4, y % 4, c % 2, x % 4
    return (((z * 2 + y % 2) * 2 + c) * 4 + x) * 2 + y // 2


def pairs(target):
    result = []
    for z in range(4):
        for y in range(4):
            for c in range(2):
                for x in range(4):
                    result.append((device_index(z, y, c, x), device_index(*target(z, y, c, x))))
    return result


def move(value, target):
    return lax.ppermute(value, AXES, pairs(target))


def other_core(value):
    return move(value, lambda z, y, c, x: (z, y, c + 1, x))


def to_x(value, step):
    return move(value, lambda z, y, c, x: (z, y, c, x + step))


def to_z(value, step):
    return move(value, lambda z, y, c, x: (z + step, y, c, x))


def to_y(value, step):
    return move(value, lambda z, y, c, x: (z, y + step, c, x))


def across(value):
    return move(value, lambda z, y, c, x: (z, 3 - y, c, x))


def to_x_or_across(value, step):
    return move(
        value, lambda z, y, c, x: (z, y, c, x + step) if c == 0 else (z, 3 - y, c, x)
    )


def to_first(value, step):
    return move(
        value, lambda z, y, c, x: (z + step, y, c, x) if c == 0 else (z, y, c, x + step)
    )


def to_second(value, step):
    return move(
        value, lambda z, y, c, x: (z, y, c, x + step) if c == 0 else (z + step, y, c, x)
    )


def call(kernel, name, grid, ins, outs, shapes, tab=None, flops=0, traffic=0, scratch=(), limit=24):
    spec = lambda pair: pl.BlockSpec(*pair)
    single = not isinstance(shapes, list)
    in_specs = [spec(i) for i in ins]
    out_specs = spec(outs[0]) if single else [spec(o) for o in outs]
    cost = pl.CostEstimate(flops=flops, bytes_accessed=traffic, transcendentals=0)
    options = dict(
        out_shape=shapes,
        compiler_params=pltpu.CompilerParams(vmem_limit_bytes=limit * 1024 * 1024),
        cost_estimate=cost,
        name=name,
    )
    if tab is None:
        return pl.pallas_call(
            kernel, grid=grid, in_specs=in_specs, out_specs=out_specs, scratch_shapes=scratch, **options
        )
    grid_spec = pltpu.PrefetchScalarGridSpec(
        num_scalar_prefetch=1, grid=grid, in_specs=in_specs, out_specs=out_specs, scratch_shapes=scratch
    )
    return functools.partial(pl.pallas_call(kernel, grid_spec=grid_spec, **options), tab)


def shaped(shape, kind=BF):
    return jax.ShapeDtypeStruct(shape, kind)


def halves_kernel(core_ref, *refs):
    out = refs[4]
    n = refs[0].shape[0]
    for k in range(2):
        out[:n, k * 512 : (k + 1) * 512] = refs[k][...]
        out[n:, k * 512 : (k + 1) * 512] = refs[2 + k][...]


def halves(core, video, short):
    nv, ns = video.shape[0], short.shape[0]
    theirs = lambda n, k: ((n, 512), lambda j, s: (0, 4 * j + 2 * k + s[0]))
    return call(
        halves_kernel, "halves", (4,), [theirs(nv, 0), theirs(nv, 1), theirs(ns, 0), theirs(ns, 1)],
        [((nv + ns, 1024), lambda j, s: (0, j))], shaped((nv + ns, 4096)), core,
        traffic=4 * (nv + ns) * 4096, limit=STREAM,
    )(video, video, short, short)


def turn_kernel(tab, video, short, other, out):
    nv, rows = video.shape[0], other.shape[0]
    step = pl.program_id(0)
    first, second, third = video[...].T, short[...].T, other[...].T
    for k in range(8):
        where = pl.ds(pl.multiple_of(tab[1 + step * 8 + k] * 64, 64), 64)
        out[where, :nv] = first[k * 64 : (k + 1) * 64]
        out[where, nv:rows] = second[k * 64 : (k + 1) * 64]
        out[where, rows:] = third[k * 64 : (k + 1) * 64]


def turned(tab, video, short, other):
    nv, ns = video.shape[0], short.shape[0]
    rows = nv + ns
    own = lambda n: ((n, 512), lambda j, s: (0, 2 * j + s[0]))
    return call(
        turn_kernel, "turned", (8,),
        [own(nv), own(ns), ((rows, 512), lambda j, s: (0, j))],
        [((4096, 2 * rows), lambda j, s: (0, 0))], shaped((4096, 2 * rows)), tab,
        traffic=8 * rows * 4096, limit=STREAM,
    )(video, short, other)


def weight_quarter_kernel(tab, block, out):
    out[0] = block[...]


def weight_quarter(tab, w):
    return call(
        weight_quarter_kernel, "weight_quarter", (2,),
        [((64, 512), lambda j, s: (0, 2 * (2 * s[1] + j) + s[0]))],
        [((1, 64, 512), lambda j, s: (j, 0, 0))], shaped((2, 64, 512)), tab, traffic=4 * 64 * 1024,
    )(w)


def project_kernel(tab, *refs, parts, added):
    video, short, other = refs[:3]
    weights = refs[3 : 3 + parts]
    out_own, out_other = refs[-2:]
    nv = video.shape[0]
    step = pl.program_id(0)

    for k in range(parts):

        @pl.when(step == k)
        def _(k=k):
            w = weights[k][...]
            first = jnp.dot(video[...], w, preferred_element_type=F32)
            second = jnp.dot(short[...], w, preferred_element_type=F32)
            third = jnp.dot(other[...], w, preferred_element_type=F32)
            if k == 0 and added:
                before_own, before_other = refs[3 + parts : 5 + parts]
                out_own[:nv] = before_own[:nv] + first
                out_own[nv:] = before_own[nv:] + second
                out_other[...] = before_other[...] + third
            elif k == 0:
                out_own[:nv], out_own[nv:], out_other[...] = first, second, third
            else:
                out_own[:nv] += first
                out_own[nv:] += second
                out_other[...] += third


def project(tab, video, short, other, weights, before=()):
    nv, ns, parts = video.shape[0], short.shape[0], len(weights)
    rows = nv + ns
    own = lambda n: ((n, 512), lambda j, s: (0, 2 * s[1 + j] + s[0]))
    whole = lambda shape: (shape, lambda j, s: (0, 0))
    return call(
        functools.partial(project_kernel, parts=parts, added=len(before) > 0), "project", (parts,),
        [own(nv), own(ns), ((rows, 512), lambda j, s: (0, s[1 + j]))]
        + [whole((512, 768))] * parts + [whole((rows, 768))] * len(before),
        [whole((rows, 768))] * 2, [shaped((rows, 768), F32)] * 2, tab,
        flops=4 * rows * 512 * 768 * parts, traffic=parts * (512 * 768 * 2 + rows * 2048) + rows * 768 * 8,
        limit=STREAM,
    )(video, short, other, *weights, *before)


def spin(block, cosines, sines):
    return block * cosines + pltpu.roll(block, HEAD // 2, 1) * sines


def heads_kernel(near, near_got, far, far_got, bias, cosines, sines, queries, keys_values):
    total = near[...] + near_got[...] + far[...] + far_got[...] + bias[...]
    for h in range(QH):
        part = slice(h * HEAD, (h + 1) * HEAD)
        queries[:, part] = spin(total[:, part], cosines[...], sines[...]).astype(BF)
    keys_values[:, :HEAD] = spin(total[:, ATT : ATT + HEAD], cosines[...], sines[...]).astype(BF)
    keys_values[:, HEAD:] = total[:, ATT + HEAD :].astype(BF)


def heads(near, near_got, far, far_got, bias, cosines, sines):
    rows = near.shape[0]
    at = lambda i: (i, 0)
    big, small = ((128, 768), at), ((128, HEAD), at)
    return call(
        heads_kernel, "heads", (rows // 128,),
        [big, big, big, big, ((1, 768), lambda i: (0, 0)), small, small],
        [((128, ATT), at), ((128, 2 * HEAD), at)],
        [shaped((rows, ATT)), shaped((rows, 2 * HEAD))], traffic=rows * 768 * 18,
    )(near, near_got, far, far_got, bias, cosines, sines)


def stacked(block, count):
    return jnp.concatenate([block[:, h * HEAD : (h + 1) * HEAD] for h in range(count)], axis=0)


def attention_core(queries, keys, values, grad, allowed):
    nt = (((1,), (1,)), ((), ()))
    scores = lax.dot_general(queries, keys, nt, preferred_element_type=F32) * SCALE
    scores = jnp.where(allowed, scores, -1e30)
    peak = jnp.max(scores, axis=1, keepdims=True)
    weights = jnp.exp(scores - peak)
    probs = weights * (1.0 / jnp.sum(weights, axis=1, keepdims=True))
    probs_half = probs.astype(BF)
    attended = jnp.dot(probs_half, values, preferred_element_type=F32).astype(BF)
    deltas = jnp.sum(grad.astype(F32) * attended.astype(F32), axis=1, keepdims=True)
    dprob = lax.dot_general(grad, values, nt, preferred_element_type=F32)
    dscore = (probs * (dprob - deltas) * SCALE).astype(BF)
    dquery = jnp.dot(dscore, keys, preferred_element_type=F32)
    dkey = jnp.dot(queries.T, dscore, preferred_element_type=F32)
    dvalue = jnp.dot(grad.T, probs_half, preferred_element_type=F32)
    return attended, dquery, dkey, dvalue


def attention_kernel(tab, queries, keys_values, segments, ga, gb, cosines, sines, result, dkv, total, *, video):
    step = pl.program_id(0)
    n = queries.shape[0]
    m = keys_values.shape[0]
    query_at = lax.broadcasted_iota(jnp.int32, (n, m), 0)
    key_at = lax.broadcasted_iota(jnp.int32, (n, m), 1)
    if video:
        allowed = key_at <= query_at + tab[0]
    else:
        allowed = (segments[1] == segments[0][:, :1]) & (key_at <= query_at)
    allowed = jnp.concatenate([allowed, allowed], axis=0)
    grad = (ga[...] + gb[...]).astype(BF)
    attended, dquery, dkey, dvalue = attention_core(
        stacked(queries[...], 2), keys_values[:, :HEAD], keys_values[:, HEAD:], stacked(grad, 2), allowed
    )
    for h in range(2):
        part = slice(h * HEAD, (h + 1) * HEAD)
        result[0, :, part] = attended[h * n : (h + 1) * n]
        result[1, :, part] = spin(dquery[h * n : (h + 1) * n], cosines[...], -sines[...]).astype(BF)

    @pl.when(step == 0)
    def _():
        total[0] = dkey
        total[1] = dvalue

    @pl.when(step == 1)
    def _():
        dkey_all = (total[0] + dkey).T
        if not video:
            dkey_all = spin(dkey_all, cosines[...], -sines[...])
        dkv[:, :HEAD] = dkey_all.astype(BF)
        dkv[:, HEAD:] = (total[1] + dvalue).T.astype(BF)


def attention(video, first_row, start, count, queries, keys_values, segments, ga, gb, cosines, sines):
    m = keys_values.shape[0] if video else count
    n = count
    row = start
    pair = ((n, 2 * HEAD), lambda i, s: (row, i))
    angle = ((n, HEAD), lambda i, s: (row, 0))
    keys = ((m, 2 * HEAD), lambda i, s: (0 if video else row, 0))
    return call(
        functools.partial(attention_kernel, video=video), "video_attention" if video else "short_attention", (2,),
        [pair, keys, (segments.shape, lambda i, s: (0, 0, 0)), pair, pair, angle, angle],
        [((2, n, 2 * HEAD), lambda i, s: (0, 0, i)), ((m, 2 * HEAD), lambda i, s: (0, 0))],
        [shaped((2, n, ATT)), shaped((m, 2 * HEAD))], first_row,
        flops=2 * 5 * QH * n * m * HEAD, traffic=m * 1024, scratch=[pltpu.VMEM((2, HEAD, m), F32)], limit=48,
    )(queries, keys_values, segments, ga, gb, cosines, sines)


def collect_kernel(parts, cosines, sines, out):
    rows = out.shape[0]
    total = jnp.zeros((rows, 2 * HEAD), F32)
    for k in range(parts.shape[0]):
        total += parts[k].astype(F32)
    out[:, :HEAD] = spin(total[:, :HEAD], cosines[...], -sines[...]).astype(BF)
    out[:, HEAD:] = total[:, HEAD:].astype(BF)


def collect(parts, cosines, sines):
    count, rows = parts.shape[:2]
    zero = lambda i: (0, 0)
    return call(
        collect_kernel, "collect", (1,),
        [((count, rows, 2 * HEAD), lambda i: (0, 0, 0)), ((rows, HEAD), zero), ((rows, HEAD), zero)],
        [((rows, 2 * HEAD), zero)], shaped((rows, 2 * HEAD)), traffic=count * rows * 512,
    )(parts, cosines, sines)


W_BLOCK = ((1, 8, 1, 64, 512), lambda j, *s: (j // 2, 0, j % 2, 0, 0))


def whole_weights(ref):
    return ref[0, :, 0].reshape(ATT, 512)


def grad_attended_kernel(core_ref, video, short, other, w, total_own, total_other):
    nv = video.shape[0]

    @pl.when(pl.program_id(0) == 0)
    def _():
        total_own[...] = jnp.zeros_like(total_own)
        total_other[...] = jnp.zeros_like(total_other)

    block = whole_weights(w).T
    total_other[...] += jnp.dot(other[...], block, preferred_element_type=F32)
    total_own[:nv] += jnp.dot(video[...], block, preferred_element_type=F32)
    total_own[nv:] += jnp.dot(short[...], block, preferred_element_type=F32)


def grad_attended_parts(core, video, short, other, w):
    nv, ns = video.shape[0], short.shape[0]
    rows = nv + ns
    own = lambda n: ((n, 512), lambda j, s: (0, 2 * j + s[0]))
    out = ((rows, ATT), lambda j, s: (0, 0))
    return call(
        grad_attended_kernel, "grad_attended", (8,),
        [own(nv), own(ns), ((rows, 512), lambda j, s: (0, j)), W_BLOCK], [out, out],
        [shaped((rows, ATT), F32)] * 2, core, flops=4 * rows * 4096 * 512,
        traffic=rows * 16384 + 4096 * 1024, limit=STREAM,
    )(video, short, other, w)


def layer_out_kernel(tab, video_att, short_att, mine, theirs, video, short):
    for w, at in ((mine, tab[0]), (theirs, 1 - tab[0])):
        block = whole_weights(w)
        where = pl.ds(pl.multiple_of(at * 512, 512), 512)
        video[:, where] = jnp.dot(video_att[0], block, preferred_element_type=F32).astype(BF)
        short[:, where] = jnp.dot(short_att[0], block, preferred_element_type=F32).astype(BF)


def layer_out(tab, video_att, short_att, mine, theirs):
    nv, ns = video_att.shape[1], short_att.shape[1]
    att = lambda n: ((1, n, ATT), lambda j, s: (0, 0, 0))
    return call(
        layer_out_kernel, "layer_out", (8,), [att(nv), att(ns), W_BLOCK, W_BLOCK],
        [((nv, 1024), lambda j, s: (0, j)), ((ns, 1024), lambda j, s: (0, j))],
        [shaped((nv, 8192)), shaped((ns, 8192))], tab,
        flops=2 * (nv + ns) * 8192 * ATT, traffic=8192 * 1024 + (nv + ns) * 16384, limit=STREAM,
    )(video_att, short_att, mine, theirs)


TAIL = 16


def numbers(*entries):
    return jnp.stack([jnp.asarray(e, jnp.int32) for e in entries])


def turn_table(at):
    core, y = at["c"], at["yh"] * 2 + at["yl"]
    order = []
    for tz in range(4):
        for tyl in range(2):
            for tx in range(4):
                for tyh in range(2):
                    dy = (tyh * 2 + tyl - y + 4) % 4
                    order.append(jnp.where(core == 0, tz * 16 + tx * 4 + dy, tx * 16 + tz * 4 + dy))
    return numbers(core, *order)


def term_kernel(tab, cot, tokens, *refs):
    rights, got, out = refs[:4], refs[4:-1], refs[-1]
    right = jnp.concatenate([r[0] for r in rights], axis=0)

    def write(left):
        total = jnp.dot(left[...], right, preferred_element_type=F32)
        for ref in got:
            total += ref[0].astype(F32)
        out[0] = total.astype(BF)

    pl.when(pl.program_id(0) < 2)(lambda: write(cot))
    pl.when(pl.program_id(0) >= 2)(lambda: write(tokens))


def term(place, cot, tokens, rights, got=()):
    wide = cot.shape[1]
    at = lambda i, s: (i // 2, i % 2, 0)
    block = ((1, 512, ATT), at)
    return call(
        term_kernel, "term", (4,),
        [
            ((512, wide), lambda i, s: (2 * s[0] + jnp.minimum(i, 1), 0)),
            ((512, wide), lambda i, s: (2 * s[0] + jnp.maximum(i - 2, 0), 0)),
        ]
        + [((1, r.shape[1], ATT), lambda i, s: (i // 2, 0, 0)) for r in rights] + [block] * len(got),
        [block], shaped((2, 1024, ATT)), numbers(place % 4),
        flops=4 * wide * 1024 * ATT, traffic=4 * wide * 1024 + 4 * wide * ATT + 4096 * ATT, limit=STREAM,
    )(cot, tokens, *rights, *got)


def summed(own, got):
    return sum((g.astype(F32) for g in got), own).astype(BF)


def scatter(places, cot, tokens, rights):
    got = [to_first(term(places[0] + far, cot, tokens, rights), far) for far in (2, 1, 3)]
    first = [f.reshape(2, 4, 256, ATT) for f in [term(places[0], cot, tokens, rights)] + got]

    def rows(far):
        place = (places[1] + far) % 4
        return sum(lax.dynamic_index_in_dim(f, place, 1, keepdims=False).astype(F32) for f in first)

    got = [to_second(rows(far).astype(BF), far) for far in (2, 1, 3)]
    piece = lambda far: sum(
        (g[:, far * 64 : (far + 1) * 64].astype(F32) for g in got), rows(0)[:, far * 64 : (far + 1) * 64]
    )
    late = [to_y(piece(far).astype(BF), far) for far in (2, 1, 3)]
    return sum((g.astype(F32) for g in late), piece(0))


def tail_of(row):
    high = lax.reduce_precision(row, 8, 7)
    n = row.shape[1]
    return jnp.concatenate(
        [high.astype(BF), (row - high).astype(BF), jnp.zeros((TAIL - 6, n), BF)], axis=0
    )


def tail_sum(tails):
    return sum(t[:3].astype(F32) + t[3:6].astype(F32) for t in tails)


def key_term_kernel(tab, left, ga, gb, tail, out):
    right = jnp.concatenate([ga[...], gb[...]], axis=0)
    rows = left[:, :, 0].reshape(1024, left.shape[4])
    out[0, :1024] = jnp.dot(rows, right, preferred_element_type=F32).astype(BF)
    out[0, 1024:] = tail[...]


def key_term(y, left, ga, gb, tail):
    rows, n = ga.shape
    whole = lambda shape: (shape, lambda i, s: (0, 0))
    return call(
        key_term_kernel, "key_term", (4,),
        [
            ((4, 4, 1, 64, 2 * rows), lambda i, s: (0, 0, ((i % 2) * 2 + i // 2 - s[0] + 4) % 4, 0, 0)),
            whole((rows, n)), whole((rows, n)), whole((TAIL, n)),
        ],
        [((1, 1024 + TAIL, n), lambda i, s: (i, 0, 0))], shaped((4, 1024 + TAIL, n)), numbers(y),
        flops=4 * rows * 4096 * n, traffic=4096 * (4 * rows + 2 * n), limit=STREAM,
    )(left.reshape(4, 4, 4, 64, 2 * rows), ga, gb, tail)


LATE_GROUPS = [
    [device_index(a, y, 0, b) if c == 0 else device_index(b, y, 1, a) for a in range(4) for b in range(4)]
    for c in range(2)
    for y in range(4)
]


def scatter_with_tail(terms):
    first = jnp.sum(terms[:, :1024].astype(F32), axis=0).astype(BF).reshape(16, 64, 256)
    tail = tail_of(tail_sum([terms[k, 1024:] for k in range(4)]))
    parts = jnp.concatenate([first, jnp.broadcast_to(tail[None], (16, TAIL, 256))], axis=1)
    parts = lax.all_to_all(parts, AXES, 0, 0, tiled=True, axis_index_groups=LATE_GROUPS)
    total = jnp.sum(parts.astype(F32), axis=0)
    return total[:64], total[64:67] + total[67:70]


def rope_angles(positions):
    half_dim = HEAD // 2
    freq_index = jnp.arange(half_dim, dtype=jnp.int32)
    inv_freq = jnp.exp(freq_index.astype(F32) * (-2.0 * THETA_LOG / HEAD))
    first_cut = HEAD // 8
    second_cut = first_cut + 3 * HEAD // 16
    pos_float = positions.astype(F32)
    chosen_pos = jnp.where(
        (freq_index < first_cut)[None, :],
        pos_float[0][:, None],
        jnp.where((freq_index < second_cut)[None, :], pos_float[1][:, None], pos_float[2][:, None]),
    )
    angles = chosen_pos * inv_freq[None, :]
    cosines, sines = jnp.cos(angles), jnp.sin(angles)
    return (
        jnp.concatenate([cosines, cosines], axis=1),
        jnp.concatenate([-sines, sines], axis=1),
    )


def to_all(value, axes, count):
    return lax.all_to_all(jnp.broadcast_to(value[None], (count,) + value.shape), axes, 0, 0)


def after(value, *others):
    return lax.optimization_barrier((value,) + others)[0]


def per_device(
    w_qkv, qkv_bias, w_out, video_x, video_pos, short_x, short_pos, short_seg, video_cot, short_cot
):
    at = {name: lax.axis_index(name) for name in AXES}
    core = numbers(at["c"])
    order = turn_table(at)
    nv, ns = video_x.shape[1], short_x.shape[1]
    rows = nv + ns
    video_x, short_x, video_cot, short_cot = video_x[0], short_x[0], video_cot[0], short_cot[0]

    mine = lax.dynamic_slice(w_qkv, (at["c"] * 512, 0), (512, 768))
    x_other = other_core(halves(1 - core, video_x, short_x))
    x_turned = turned(order, video_x, short_x, x_other)
    first, third, facing, quarters, x_turned, x_other, c_send = lax.optimization_barrier((
        to_x(mine, 1), to_x(mine, 3), across(mine),
        to_all(weight_quarter(numbers(at["c"], at["z"]), w_out), DP, 8),
        x_turned, x_other, halves(1 - core, video_cot, short_cot),
    ))
    wo = to_all(quarters, ("z",), 4)
    c_other = other_core(c_send)
    relay = lambda near: jnp.where(at["c"] == 0, facing, near)
    shard = lambda step, yh: ((at["x"] - step + 4) % 4) * 2 + yh
    near, off = at["yh"], 1 - at["yh"]
    part = project(
        numbers(at["c"], shard(0, near), shard(1, near), shard(3, near), shard(0, off)),
        video_x, short_x, x_other, [mine, first, third, facing],
    )
    far_first, far_third, second, c_turned, part = lax.optimization_barrier((
        to_x_or_across(relay(first), 1), to_x_or_across(relay(third), 3), to_x(mine, 2),
        turned(order, video_cot, short_cot, c_other), part,
    ))
    near_own, near_other = project(
        numbers(at["c"], shard(2, near), shard(1, off), shard(3, off)),
        video_x, short_x, x_other, [second, far_first, far_third], part,
    )
    far_second, near_own, near_other = lax.optimization_barrier(
        (to_x_or_across(relay(second), 2), near_own, near_other)
    )

    places = jnp.concatenate([video_pos[:, 0, :], short_pos[:, 0, :]], axis=1)
    cosines, sines = rope_angles(places)
    near_other = other_core(near_other)
    far_own, far_other = project(numbers(at["c"], shard(2, off)), video_x, short_x, x_other, [far_second])
    queries, keys_values = heads(
        near_own, near_other, far_own, other_core(far_other), qkv_bias[None], cosines, sines
    )
    wide = jnp.broadcast_to(keys_values[:nv][None], (16, nv, 2 * HEAD))
    wide, wo = lax.optimization_barrier((wide, wo))
    group = lax.all_to_all(wide, GRP, 0, 0).reshape(16 * nv, 2 * HEAD)

    wo_other = other_core(wo)
    grad_own, grad_other = grad_attended_parts(core, video_cot, short_cot, c_other, wo)
    grad_other = other_core(grad_other)

    segment = short_seg[0]
    segments = jnp.stack([jnp.broadcast_to(segment[:, None], (ns, ns)), jnp.broadcast_to(segment[None, :], (ns, ns))])
    first_row = ((at["z"] * 2 + at["yl"]) * 2 + at["c"]) * nv
    cut = lambda a: a[nv:]
    short_result, short_dkv = attention(
        False, numbers(0), 0, ns, cut(queries), cut(keys_values), segments, cut(grad_own), cut(grad_other),
        cut(cosines), cut(sines),
    )
    group, wo_other = lax.optimization_barrier((group, wo_other))
    video_result, video_dkv = attention(
        True, numbers(first_row), 0, nv, queries, group, jnp.zeros((1, 8, 128), jnp.int32), grad_own, grad_other,
        cosines, sines,
    )
    arrived = lax.all_to_all(video_dkv.reshape(16, nv, 2 * HEAD), GRP, 0, 0, tiled=True)

    results = (video_result, short_result, other_core(video_result), other_core(short_result))
    place = jnp.where(at["c"] == 0, at["z"], at["x"])
    second_place = jnp.where(at["c"] == 0, at["x"], at["z"])
    grad_out, grad_q = scatter((place, second_place), c_turned, x_turned, results)

    video_dkv = collect(arrived, cosines[:nv], sines[:nv])
    dkv = jnp.concatenate([video_dkv, short_dkv], axis=0)
    dkv_other = other_core(dkv)
    sum_q = sum(jnp.sum(r[1].astype(F32), axis=0) for r in results).reshape(2, 256)
    sum_kv = jnp.sum(dkv.astype(F32) + dkv_other.astype(F32), axis=0)[None]
    terms = key_term(at["yh"] * 2 + at["yl"], x_turned, dkv, dkv_other, tail_of(jnp.concatenate([sum_q, sum_kv], axis=0)))
    video_y, short_y = layer_out(core, after(video_result, terms), short_result, wo, wo_other)
    terms, video_y, short_y = lax.optimization_barrier(
        (lax.all_to_all(terms, ("yl", "yh"), 0, 0, tiled=True), video_y, short_y)
    )
    grad_kv, bias = scatter_with_tail(terms)
    return (
        video_y[None],
        short_y[None],
        jnp.concatenate([grad_q, grad_kv], axis=1),
        grad_out.T,
        bias.reshape(768),
    )


def solution(mesh):
    fine = Mesh(mesh.devices.reshape(SIZES), AXES)
    return jax.shard_map(
        per_device,
        mesh=fine,
        in_specs=(
            P(DP, None),
            P(),
            P(DP, None),
            P(DP, GRP, None),
            P(None, DP, GRP),
            P(DP + GRP, None, None),
            P(None, DP + GRP, None),
            P(DP + GRP, None),
            P(DP, GRP, None),
            P(DP + GRP, None, None),
        ),
        out_specs=(
            P(DP, GRP, None),
            P(DP + GRP, None, None),
            P(GRP + DP, None),
            P(None, GRP + DP),
            P(),
        ),
        check_vma=False,
    )
```

time: 804 us -> 256 us (0.32)
  waiting for transfers between devices: 581 us -> 66.5 us
  blocking collectives: 105 us -> 0 us
  Pallas kernels: 0 us -> 101 us
  matrix products: 68 us -> 0 us
  starting transfers between devices: 0.5 us -> 56.9 us
  between operations: 14.7 us -> 1.35 us
    reduce_scatter x4 -> x0, waiting for transfers between devices: 334 us -> none  [the longest x1 129 us: per_device(): lax.psum_scatter(term_proj.astype(jnp.bfloat16), 'grp', scatter_dimension...]
    all_gather x2 -> x0, waiting for transfers between devices: 245 us -> none  [the longest x1 137 us: per_device(): lax.all_gather(w_qkv, 'dp', axis=0, tiled=True)]
    pallas_call x0 -> x19, Pallas kernels: none -> 101 us  [the longest x4 21.7 us: term(): call(term_kernel, 'term', (4,), [((512, wide), lambda i, s: (2 * s[0] + j...]
    psum x1 -> x0, blocking collectives: 65.3 us -> none  [per_device(): grad_bias = lax.psum(bias_term, ('grp', 'dp'))]
    dot_general x15 -> x0, matrix products: 62.5 us -> none  [the longest x1 12.5 us: per_device(): lax.dot_general(tokens, grad_rows, (((0,), (0,)), ((), ())), preferred_el...]
    ppermute x0 -> x25, waiting for transfers between devices: none -> 51.4 us  [move(): return lax.ppermute(value, AXES, pairs(target))]
    all_gather x2 -> x0, blocking collectives: 40 us -> none  [the longest x1 21.2 us: per_device(): lax.all_gather(key_local[:long_count], 'grp', axis=0, tiled=True)]
    all_to_all x0 -> x6, starting transfers between devices: none -> 28.8 us  [the longest x2 12.3 us: to_all(): lax.all_to_all(jnp.broadcast_to(value[None], (count,) + value.shape), axe...]
  transfers between devices with their start and end apart: 7 -> 31, of which waited for: 6 -> 14; matrix products, arithmetic and copies ran while one was open for 9% -> 8% of each run, Pallas kernels for 0% -> 38%
where the time goes in v2:
time: 256 us; the launch traced here: 253 us
  Pallas kernels  101 us (39%)
  waiting for transfers between devices  66.5 us (26%)
  starting transfers between devices  56.9 us (22%)
  other arithmetic  15.3 us (6%)
  local copies, waits for them, and re-layouts  12.5 us (5%)
    ppermute x25, waiting for transfers between devices, move(): return lax.ppermute(value, AXES, pairs(target))  51.4 us
    ppermute x25, starting transfers between devices, move(): return lax.ppermute(value, AXES, pairs(target))  28.1 us
    pallas_call x4, Pallas kernels, term(): call(term_kernel, 'term', (4,), [((512, wide), lambda i, s: (2 * s[0] + j...  21.7 us
    pallas_call x2, Pallas kernels, turned(): call(turn_kernel, 'turned', (8,), [own(nv), own(ns), ((rows, 512), lambda...  18.9 us
    pallas_call x3, Pallas kernels, project(): call(functools.partial(project_kernel, parts=parts, added=len(before) > 0...  17.9 us
    all_to_all x2, starting transfers between devices, to_all(): lax.all_to_all(jnp.broadcast_to(value[None], (count,) + value.shape), axe...  12.3 us
    pallas_call x1, Pallas kernels, layer_out(): call(layer_out_kernel, 'layer_out', (8,), [att(nv), att(ns), W_BLOCK, W_B...  9.55 us
    pallas_call x1, Pallas kernels, grad_attended_parts(): call(grad_attended_kernel, 'grad_attended', (8,), [own(nv), own(ns), ((ro...  9.52 us
  transfers between devices with their start and end apart: 31, of which 14 were waited for; matrix products, arithmetic and copies ran while one was open for 8% of the time, Pallas kernels for 38%

profile of v2, /device:TPU:0, one launch (start us, length us, event | category | flops | bytes accessed | tf_op | source)
XLA Modules:
  0.0 253.4 jit_solution(16171548083016443960)
XLA Ops:
  0.7 4.4 %halves.2 = bf16[384,4096]{1,0:T(8,128)(2,1)} custom-call(s32[1]{0:T(128)S(6)} %sub.8.core_ref, bf16[128,8192]{1,0:T(8,128)(2,1)} %bitcast.160, bf16[128,8192]{1,0:T(8,128)(2,1)} %bitcast.161, bf16[256,8192]{1,0:T(8,128)(2,1)} %bitcast.154, bf16[256,8192]{1,0:T(8,128)(2,1)} %bitcast.155), custom_call_target="tpu_custom_call" | custom-call | bytes 6291456 | tf_op jit(solution)/shard_map/halves/pallas_call | solution.py:119
  6.9 7.0 %all-to-all-start = ((bf16[8,2,64,512]{3,2,1,0:T(8,128)(2,1)}), bf16[8,2,64,512]{3,2,1,0:T(8,128)(2,1)}, u32[]{:S(2)}, u32[]{:S(2)}) async-start(bf16[8,2,64,512]{3,2,1,0:T(8,128)(2,1)} %broadcast_in_dim.88), calls=%async_computation | async-start | bytes 2097152 | tf_op jit(solution)/shard_map/all_to_all | solution.py:512
  14.0 2.1 collective-permute-start
  16.0 1.3 collective-permute-start.1
  17.3 3.3 %collective-permute-start.2 = (bf16[512,768]{1,0:T(8,128)(2,1)S(1)}, bf16[512,768]{1,0:T(8,128)(2,1)S(1)}, u32[]{:S(2)}, u32[]{:S(2)}) collective-permute-start(bf16[512,768]{1,0:T(8,128)(2,1)S(1)} %constant_dynamic-slice_fusion.refs_3_), channel_id=1, source_target_pairs={{0,17},{2,19},{4,21},{6,23},{8,25},{10,27},{12,29},{14,31},{16,1},... | collective-permute-start | bytes 2359304 | tf_op jit(solution)/shard_map/ppermute | solution.py:41
  20.6 4.3 %halves.3 = bf16[384,4096]{1,0:T(8,128)(2,1)} custom-call(s32[1]{0:T(128)S(6)} %sub.8.core_ref, bf16[128,8192]{1,0:T(8,128)(2,1)} %bitcast.170, bf16[128,8192]{1,0:T(8,128)(2,1)} %bitcast.171, bf16[256,8192]{1,0:T(8,128)(2,1)} %bitcast.166, bf16[256,8192]{1,0:T(8,128)(2,1)} %bitcast.167), custom_call_target="tpu_custom_call" | custom-call | bytes 6291456 | tf_op jit(solution)/shard_map/halves/pallas_call | solution.py:119
  25.1 9.4 %turned.2.tokens = bf16[4096,768]{1,0:T(8,128)(2,1)} custom-call(s32[65]{0:T(128)S(1)} %stack.331.tab, bf16[128,8192]{1,0:T(8,128)(2,1)} %bitcast.162, bf16[256,8192]{1,0:T(8,128)(2,1)} %bitcast.156, bf16[384,4096]{1,0:T(8,128)(2,1)} %collective-permute-done.3.other.refs_2_), custom_call_target="tpu_custom_call" | custom-call | bytes 12582912 | tf_op jit(solution)/shard_map/turned/pallas_call | solution.py:141
  34.5 11.7 %collective-permute-done.refs_4_ = bf16[512,768]{1,0:T(8,128)(2,1)S(1)} collective-permute-done((bf16[512,768]{1,0:T(8,128)(2,1)S(1)}, bf16[512,768]{1,0:T(8,128)(2,1)S(1)}, u32[]{:S(2)}, u32[]{:S(2)}) %collective-permute-start) | collective-permute-done | bytes 786464 | tf_op jit(solution)/shard_map/ppermute | solution.py:41
  46.5 3.0 %collective-permute-start.6 = (bf16[512,768]{1,0:T(8,128)(2,1)S(1)}, bf16[512,768]{1,0:T(8,128)(2,1)S(1)}, u32[]{:S(2)}, u32[]{:S(2)}) collective-permute-start(bf16[512,768]{1,0:T(8,128)(2,1)S(1)} %constant_dynamic-slice_fusion.refs_3_), channel_id=1, source_target_pairs={{0,4},{2,6},{4,0},{6,2},{8,12},{10,14},{12,8},{14,10},{16,20},{18,... | collective-permute-start | bytes 2359304 | tf_op jit(solution)/shard_map/ppermute | solution.py:41
  49.6 3.8 %broadcast_in_dim.99 = bf16[4,8,2,64,512]{4,3,2,1,0:T(8,128)(2,1)} broadcast(bf16[8,2,64,512]{3,2,1,0:T(8,128)(2,1)} %all-to-all-done), dimensions={1,2,3,4} | broadcast | bytes 5242880 | tf_op jit(solution)/shard_map/broadcast_in_dim | solution.py:512
  53.4 5.3 %all-to-all-start.1 = ((bf16[4,8,2,64,512]{4,3,2,1,0:T(8,128)(2,1)}), bf16[4,8,2,64,512]{4,3,2,1,0:T(8,128)(2,1)}, u32[]{:S(2)}, u32[]{:S(2)}) async-start(bf16[4,8,2,64,512]{4,3,2,1,0:T(8,128)(2,1)} %broadcast_in_dim.99), calls=%async_computation.1 | async-start | bytes 8388608 | tf_op jit(solution)/shard_map/all_to_all | solution.py:512
  58.7 1.3 broadcast_select_fusion.1
  60.5 2.7 %collective-permute-start.5 = (bf16[512,768]{1,0:T(8,128)(2,1)}, bf16[512,768]{1,0:T(8,128)(2,1)}, u32[]{:S(2)}, u32[]{:S(2)}) collective-permute-start(bf16[512,768]{1,0:T(8,128)(2,1)} %get-tuple-element.97), channel_id=1, source_target_pairs={{0,6},{2,0},{4,2},{6,4},{8,25},{10,27},{12,29},{14,31},{16,22},{18... | collective-permute-start | bytes 2359304 | tf_op jit(solution)/shard_map/ppermute | solution.py:41
  63.3 7.4 %project.3 = (f32[384,768]{1,0:T(8,128)}, f32[384,768]{1,0:T(8,128)}) custom-call(s32[5]{0:T(128)S(1)} %stack.337.tab, bf16[128,8192]{1,0:T(8,128)(2,1)} %bitcast.163, bf16[256,8192]{1,0:T(8,128)(2,1)} %bitcast.157, bf16[384,4096]{1,0:T(8,128)(2,1)} %collective-permute-done.3.other.refs_2_, bf16[512,768]{1,0:T(8,128)(2,1)S(1)} %constant_dynamic-slice_fusion.refs_3_, ...), custom_call_target="tpu_custom_call" | custom-call | flops 2415919104 | bytes 8650752 | tf_op jit(solution)/shard_map/project/pallas_call | solution.py:194
  70.7 9.4 %turned.3.cot = bf16[4096,768]{1,0:T(8,128)(2,1)} custom-call(s32[65]{0:T(128)S(1)} %stack.331.tab, bf16[128,8192]{1,0:T(8,128)(2,1)} %bitcast.172, bf16[256,8192]{1,0:T(8,128)(2,1)} %bitcast.168, bf16[384,4096]{1,0:T(8,128)(2,1)} %collective-permute-done.7.other), custom_call_target="tpu_custom_call" | custom-call | bytes 12582912 | tf_op jit(solution)/shard_map/turned/pallas_call | solution.py:141
  80.5 7.0 %project.4 = (f32[384,768]{1,0:T(8,128)}, f32[384,768]{1,0:T(8,128)}) custom-call(s32[4]{0:T(128)S(1)} %pad_add_fusion.3.tab, bf16[128,8192]{1,0:T(8,128)(2,1)} %bitcast.164, bf16[256,8192]{1,0:T(8,128)(2,1)} %bitcast.158, bf16[384,4096]{1,0:T(8,128)(2,1)} %collective-permute-done.3.other.refs_2_, bf16[512,768]{1,0:T(8,128)(2,1)S(1)} %collective-permute-done.6.refs_3_, ...), custom_call_target="tpu_custom_call" | custom-call | flops 1811939328 | bytes 7077888 | tf_op jit(solution)/shard_map/project/pallas_call | solution.py:194
  87.5 6.3 %collective-permute-done.8.refs_3_ = bf16[512,768]{1,0:T(8,128)(2,1)S(1)} collective-permute-done((bf16[512,768]{1,0:T(8,128)(2,1)S(1)}, bf16[512,768]{1,0:T(8,128)(2,1)S(1)}, u32[]{:S(2)}, u32[]{:S(2)}) %collective-permute-start.8) | collective-permute-done | bytes 786464 | tf_op jit(solution)/shard_map/ppermute | solution.py:41
  94.7 3.5 %project.5 = (f32[384,768]{1,0:T(8,128)S(1)}, f32[384,768]{1,0:T(8,128)}) custom-call(s32[2]{0:T(128)S(1)} %pad_add_fusion.4.tab, bf16[128,8192]{1,0:T(8,128)(2,1)} %bitcast.165, bf16[256,8192]{1,0:T(8,128)(2,1)} %bitcast.159, bf16[384,4096]{1,0:T(8,128)(2,1)} %collective-permute-done.3.other.refs_2_, bf16[512,768]{1,0:T(8,128)(2,1)S(1)} %collective-permute-done.8.refs_3_), custom_call_target="tpu_custom_call" | custom-call | flops 603979776 | bytes 3932160 | tf_op jit(solution)/shard_map/project/pallas_call | solution.py:194
  99.6 1.6 collective-permute-done.10.far_got
  101.8 6.7 %all-to-all-done.1.w.mine = bf16[4,8,2,64,512]{4,3,2,1,0:T(8,128)(2,1)} async-done(((bf16[4,8,2,64,512]{4,3,2,1,0:T(8,128)(2,1)}), bf16[4,8,2,64,512]{4,3,2,1,0:T(8,128)(2,1)}, u32[]{:S(2)}, u32[]{:S(2)}) %all-to-all-start.1) | async-done | bytes 4194336 | tf_op jit(solution)/shard_map/all_to_all | solution.py:512
  109.5 3.7 %all-to-all-start.2 = ((bf16[16,128,256]{2,1,0:T(8,128)(2,1)}), bf16[16,128,256]{2,1,0:T(8,128)(2,1)S(1)}, u32[]{:S(2)}, u32[]{:S(2)}) async-start(bf16[16,128,256]{2,1,0:T(8,128)(2,1)} %broadcast_in_dim.98), calls=%async_computation.2 | async-start | bytes 2097152 | tf_op jit(solution)/shard_map/all_to_all | solution.py:567
  113.3 9.5 %grad_attended.1 = (f32[384,512]{1,0:T(8,128)S(1)}, f32[384,512]{1,0:T(8,128)S(1)}) custom-call(s32[1]{0:T(128)} %bitcast.1.core_ref.tab, bf16[128,8192]{1,0:T(8,128)(2,1)} %bitcast.173, bf16[256,8192]{1,0:T(8,128)(2,1)} %bitcast.169, bf16[384,4096]{1,0:T(8,128)(2,1)} %collective-permute-done.7.other, bf16[4,8,2,64,512]{4,3,2,1,0:T(8,128)(2,1)} %all-to-all-done.1.w.mine), custom_call_target="tpu_custom_call" | custom-call | flops 3221225472 | bytes 10485760 | tf_op jit(solution)/shard_map/grad_attended/pallas_call | solution.py:346
  126.1 2.5 short_attention.1
  130.9 1.1 copy-done.8
  132.1 5.0 %video_attention.1 = (bf16[2,128,512]{2,1,0:T(8,128)(2,1)S(1)}, bf16[2048,256]{1,0:T(8,128)(2,1)S(1)}) custom-call(s32[1]{0:T(128)} %bitcast.72.tab, bf16[384,512]{1,0:T(8,128)(2,1)S(1)} %copy-done.11, bf16[2048,256]{1,0:T(8,128)(2,1)S(1)} %bitcast.152, s32[1,8,128]{2,1,0:T(8,128)S(1)} %broadcast_in_dim.100.segments, f32[384,512]{1,0:T(8,128)S(1)} %copy-done.6, ...), custom_call_target="tpu_custom_call" | custom-call | flops 1342177280 | bytes 2097152 | tf_op jit(solution)/shard_map/video_attention/pallas_call | solution.py:292
  138.0 4.8 %all-to-all-start.3 = ((bf16[16,128,256]{2,1,0:T(8,128)(2,1)}), bf16[16,128,256]{2,1,0:T(8,128)(2,1)S(1)}, u32[]{:S(2)}, u32[]{:S(2)}) async-start(bf16[16,128,256]{2,1,0:T(8,128)(2,1)} %bitcast.151), calls=%async_computation.3 | async-start | bytes 2097152 | tf_op jit(solution)/shard_map/all_to_all | solution.py:586
  144.7 5.4 %term.7 = bf16[2,1024,512]{2,1,0:T(8,128)(2,1)} custom-call(s32[1]{0:T(128)} %bitcast.93.tab, bf16[4096,768]{1,0:T(8,128)(2,1)} %turned.3.cot, bf16[4096,768]{1,0:T(8,128)(2,1)} %turned.2.tokens, bf16[2,128,512]{2,1,0:T(8,128)(2,1)S(1)} %get-tuple-element.77.video_att.refs_0_, bf16[2,256,512]{2,1,0:T(8,128)(2,1)S(1)} %get-tuple-element.76.short_att.refs_1_, ...), custom_call_target="tpu_custom_call" | custom-call | flops 1610612736 | bytes 6815744 | tf_op jit(solution)/shard_map/term/pallas_call | solution.py:410
  150.1 3.1 %collective-permute-start.18 = (bf16[2,1024,512]{2,1,0:T(8,128)(2,1)}, bf16[2,1024,512]{2,1,0:T(8,128)(2,1)}, u32[]{:S(2)}, u32[]{:S(2)}) collective-permute-start(bf16[2,1024,512]{2,1,0:T(8,128)(2,1)} %term.7), channel_id=1, source_target_pairs={{0,96},{2,98},{4,100},{6,102},{8,14},{10,8},{12,10},{14,12},{16,11... | collective-permute-start | bytes 6291464 | tf_op jit(solution)/shard_map/ppermute | solution.py:41
  153.2 5.4 %term.6 = bf16[2,1024,512]{2,1,0:T(8,128)(2,1)} custom-call(s32[1]{0:T(128)} %bitcast.91.tab, bf16[4096,768]{1,0:T(8,128)(2,1)} %turned.3.cot, bf16[4096,768]{1,0:T(8,128)(2,1)} %turned.2.tokens, bf16[2,128,512]{2,1,0:T(8,128)(2,1)S(1)} %get-tuple-element.77.video_att.refs_0_, bf16[2,256,512]{2,1,0:T(8,128)(2,1)S(1)} %get-tuple-element.76.short_att.refs_1_, ...), custom_call_target="tpu_custom_call" | custom-call | flops 1610612736 | bytes 6815744 | tf_op jit(solution)/shard_map/term/pallas_call | solution.py:410
  158.6 5.4 %term.5 = bf16[2,1024,512]{2,1,0:T(8,128)(2,1)} custom-call(s32[1]{0:T(128)} %bitcast.89.tab, bf16[4096,768]{1,0:T(8,128)(2,1)} %turned.3.cot, bf16[4096,768]{1,0:T(8,128)(2,1)} %turned.2.tokens, bf16[2,128,512]{2,1,0:T(8,128)(2,1)S(1)} %get-tuple-element.77.video_att.refs_0_, bf16[2,256,512]{2,1,0:T(8,128)(2,1)S(1)} %get-tuple-element.76.short_att.refs_1_, ...), custom_call_target="tpu_custom_call" | custom-call | flops 1610612736 | bytes 6815744 | tf_op jit(solution)/shard_map/term/pallas_call | solution.py:410
  164.0 2.3 collective-permute-start.16
  166.9 1.4 collective-permute-done.13.gb
  168.5 5.8 %key_term.1 = bf16[4,1040,256]{2,1,0:T(8,128)(2,1)} custom-call(s32[1]{0:T(128)} %bitcast.tab, bf16[4,4,4,64,768]{4,3,2,1,0:T(8,128)(2,1)} %bitcast.153, bf16[384,256]{1,0:T(8,128)(2,1)S(1)} %pad_maximum_fusion.1.ga, bf16[384,256]{1,0:T(8,128)(2,1)S(1)} %collective-permute-done.13.gb, bf16[16,256]{1,0:T(8,128)(2,1)S(1)} %maximum_maximum_fusion.tail), custom_call_target="tpu_custom_call" | custom-call | flops 1610612736 | bytes 8388608 | tf_op jit(solution)/shard_map/key_term/pallas_call | solution.py:464
  174.3 4.5 %all-to-all-start.4 = ((bf16[4,1040,256]{2,1,0:T(8,128)(2,1)}), bf16[4,1040,256]{2,1,0:T(8,128)(2,1)}, u32[]{:S(2)}, u32[]{:S(2)}) async-start(bf16[4,1040,256]{2,1,0:T(8,128)(2,1)} %key_term.1), calls=%async_computation.4 | async-start | bytes 4259840 | tf_op jit(solution)/shard_map/all_to_all | solution.py:601
  178.8 5.4 %term.4 = bf16[2,1024,512]{2,1,0:T(8,128)(2,1)} custom-call(s32[1]{0:T(128)} %bitcast.87.tab, bf16[4096,768]{1,0:T(8,128)(2,1)} %turned.3.cot, bf16[4096,768]{1,0:T(8,128)(2,1)} %turned.2.tokens, bf16[2,128,512]{2,1,0:T(8,128)(2,1)S(1)} %get-tuple-element.77.video_att.refs_0_, bf16[2,256,512]{2,1,0:T(8,128)(2,1)S(1)} %get-tuple-element.76.short_att.refs_1_, ...), custom_call_target="tpu_custom_call" | custom-call | flops 1610612736 | bytes 6815744 | tf_op jit(solution)/shard_map/term/pallas_call | solution.py:410
  184.3 9.5 %layer_out.1 = (bf16[128,8192]{1,0:T(8,128)(2,1)}, bf16[256,8192]{1,0:T(8,128)(2,1)}) custom-call(s32[1]{0:T(128)} %bitcast.1.core_ref.tab, bf16[2,128,512]{2,1,0:T(8,128)(2,1)S(1)} %get-tuple-element.77.video_att.refs_0_, bf16[2,256,512]{2,1,0:T(8,128)(2,1)S(1)} %get-tuple-element.76.short_att.refs_1_, bf16[4,8,2,64,512]{4,3,2,1,0:T(8,128)(2,1)} %all-to-all-done.1.w.mine, ...), custom_call_target="tpu_custom_call" | custom-call | flops 3221225472 | bytes 14680064 | tf_op jit(solution)/shard_map/layer_out/pallas_call | solution.py:365
  193.8 14.8 %collective-permute-done.17 = bf16[2,1024,512]{2,1,0:T(8,128)(2,1)} collective-permute-done((bf16[2,1024,512]{2,1,0:T(8,128)(2,1)}, bf16[2,1024,512]{2,1,0:T(8,128)(2,1)}, u32[]{:S(2)}, u32[]{:S(2)}) %collective-permute-start.17) | collective-permute-done | bytes 2097184 | tf_op jit(solution)/shard_map/ppermute | solution.py:41
  208.6 5.0 %fusion = (bf16[2,256,512]{2,1,0:T(8,128)(2,1)S(1)}, bf16[2,256,512]{2,1,0:T(8,128)(2,1)}, f32[2,256,512]{2,1,0:T(8,128)S(1)}, bf16[2,256,512]{2,1,0:T(8,128)(2,1)}) fusion(bf16[2,4,256,512]{3,2,1,0:T(8,128)(2,1)} %bitcast.94, s32[]{:T(128)S(6)} %select_n.503, bf16[2,4,256,512]{3,2,1,0:T(8,128)(2,1)} %bitcast.92, bf16[2,4,256,512]{3,2,1,0:T(8,128)(2,1)} %bitcast.90, ...), kind=kLoop, calls=%fused_computation.10 | loop fusion | flops 8126464 | bytes 11010064 | tf_op jit(solution)/shard_map/add | solution.py:432
  213.6 1.2 collective-permute-start.21
  217.2 1.9 slice_reduce_fusion
  219.1 4.0 %collective-permute-done.21 = bf16[2,256,512]{2,1,0:T(8,128)(2,1)S(1)} collective-permute-done((bf16[2,256,512]{2,1,0:T(8,128)(2,1)}, bf16[2,256,512]{2,1,0:T(8,128)(2,1)S(1)}, u32[]{:S(2)}, u32[]{:S(2)}) %collective-permute-start.21) | collective-permute-done | bytes 524320 | tf_op jit(solution)/shard_map/ppermute | solution.py:41
  223.0 8.0 %collective-permute-done.20 = bf16[2,256,512]{2,1,0:T(8,128)(2,1)S(1)} collective-permute-done((bf16[2,256,512]{2,1,0:T(8,128)(2,1)}, bf16[2,256,512]{2,1,0:T(8,128)(2,1)S(1)}, u32[]{:S(2)}, u32[]{:S(2)}) %collective-permute-start.20) | collective-permute-done | bytes 524320 | tf_op jit(solution)/shard_map/ppermute | solution.py:41
  232.2 2.4 collective-permute-start.24
  234.6 2.0 collective-permute-start.22
  237.6 3.6 %all-to-all-start.5 = ((bf16[16,80,256]{2,1,0:T(8,128)(2,1)}), bf16[16,80,256]{2,1,0:T(8,128)(2,1)S(1)}, u32[]{:S(2)}, u32[]{:S(2)}) async-start(bf16[16,80,256]{2,1,0:T(8,128)(2,1)} %pad_maximum_fusion), calls=%async_computation.5 | async-start | bytes 1310720 | tf_op jit(solution)/shard_map/all_to_all | solution.py:486
  241.2 1.2 collective-permute-done.23
  242.4 1.2 fusion.16
  244.3 7.7 %all-to-all-done.5 = bf16[16,80,256]{2,1,0:T(8,128)(2,1)S(1)} async-done(((bf16[16,80,256]{2,1,0:T(8,128)(2,1)}), bf16[16,80,256]{2,1,0:T(8,128)(2,1)S(1)}, u32[]{:S(2)}, u32[]{:S(2)}) %all-to-all-start.5) | async-done | bytes 655392 | tf_op jit(solution)/shard_map/all_to_all | solution.py:486
  (151 shorter events, 22.8 us)
Async XLA Ops:
  0.6 13.3 %copy-start = (bf16[1024,768]{1,0:T(8,128)(2,1)S(1)}, bf16[1024,768]{1,0:T(8,128)(2,1)}, u32[]{:S(2)}) copy-start(bf16[1024,768]{1,0:T(8,128)(2,1)} %param.10) | copy-start | bytes 4718596
  0.7 4.5 %copy-start.3 = (bf16[64,8192]{1,0:T(8,128)(2,1)S(1)}, bf16[64,8192]{1,0:T(8,128)(2,1)}, u32[]{:S(2)}) copy-start(bf16[64,8192]{1,0:T(8,128)(2,1)} %block.1) | copy-start | bytes 3145732
  5.1 20.0 %collective-permute-start.3 = (bf16[384,4096]{1,0:T(8,128)(2,1)}, bf16[384,4096]{1,0:T(8,128)(2,1)}, u32[]{:S(2)}, u32[]{:S(2)}) collective-permute-start(bf16[384,4096]{1,0:T(8,128)(2,1)} %halves.2), channel_id=1, source_target_pairs={{0,8},{2,10},{4,12},{6,14},{8,0},{10,2},{12,4},{14,6},{16,24},{18,... | collective-permute-start | bytes 9437192 | tf_op jit(solution)/shard_map/ppermute | solution.py:41
  6.9 39.6 %all-to-all-start = ((bf16[8,2,64,512]{3,2,1,0:T(8,128)(2,1)}), bf16[8,2,64,512]{3,2,1,0:T(8,128)(2,1)}, u32[]{:S(2)}, u32[]{:S(2)}) async-start(bf16[8,2,64,512]{3,2,1,0:T(8,128)(2,1)} %broadcast_in_dim.88), calls=%async_computation | async-start | bytes 2097152 | tf_op jit(solution)/shard_map/all_to_all | solution.py:512
  14.0 32.3 %collective-permute-start = (bf16[512,768]{1,0:T(8,128)(2,1)S(1)}, bf16[512,768]{1,0:T(8,128)(2,1)S(1)}, u32[]{:S(2)}, u32[]{:S(2)}) collective-permute-start(bf16[512,768]{1,0:T(8,128)(2,1)S(1)} %constant_dynamic-slice_fusion.refs_3_), channel_id=1, source_target_pairs={{0,2},{2,4},{4,6},{6,0},{8,10},{10,12},{12,14},{14,8},{16,18},{18,... | collective-permute-start | bytes 2359304 | tf_op jit(solution)/shard_map/ppermute | solution.py:41
  16.0 30.2 %collective-permute-start.1 = (bf16[512,768]{1,0:T(8,128)(2,1)S(1)}, bf16[512,768]{1,0:T(8,128)(2,1)}, u32[]{:S(2)}, u32[]{:S(2)}) collective-permute-start(bf16[512,768]{1,0:T(8,128)(2,1)S(1)} %constant_dynamic-slice_fusion.refs_3_), channel_id=1, source_target_pairs={{0,6},{2,0},{4,2},{6,4},{8,14},{10,8},{12,10},{14,12},{16,22},{18,... | collective-permute-start | bytes 2359304 | tf_op jit(solution)/shard_map/ppermute | solution.py:41
  17.3 29.2 %collective-permute-start.2 = (bf16[512,768]{1,0:T(8,128)(2,1)S(1)}, bf16[512,768]{1,0:T(8,128)(2,1)S(1)}, u32[]{:S(2)}, u32[]{:S(2)}) collective-permute-start(bf16[512,768]{1,0:T(8,128)(2,1)S(1)} %constant_dynamic-slice_fusion.refs_3_), channel_id=1, source_target_pairs={{0,17},{2,19},{4,21},{6,23},{8,25},{10,27},{12,29},{14,31},{16,1},... | collective-permute-start | bytes 2359304 | tf_op jit(solution)/shard_map/ppermute | solution.py:41
  46.5 12.2 %copy-start.13 = (bf16[512,768]{1,0:T(8,128)(2,1)}, bf16[512,768]{1,0:T(8,128)(2,1)S(1)}, u32[]{:S(2)}) copy-start(bf16[512,768]{1,0:T(8,128)(2,1)S(1)} %collective-permute-done.2.refs_6_) | copy-start | bytes 2359300
  46.5 24.2 %collective-permute-start.7 = (bf16[384,4096]{1,0:T(8,128)(2,1)}, bf16[384,4096]{1,0:T(8,128)(2,1)}, u32[]{:S(2)}, u32[]{:S(2)}) collective-permute-start(bf16[384,4096]{1,0:T(8,128)(2,1)} %halves.3), channel_id=1, source_target_pairs={{0,8},{2,10},{4,12},{6,14},{8,0},{10,2},{12,4},{14,6},{16,24},{18,... | collective-permute-start | bytes 9437192 | tf_op jit(solution)/shard_map/ppermute | solution.py:41
  46.5 33.6 %collective-permute-start.6 = (bf16[512,768]{1,0:T(8,128)(2,1)S(1)}, bf16[512,768]{1,0:T(8,128)(2,1)S(1)}, u32[]{:S(2)}, u32[]{:S(2)}) collective-permute-start(bf16[512,768]{1,0:T(8,128)(2,1)S(1)} %constant_dynamic-slice_fusion.refs_3_), channel_id=1, source_target_pairs={{0,4},{2,6},{4,0},{6,2},{8,12},{10,14},{12,8},{14,10},{16,20},{18,... | collective-permute-start | bytes 2359304 | tf_op jit(solution)/shard_map/ppermute | solution.py:41
  53.4 55.1 %all-to-all-start.1 = ((bf16[4,8,2,64,512]{4,3,2,1,0:T(8,128)(2,1)}), bf16[4,8,2,64,512]{4,3,2,1,0:T(8,128)(2,1)}, u32[]{:S(2)}, u32[]{:S(2)}) async-start(bf16[4,8,2,64,512]{4,3,2,1,0:T(8,128)(2,1)} %broadcast_in_dim.99), calls=%async_computation.1 | async-start | bytes 8388608 | tf_op jit(solution)/shard_map/all_to_all | solution.py:512
  59.9 20.2 %collective-permute-start.4 = (bf16[512,768]{1,0:T(8,128)(2,1)}, bf16[512,768]{1,0:T(8,128)(2,1)S(1)}, u32[]{:S(2)}, u32[]{:S(2)}) collective-permute-start(bf16[512,768]{1,0:T(8,128)(2,1)} %get-tuple-element.98), channel_id=1, source_target_pairs={{0,2},{2,4},{4,6},{6,0},{8,25},{10,27},{12,29},{14,31},{16,18},{18... | collective-permute-start | bytes 2359304 | tf_op jit(solution)/shard_map/ppermute | solution.py:41
  60.5 19.7 %collective-permute-start.5 = (bf16[512,768]{1,0:T(8,128)(2,1)}, bf16[512,768]{1,0:T(8,128)(2,1)}, u32[]{:S(2)}, u32[]{:S(2)}) collective-permute-start(bf16[512,768]{1,0:T(8,128)(2,1)} %get-tuple-element.97), channel_id=1, source_target_pairs={{0,6},{2,0},{4,2},{6,4},{8,25},{10,27},{12,29},{14,31},{16,22},{18... | collective-permute-start | bytes 2359304 | tf_op jit(solution)/shard_map/ppermute | solution.py:41
  70.7 9.5 %copy-start.14 = (bf16[512,768]{1,0:T(8,128)(2,1)S(1)}, bf16[512,768]{1,0:T(8,128)(2,1)}, u32[]{:S(2)}) copy-start(bf16[512,768]{1,0:T(8,128)(2,1)} %copy-done.13) | copy-start | bytes 2359300
  80.3 13.6 %collective-permute-start.8 = (bf16[512,768]{1,0:T(8,128)(2,1)S(1)}, bf16[512,768]{1,0:T(8,128)(2,1)S(1)}, u32[]{:S(2)}, u32[]{:S(2)}) collective-permute-start(bf16[512,768]{1,0:T(8,128)(2,1)S(1)} %broadcast_select_fusion), channel_id=1, source_target_pairs={{0,4},{2,6},{4,0},{6,2},{8,25},{10,27},{12,29},{14,31},{16,20},{18... | collective-permute-start | bytes 2359304 | tf_op jit(solution)/shard_map/ppermute | solution.py:41
  93.9 4.3 %copy-start.28 = (s32[3,1,256]{2,1,0:T(1,128)S(1)}, s32[3,1,256]{2,1,0:T(1,128)}, u32[]{:S(2)}) copy-start(s32[3,1,256]{2,1,0:T(1,128)} %param.16) | copy-start | bytes 9220
  93.9 4.3 %copy-start.29 = (s32[3,1,128]{2,1,0:T(1,128)S(1)}, s32[3,1,128]{2,1,0:T(1,128)}, u32[]{:S(2)}) copy-start(s32[3,1,128]{2,1,0:T(1,128)} %param.14) | copy-start | bytes 4612
  93.9 5.7 %collective-permute-start.9 = (f32[384,768]{1,0:T(8,128)}, f32[384,768]{1,0:T(8,128)S(1)}, u32[]{:S(2)}, u32[]{:S(2)}) collective-permute-start(f32[384,768]{1,0:T(8,128)} %get-tuple-element.61), channel_id=1, source_target_pairs={{0,8},{2,10},{4,12},{6,14},{8,0},{10,2},{12,4},{14,6},{16,24},{18,... | collective-permute-start | bytes 3538952 | tf_op jit(solution)/shard_map/ppermute | solution.py:41
  98.2 3.1 %collective-permute-start.10 = (f32[384,768]{1,0:T(8,128)}, f32[384,768]{1,0:T(8,128)S(1)}, u32[]{:S(2)}, u32[]{:S(2)}) collective-permute-start(f32[384,768]{1,0:T(8,128)} %get-tuple-element.64), channel_id=1, source_target_pairs={{0,8},{2,10},{4,12},{6,14},{8,0},{10,2},{12,4},{14,6},{16,24},{18,... | collective-permute-start | bytes 3538952 | tf_op jit(solution)/shard_map/ppermute | solution.py:41
  101.8 7.8 %copy-start.9 = (bf16[384,512]{1,0:T(8,128)(2,1)}, bf16[384,512]{1,0:T(8,128)(2,1)S(1)}, u32[]{:S(2)}) copy-start(bf16[384,512]{1,0:T(8,128)(2,1)S(1)} %get-tuple-element.65.queries) | copy-start | bytes 1179652
  109.5 20.2 %collective-permute-start.11 = (bf16[4,8,2,64,512]{4,3,2,1,0:T(8,128)(2,1)}, bf16[4,8,2,64,512]{4,3,2,1,0:T(8,128)(2,1)}, u32[]{:S(2)}, u32[]{:S(2)}) collective-permute-start(bf16[4,8,2,64,512]{4,3,2,1,0:T(8,128)(2,1)} %all-to-all-done.1.w.mine), channel_id=1, source_target_pairs={{0,8},{2,10},{4,12},{6,14},{8,0},{10,2},{12,4},{14,6},{16,24},{18,... | collective-permute-start | bytes 12582920 | tf_op jit(solution)/shard_map/ppermute | solution.py:41
  109.5 20.2 %all-to-all-start.2 = ((bf16[16,128,256]{2,1,0:T(8,128)(2,1)}), bf16[16,128,256]{2,1,0:T(8,128)(2,1)S(1)}, u32[]{:S(2)}, u32[]{:S(2)}) async-start(bf16[16,128,256]{2,1,0:T(8,128)(2,1)} %broadcast_in_dim.98), calls=%async_computation.2 | async-start | bytes 2097152 | tf_op jit(solution)/shard_map/all_to_all | solution.py:567
  113.2 10.1 %copy-start.16 = (f32[384,64]{1,0:T(8,128)S(1)}, f32[384,64]{1,0:T(8,128)}, u32[]{:S(2)}) copy-start(f32[384,64]{1,0:T(8,128)} %copy-done.15) | copy-start | bytes 294916
  113.2 10.1 %copy-start.18 = (f32[384,64]{1,0:T(8,128)S(1)}, f32[384,64]{1,0:T(8,128)}, u32[]{:S(2)}) copy-start(f32[384,64]{1,0:T(8,128)} %copy-done.17) | copy-start | bytes 294916
  113.2 10.1 %copy-start.21 = (f32[384,64]{1,0:T(8,128)S(1)}, f32[384,64]{1,0:T(8,128)}, u32[]{:S(2)}) copy-start(f32[384,64]{1,0:T(8,128)} %copy-done.20) | copy-start | bytes 294916
  113.2 10.2 %copy-start.26 = (s32[1,256]{1,0:T(1,128)S(1)}, s32[1,256]{1,0:T(1,128)}, u32[]{:S(2)}) copy-start(s32[1,256]{1,0:T(1,128)} %param.17) | copy-start | bytes 3076
  122.8 2.4 collective-permute-start.12
  124.1 5.7 %copy-start.11 = (bf16[384,512]{1,0:T(8,128)(2,1)S(1)}, bf16[384,512]{1,0:T(8,128)(2,1)}, u32[]{:S(2)}) copy-start(bf16[384,512]{1,0:T(8,128)(2,1)} %copy-done.9) | copy-start | bytes 1179652
  128.6 15.0 %collective-permute-start.15 = (bf16[2,256,512]{2,1,0:T(8,128)(2,1)S(1)}, bf16[2,256,512]{2,1,0:T(8,128)(2,1)S(1)}, u32[]{:S(2)}, u32[]{:S(2)}) collective-permute-start(bf16[2,256,512]{2,1,0:T(8,128)(2,1)S(1)} %get-tuple-element.76.short_att.refs_1_), channel_id=1, source_target_pairs={{0,8},{2,10},{4,12},{6,14},{8,0},{10,2},{12,4},{14,6},{16,24},{18,... | collective-permute-start | bytes 1572872 | tf_op jit(solution)/shard_map/ppermute | solution.py:41
  138.0 4.8 %copy-start.19 = (f32[384,64]{1,0:T(8,128)S(1)}, f32[384,64]{1,0:T(8,128)}, u32[]{:S(2)}) copy-start(f32[384,64]{1,0:T(8,128)} %copy-done.17) | copy-start | bytes 294916
  138.0 4.8 %copy-start.22 = (f32[384,64]{1,0:T(8,128)S(1)}, f32[384,64]{1,0:T(8,128)}, u32[]{:S(2)}) copy-start(f32[384,64]{1,0:T(8,128)} %copy-done.20) | copy-start | bytes 294916
  138.0 28.3 %all-to-all-start.3 = ((bf16[16,128,256]{2,1,0:T(8,128)(2,1)}), bf16[16,128,256]{2,1,0:T(8,128)(2,1)S(1)}, u32[]{:S(2)}, u32[]{:S(2)}) async-start(bf16[16,128,256]{2,1,0:T(8,128)(2,1)} %bitcast.151), calls=%async_computation.3 | async-start | bytes 2097152 | tf_op jit(solution)/shard_map/all_to_all | solution.py:586
  143.1 1.6 collective-permute-start.14
  150.1 43.7 %collective-permute-start.18 = (bf16[2,1024,512]{2,1,0:T(8,128)(2,1)}, bf16[2,1024,512]{2,1,0:T(8,128)(2,1)}, u32[]{:S(2)}, u32[]{:S(2)}) collective-permute-start(bf16[2,1024,512]{2,1,0:T(8,128)(2,1)} %term.7), channel_id=1, source_target_pairs={{0,96},{2,98},{4,100},{6,102},{8,14},{10,8},{12,10},{14,12},{16,11... | collective-permute-start | bytes 6291464 | tf_op jit(solution)/shard_map/ppermute | solution.py:41
  158.6 50.0 %collective-permute-start.17 = (bf16[2,1024,512]{2,1,0:T(8,128)(2,1)}, bf16[2,1024,512]{2,1,0:T(8,128)(2,1)}, u32[]{:S(2)}, u32[]{:S(2)}) collective-permute-start(bf16[2,1024,512]{2,1,0:T(8,128)(2,1)} %term.6), channel_id=1, source_target_pairs={{0,32},{2,34},{4,36},{6,38},{8,10},{10,12},{12,14},{14,8},{16,48},... | collective-permute-start | bytes 6291464 | tf_op jit(solution)/shard_map/ppermute | solution.py:41
  164.0 44.6 %collective-permute-start.16 = (bf16[2,1024,512]{2,1,0:T(8,128)(2,1)}, bf16[2,1024,512]{2,1,0:T(8,128)(2,1)}, u32[]{:S(2)}, u32[]{:S(2)}) collective-permute-start(bf16[2,1024,512]{2,1,0:T(8,128)(2,1)} %term.5), channel_id=1, source_target_pairs={{0,64},{2,66},{4,68},{6,70},{8,12},{10,14},{12,8},{14,10},{16,80},... | collective-permute-start | bytes 6291464 | tf_op jit(solution)/shard_map/ppermute | solution.py:41
  166.6 1.7 collective-permute-start.13
  174.3 42.0 %all-to-all-start.4 = ((bf16[4,1040,256]{2,1,0:T(8,128)(2,1)}), bf16[4,1040,256]{2,1,0:T(8,128)(2,1)}, u32[]{:S(2)}, u32[]{:S(2)}) async-start(bf16[4,1040,256]{2,1,0:T(8,128)(2,1)} %key_term.1), calls=%async_computation.4 | async-start | bytes 4259840 | tf_op jit(solution)/shard_map/all_to_all | solution.py:601
  184.3 24.4 %copy-start.12 = (bf16[2,1024,512]{2,1,0:T(8,128)(2,1)S(1)}, bf16[2,1024,512]{2,1,0:T(8,128)(2,1)}, u32[]{:S(2)}) copy-start(bf16[2,1024,512]{2,1,0:T(8,128)(2,1)} %term.4) | copy-start | bytes 6291460
  213.6 9.4 %collective-permute-start.21 = (bf16[2,256,512]{2,1,0:T(8,128)(2,1)}, bf16[2,256,512]{2,1,0:T(8,128)(2,1)S(1)}, u32[]{:S(2)}, u32[]{:S(2)}) collective-permute-start(bf16[2,256,512]{2,1,0:T(8,128)(2,1)} %get-tuple-element.93), channel_id=1, source_target_pairs={{0,6},{2,0},{4,2},{6,4},{8,104},{10,106},{12,108},{14,110},{16,22}... | collective-permute-start | bytes 1572872 | tf_op jit(solution)/shard_map/ppermute | solution.py:41
  214.8 16.2 %collective-permute-start.20 = (bf16[2,256,512]{2,1,0:T(8,128)(2,1)}, bf16[2,256,512]{2,1,0:T(8,128)(2,1)S(1)}, u32[]{:S(2)}, u32[]{:S(2)}) collective-permute-start(bf16[2,256,512]{2,1,0:T(8,128)(2,1)} %get-tuple-element.91), channel_id=1, source_target_pairs={{0,2},{2,4},{4,6},{6,0},{8,40},{10,42},{12,44},{14,46},{16,18},{18... | collective-permute-start | bytes 1572872 | tf_op jit(solution)/shard_map/ppermute | solution.py:41
  215.6 15.4 %collective-permute-start.19 = (bf16[2,256,512]{2,1,0:T(8,128)(2,1)S(1)}, bf16[2,256,512]{2,1,0:T(8,128)(2,1)S(1)}, u32[]{:S(2)}, u32[]{:S(2)}) collective-permute-start(bf16[2,256,512]{2,1,0:T(8,128)(2,1)S(1)} %get-tuple-element.90), channel_id=1, source_target_pairs={{0,4},{2,6},{4,0},{6,2},{8,72},{10,74},{12,76},{14,78},{16,20},{18... | collective-permute-start | bytes 1572872 | tf_op jit(solution)/shard_map/ppermute | solution.py:41
  223.0 8.0 %copy-start.23 = (bf16[2,256,512]{2,1,0:T(8,128)(2,1)}, bf16[2,256,512]{2,1,0:T(8,128)(2,1)S(1)}, u32[]{:S(2)}) copy-start(bf16[2,256,512]{2,1,0:T(8,128)(2,1)S(1)} %collective-permute-done.21) | copy-start | bytes 1572868
  232.2 9.0 %collective-permute-start.24 = (bf16[2,64,512]{2,1,0:T(8,128)(2,1)}, bf16[2,64,512]{2,1,0:T(8,128)(2,1)S(1)}, u32[]{:S(2)}, u32[]{:S(2)}) collective-permute-start(bf16[2,64,512]{2,1,0:T(8,128)(2,1)} %get-tuple-element.95), channel_id=1, source_target_pairs={{0,17},{2,19},{4,21},{6,23},{8,25},{10,27},{12,29},{14,31},{16,0},... | collective-permute-start | bytes 393224 | tf_op jit(solution)/shard_map/ppermute | solution.py:41
  234.6 7.8 %collective-permute-start.23 = (bf16[2,64,512]{2,1,0:T(8,128)(2,1)}, bf16[2,64,512]{2,1,0:T(8,128)(2,1)S(1)}, u32[]{:S(2)}, u32[]{:S(2)}) collective-permute-start(bf16[2,64,512]{2,1,0:T(8,128)(2,1)} %get-tuple-element.96), channel_id=1, source_target_pairs={{0,16},{2,18},{4,20},{6,22},{8,24},{10,26},{12,28},{14,30},{16,1},... | collective-permute-start | bytes 393224 | tf_op jit(solution)/shard_map/ppermute | solution.py:41
  234.6 7.8 %collective-permute-start.22 = (bf16[2,64,512]{2,1,0:T(8,128)(2,1)}, bf16[2,64,512]{2,1,0:T(8,128)(2,1)}, u32[]{:S(2)}, u32[]{:S(2)}) collective-permute-start(bf16[2,64,512]{2,1,0:T(8,128)(2,1)} %get-tuple-element.94), channel_id=1, source_target_pairs={{0,1},{2,3},{4,5},{6,7},{8,9},{10,11},{12,13},{14,15},{16,17},{18,... | collective-permute-start | bytes 393224 | tf_op jit(solution)/shard_map/ppermute | solution.py:41
  236.6 16.7 %copy-start.1 = (bf16[1024,768]{1,0:T(8,128)(2,1)S(1)}, bf16[1024,768]{1,0:T(8,128)(2,1)}, u32[]{:S(2)}) copy-start(bf16[1024,768]{1,0:T(8,128)(2,1)} %param.10) | copy-start | bytes 4718596
  237.6 14.4 %all-to-all-start.5 = ((bf16[16,80,256]{2,1,0:T(8,128)(2,1)}), bf16[16,80,256]{2,1,0:T(8,128)(2,1)S(1)}, u32[]{:S(2)}, u32[]{:S(2)}) async-start(bf16[16,80,256]{2,1,0:T(8,128)(2,1)} %pad_maximum_fusion), calls=%async_computation.5 | async-start | bytes 1310720 | tf_op jit(solution)/shard_map/all_to_all | solution.py:486
  (13 other events, 23.6 us)

commit v3 on v2

--- a/solution.py
+++ b/solution.py
@@ -423,7 +423,7 @@
     return sum((g.astype(F32) for g in got), own).astype(BF)
 
 
-def scatter(places, cot, tokens, rights):
+def scatter(places, cot, tokens, rights, parts):
     got = [to_first(term(places[0] + far, cot, tokens, rights), far) for far in (2, 1, 3)]
     first = [f.reshape(2, 4, 256, ATT) for f in [term(places[0], cot, tokens, rights)] + got]
 
@@ -431,12 +431,17 @@
         place = (places[1] + far) % 4
         return sum(lax.dynamic_index_in_dim(f, place, 1, keepdims=False).astype(F32) for f in first)
 
-    got = [to_second(rows(far).astype(BF), far) for far in (2, 1, 3)]
+    got = []
+    for far in (2, 1, 3):
+        chunk = rows(far).astype(BF)
+        *first, chunk = lax.optimization_barrier((*first, chunk))
+        got.append(to_second(chunk, far))
+    *got, parts = lax.optimization_barrier((*got, parts))
     piece = lambda far: sum(
         (g[:, far * 64 : (far + 1) * 64].astype(F32) for g in got), rows(0)[:, far * 64 : (far + 1) * 64]
     )
     late = [to_y(piece(far).astype(BF), far) for far in (2, 1, 3)]
-    return sum((g.astype(F32) for g in late), piece(0))
+    return sum((g.astype(F32) for g in late), piece(0)), parts
 
 
 def tail_of(row):
@@ -479,10 +484,13 @@
 ]
 
 
-def scatter_with_tail(terms):
+def key_parts(terms):
     first = jnp.sum(terms[:, :1024].astype(F32), axis=0).astype(BF).reshape(16, 64, 256)
     tail = tail_of(tail_sum([terms[k, 1024:] for k in range(4)]))
-    parts = jnp.concatenate([first, jnp.broadcast_to(tail[None], (16, TAIL, 256))], axis=1)
+    return jnp.concatenate([first, jnp.broadcast_to(tail[None], (16, TAIL, 256))], axis=1)
+
+
+def key_sum(parts):
     parts = lax.all_to_all(parts, AXES, 0, 0, tiled=True, axis_index_groups=LATE_GROUPS)
     total = jnp.sum(parts.astype(F32), axis=0)
     return total[:64], total[64:67] + total[67:70]
@@ -529,12 +537,15 @@
     mine = lax.dynamic_slice(w_qkv, (at["c"] * 512, 0), (512, 768))
     x_other = other_core(halves(1 - core, video_x, short_x))
     x_turned = turned(order, video_x, short_x, x_other)
-    first, third, facing, quarters, x_turned, x_other, c_send = lax.optimization_barrier((
-        to_x(mine, 1), to_x(mine, 3), across(mine),
-        to_all(weight_quarter(numbers(at["c"], at["z"]), w_out), DP, 8),
-        x_turned, x_other, halves(1 - core, video_cot, short_cot),
+    quarters = to_all(weight_quarter(numbers(at["c"], at["z"]), w_out), DP, 8)
+    wide, later_cot, x_turned = lax.optimization_barrier(
+        (jnp.broadcast_to(quarters[None], (4,) + quarters.shape), video_cot, x_turned)
+    )
+    wo = lax.all_to_all(wide, ("z",), 0, 0)
+    first, third, facing, x_turned, x_other, c_send = lax.optimization_barrier((
+        to_x(mine, 1), to_x(mine, 3), across(mine), x_turned, x_other,
+        halves(1 - core, later_cot, short_cot),
     ))
-    wo = to_all(quarters, ("z",), 4)
     c_other = other_core(c_send)
     relay = lambda near: jnp.where(at["c"] == 0, facing, near)
     shard = lambda step, yh: ((at["x"] - step + 4) % 4) * 2 + yh
@@ -588,7 +599,6 @@
     results = (video_result, short_result, other_core(video_result), other_core(short_result))
     place = jnp.where(at["c"] == 0, at["z"], at["x"])
     second_place = jnp.where(at["c"] == 0, at["x"], at["z"])
-    grad_out, grad_q = scatter((place, second_place), c_turned, x_turned, results)
 
     video_dkv = collect(arrived, cosines[:nv], sines[:nv])
     dkv = jnp.concatenate([video_dkv, short_dkv], axis=0)
@@ -600,7 +610,10 @@
     terms, video_y, short_y = lax.optimization_barrier(
         (lax.all_to_all(terms, ("yl", "yh"), 0, 0, tiled=True), video_y, short_y)
     )
-    grad_kv, bias = scatter_with_tail(terms)
+    (grad_out, grad_q), parts = scatter(
+        (place, second_place), c_turned, x_turned, results, key_parts(terms)
+    )
+    grad_kv, bias = key_sum(parts)
     return (
         video_y[None],
         short_y[None],

time: 256 us -> 249 us (0.973)
  waiting for transfers between devices: 66.5 us -> 45.2 us
  starting transfers between devices: 56.9 us -> 67.6 us
  other arithmetic: 15.3 us -> 19.3 us
    ppermute x25, waiting for transfers between devices: 51.4 us -> 26.7 us  [move(): return lax.ppermute(value, AXES, pairs(target))]
    all_to_all x1 -> x2, starting transfers between devices: 3.59 us -> 14.9 us  [the longest x1 9.64 us: key_sum(): lax.all_to_all(parts, AXES, 0, 0, tiled=True, axis_index_groups=LATE_GROUPS)]
    all_to_all x1 -> x2, waiting for transfers between devices: 7.68 us -> 15.8 us  [the longest x1 9.13 us: key_sum(): lax.all_to_all(parts, AXES, 0, 0, tiled=True, axis_index_groups=LATE_GROUPS)]
    all_to_all x2 -> x1, starting transfers between devices: 12.3 us -> 7.01 us  [to_all(): lax.all_to_all(jnp.broadcast_to(value[None], (count,) + value.shape), axe...]
    all_to_all x2 -> x1, waiting for transfers between devices: 6.66 us -> 2.02 us  [to_all(): lax.all_to_all(jnp.broadcast_to(value[None], (count,) + value.shape), axe...]
    ppermute x25, starting transfers between devices: 28.1 us -> 32.5 us  [move(): return lax.ppermute(value, AXES, pairs(target))]
    add x1 -> x4, other arithmetic: 4.99 us -> 8.93 us  [rows(): sum((lax.dynamic_index_in_dim(f, place, 1, keepdims=False).astype(F32) fo...]
    broadcast_in_dim x1 -> x2, local copies, waits for them, and re-layouts: 0.01 us -> 3.81 us  [the longest x1 3.8 us: per_device(): jnp.broadcast_to(quarters[None], (4,) + quarters.shape)]
  transfers between devices with their start and end apart: 31 -> 31, of which waited for: 14 -> 14; matrix products, arithmetic and copies ran while one was open for 8% -> 10% of each run, Pallas kernels for 38% -> 39%
where the time goes in v3:
time: 249 us; the launch traced here: 247 us
  Pallas kernels  101 us (41%)
  starting transfers between devices  67.6 us (27%)
  waiting for transfers between devices  45.2 us (18%)
  other arithmetic  19.3 us (8%)
  local copies, waits for them, and re-layouts  12.5 us (5%)
    ppermute x25, starting transfers between devices, move(): return lax.ppermute(value, AXES, pairs(target))  32.5 us
    ppermute x25, waiting for transfers between devices, move(): return lax.ppermute(value, AXES, pairs(target))  26.7 us
    pallas_call x4, Pallas kernels, term(): call(term_kernel, 'term', (4,), [((512, wide), lambda i, s: (2 * s[0] + j...  21.7 us
    pallas_call x2, Pallas kernels, turned(): call(turn_kernel, 'turned', (8,), [own(nv), own(ns), ((rows, 512), lambda...  18.9 us
    pallas_call x3, Pallas kernels, project(): call(functools.partial(project_kernel, parts=parts, added=len(before) > 0...  17.9 us
    all_to_all x1, starting transfers between devices, key_sum(): lax.all_to_all(parts, AXES, 0, 0, tiled=True, axis_index_groups=LATE_GROUPS)  9.64 us
    pallas_call x1, Pallas kernels, layer_out(): call(layer_out_kernel, 'layer_out', (8,), [att(nv), att(ns), W_BLOCK, W_B...  9.54 us
    pallas_call x1, Pallas kernels, grad_attended_parts(): call(grad_attended_kernel, 'grad_attended', (8,), [own(nv), own(ns), ((ro...  9.52 us
  transfers between devices with their start and end apart: 31, of which 14 were waited for; matrix products, arithmetic and copies ran while one was open for 10% of the time, Pallas kernels for 39%

profile of v3, /device:TPU:0, one launch (start us, length us, event | category | flops | bytes accessed | tf_op | source)
XLA Modules:
  0.0 246.7 jit_solution(6231029583556799563)
XLA Ops:
  0.7 4.4 %halves.2 = bf16[384,4096]{1,0:T(8,128)(2,1)} custom-call(s32[1]{0:T(128)S(6)} %sub.8.core_ref, bf16[128,8192]{1,0:T(8,128)(2,1)} %bitcast.136, bf16[128,8192]{1,0:T(8,128)(2,1)} %bitcast.137, bf16[256,8192]{1,0:T(8,128)(2,1)} %bitcast.130, bf16[256,8192]{1,0:T(8,128)(2,1)} %bitcast.131), custom_call_target="tpu_custom_call" | custom-call | bytes 6291456 | tf_op jit(solution)/shard_map/halves/pallas_call | solution.py:119
  6.9 7.0 %all-to-all-start = ((bf16[8,2,64,512]{3,2,1,0:T(8,128)(2,1)}), bf16[8,2,64,512]{3,2,1,0:T(8,128)(2,1)}, u32[]{:S(2)}, u32[]{:S(2)}) async-start(bf16[8,2,64,512]{3,2,1,0:T(8,128)(2,1)} %broadcast_in_dim.88), calls=%async_computation | async-start | bytes 2097152 | tf_op jit(solution)/shard_map/all_to_all | solution.py:520
  14.0 2.1 collective-permute-start
  17.3 3.3 %collective-permute-start.2 = (bf16[512,768]{1,0:T(8,128)(2,1)S(1)}, bf16[512,768]{1,0:T(8,128)(2,1)S(1)}, u32[]{:S(2)}, u32[]{:S(2)}) collective-permute-start(bf16[512,768]{1,0:T(8,128)(2,1)S(1)} %constant_dynamic-slice_fusion.refs_3_), channel_id=1, source_target_pairs={{0,17},{2,19},{4,21},{6,23},{8,25},{10,27},{12,29},{14,31},{16,1},... | collective-permute-start | bytes 2359304 | tf_op jit(solution)/shard_map/ppermute | solution.py:41
  20.7 9.4 %turned.2.tokens = bf16[4096,768]{1,0:T(8,128)(2,1)} custom-call(s32[65]{0:T(128)S(1)} %stack.331.tab, bf16[128,8192]{1,0:T(8,128)(2,1)} %bitcast.138, bf16[256,8192]{1,0:T(8,128)(2,1)} %bitcast.132, bf16[384,4096]{1,0:T(8,128)(2,1)} %collective-permute-done.3.other.refs_2_), custom_call_target="tpu_custom_call" | custom-call | bytes 12582912 | tf_op jit(solution)/shard_map/turned/pallas_call | solution.py:141
  30.2 2.0 all-to-all-done
  32.2 3.8 %broadcast_in_dim.89 = bf16[4,8,2,64,512]{4,3,2,1,0:T(8,128)(2,1)} broadcast(bf16[8,2,64,512]{3,2,1,0:T(8,128)(2,1)} %all-to-all-done), dimensions={1,2,3,4} | broadcast | bytes 5242880 | tf_op jit(solution)/shard_map/broadcast_in_dim | solution.py:542
  36.0 4.4 %halves.3 = bf16[384,4096]{1,0:T(8,128)(2,1)} custom-call(s32[1]{0:T(128)S(6)} %sub.8.core_ref, bf16[128,8192]{1,0:T(8,128)(2,1)} %bitcast.146, bf16[128,8192]{1,0:T(8,128)(2,1)} %bitcast.147, bf16[256,8192]{1,0:T(8,128)(2,1)} %bitcast.142, bf16[256,8192]{1,0:T(8,128)(2,1)} %bitcast.143), custom_call_target="tpu_custom_call" | custom-call | bytes 6291456 | tf_op jit(solution)/shard_map/halves/pallas_call | solution.py:119
  40.4 5.8 %collective-permute-done.refs_4_ = bf16[512,768]{1,0:T(8,128)(2,1)S(1)} collective-permute-done((bf16[512,768]{1,0:T(8,128)(2,1)S(1)}, bf16[512,768]{1,0:T(8,128)(2,1)S(1)}, u32[]{:S(2)}, u32[]{:S(2)}) %collective-permute-start) | collective-permute-done | bytes 786464 | tf_op jit(solution)/shard_map/ppermute | solution.py:41
  46.5 3.0 %collective-permute-start.6 = (bf16[512,768]{1,0:T(8,128)(2,1)S(1)}, bf16[512,768]{1,0:T(8,128)(2,1)S(1)}, u32[]{:S(2)}, u32[]{:S(2)}) collective-permute-start(bf16[512,768]{1,0:T(8,128)(2,1)S(1)} %constant_dynamic-slice_fusion.refs_3_), channel_id=1, source_target_pairs={{0,4},{2,6},{4,0},{6,2},{8,12},{10,14},{12,8},{14,10},{16,20},{18,... | collective-permute-start | bytes 2359304 | tf_op jit(solution)/shard_map/ppermute | solution.py:41
  49.5 5.3 %all-to-all-start.1 = ((bf16[4,8,2,64,512]{4,3,2,1,0:T(8,128)(2,1)}), bf16[4,8,2,64,512]{4,3,2,1,0:T(8,128)(2,1)}, u32[]{:S(2)}, u32[]{:S(2)}) async-start(bf16[4,8,2,64,512]{4,3,2,1,0:T(8,128)(2,1)} %broadcast_in_dim.89), calls=%async_computation.1 | async-start | bytes 8388608 | tf_op jit(solution)/shard_map/all_to_all | solution.py:544
  56.6 2.7 %collective-permute-start.5 = (bf16[512,768]{1,0:T(8,128)(2,1)}, bf16[512,768]{1,0:T(8,128)(2,1)}, u32[]{:S(2)}, u32[]{:S(2)}) collective-permute-start(bf16[512,768]{1,0:T(8,128)(2,1)} %get-tuple-element.135), channel_id=1, source_target_pairs={{0,6},{2,0},{4,2},{6,4},{8,25},{10,27},{12,29},{14,31},{16,22},{18... | collective-permute-start | bytes 2359304 | tf_op jit(solution)/shard_map/ppermute | solution.py:41
  59.4 7.4 %project.3 = (f32[384,768]{1,0:T(8,128)}, f32[384,768]{1,0:T(8,128)}) custom-call(s32[5]{0:T(128)S(1)} %stack.337.tab, bf16[128,8192]{1,0:T(8,128)(2,1)} %bitcast.139, bf16[256,8192]{1,0:T(8,128)(2,1)} %bitcast.133, bf16[384,4096]{1,0:T(8,128)(2,1)} %collective-permute-done.3.other.refs_2_, bf16[512,768]{1,0:T(8,128)(2,1)S(1)} %constant_dynamic-slice_fusion.refs_3_, ...), custom_call_target="tpu_custom_call" | custom-call | flops 2415919104 | bytes 8650752 | tf_op jit(solution)/shard_map/project/pallas_call | solution.py:194
  66.9 9.4 %turned.3.cot = bf16[4096,768]{1,0:T(8,128)(2,1)} custom-call(s32[65]{0:T(128)S(1)} %stack.331.tab, bf16[128,8192]{1,0:T(8,128)(2,1)} %bitcast.148, bf16[256,8192]{1,0:T(8,128)(2,1)} %bitcast.144, bf16[384,4096]{1,0:T(8,128)(2,1)} %collective-permute-done.7.other), custom_call_target="tpu_custom_call" | custom-call | bytes 12582912 | tf_op jit(solution)/shard_map/turned/pallas_call | solution.py:141
  76.6 2.9 %collective-permute-start.8 = (bf16[512,768]{1,0:T(8,128)(2,1)S(1)}, bf16[512,768]{1,0:T(8,128)(2,1)S(1)}, u32[]{:S(2)}, u32[]{:S(2)}) collective-permute-start(bf16[512,768]{1,0:T(8,128)(2,1)S(1)} %broadcast_select_fusion), channel_id=1, source_target_pairs={{0,4},{2,6},{4,0},{6,2},{8,25},{10,27},{12,29},{14,31},{16,20},{18... | collective-permute-start | bytes 2359304 | tf_op jit(solution)/shard_map/ppermute | solution.py:41
  79.7 7.0 %project.4 = (f32[384,768]{1,0:T(8,128)}, f32[384,768]{1,0:T(8,128)}) custom-call(s32[4]{0:T(128)S(1)} %pad_add_fusion.3.tab, bf16[128,8192]{1,0:T(8,128)(2,1)} %bitcast.140, bf16[256,8192]{1,0:T(8,128)(2,1)} %bitcast.134, bf16[384,4096]{1,0:T(8,128)(2,1)} %collective-permute-done.3.other.refs_2_, bf16[512,768]{1,0:T(8,128)(2,1)S(1)} %collective-permute-done.6.refs_3_, ...), custom_call_target="tpu_custom_call" | custom-call | flops 1811939328 | bytes 7077888 | tf_op jit(solution)/shard_map/project/pallas_call | solution.py:194
  86.6 3.6 %collective-permute-done.8.refs_3_ = bf16[512,768]{1,0:T(8,128)(2,1)S(1)} collective-permute-done((bf16[512,768]{1,0:T(8,128)(2,1)S(1)}, bf16[512,768]{1,0:T(8,128)(2,1)S(1)}, u32[]{:S(2)}, u32[]{:S(2)}) %collective-permute-start.8) | collective-permute-done | bytes 786464 | tf_op jit(solution)/shard_map/ppermute | solution.py:41
  90.9 3.5 %project.5 = (f32[384,768]{1,0:T(8,128)S(1)}, f32[384,768]{1,0:T(8,128)}) custom-call(s32[2]{0:T(128)S(1)} %pad_add_fusion.4.tab, bf16[128,8192]{1,0:T(8,128)(2,1)} %bitcast.141, bf16[256,8192]{1,0:T(8,128)(2,1)} %bitcast.135, bf16[384,4096]{1,0:T(8,128)(2,1)} %collective-permute-done.3.other.refs_2_, bf16[512,768]{1,0:T(8,128)(2,1)S(1)} %collective-permute-done.8.refs_3_), custom_call_target="tpu_custom_call" | custom-call | flops 603979776 | bytes 3932160 | tf_op jit(solution)/shard_map/project/pallas_call | solution.py:194
  95.8 1.6 collective-permute-done.10.far_got
  98.0 6.7 %all-to-all-done.1.w.mine = bf16[4,8,2,64,512]{4,3,2,1,0:T(8,128)(2,1)} async-done(((bf16[4,8,2,64,512]{4,3,2,1,0:T(8,128)(2,1)}), bf16[4,8,2,64,512]{4,3,2,1,0:T(8,128)(2,1)}, u32[]{:S(2)}, u32[]{:S(2)}) %all-to-all-start.1) | async-done | bytes 4194336 | tf_op jit(solution)/shard_map/all_to_all | solution.py:544
  105.7 3.7 %all-to-all-start.2 = ((bf16[16,128,256]{2,1,0:T(8,128)(2,1)}), bf16[16,128,256]{2,1,0:T(8,128)(2,1)S(1)}, u32[]{:S(2)}, u32[]{:S(2)}) async-start(bf16[16,128,256]{2,1,0:T(8,128)(2,1)} %broadcast_in_dim.99), calls=%async_computation.2 | async-start | bytes 2097152 | tf_op jit(solution)/shard_map/all_to_all | solution.py:578
  109.4 9.5 %grad_attended.1 = (f32[384,512]{1,0:T(8,128)S(1)}, f32[384,512]{1,0:T(8,128)S(1)}) custom-call(s32[1]{0:T(128)} %bitcast.1.core_ref.tab, bf16[128,8192]{1,0:T(8,128)(2,1)} %bitcast.149, bf16[256,8192]{1,0:T(8,128)(2,1)} %bitcast.145, bf16[384,4096]{1,0:T(8,128)(2,1)} %collective-permute-done.7.other, bf16[4,8,2,64,512]{4,3,2,1,0:T(8,128)(2,1)} %all-to-all-done.1.w.mine), custom_call_target="tpu_custom_call" | custom-call | flops 3221225472 | bytes 10485760 | tf_op jit(solution)/shard_map/grad_attended/pallas_call | solution.py:346
  122.3 2.5 short_attention.1
  128.2 5.0 %video_attention.1 = (bf16[2,128,512]{2,1,0:T(8,128)(2,1)S(1)}, bf16[2048,256]{1,0:T(8,128)(2,1)S(1)}) custom-call(s32[1]{0:T(128)} %bitcast.72.tab, bf16[384,512]{1,0:T(8,128)(2,1)S(1)} %copy-done.11, bf16[2048,256]{1,0:T(8,128)(2,1)S(1)} %bitcast.128, s32[1,8,128]{2,1,0:T(8,128)S(1)} %broadcast_in_dim.100.segments, f32[384,512]{1,0:T(8,128)S(1)} %copy-done.6, ...), custom_call_target="tpu_custom_call" | custom-call | flops 1342177280 | bytes 2097152 | tf_op jit(solution)/shard_map/video_attention/pallas_call | solution.py:292
  134.2 5.0 %all-to-all-start.3 = ((bf16[16,128,256]{2,1,0:T(8,128)(2,1)}), bf16[16,128,256]{2,1,0:T(8,128)(2,1)S(1)}, u32[]{:S(2)}, u32[]{:S(2)}) async-start(bf16[16,128,256]{2,1,0:T(8,128)(2,1)} %bitcast.127), calls=%async_computation.3 | async-start | bytes 2097152 | tf_op jit(solution)/shard_map/all_to_all | solution.py:597
  139.2 5.4 %term.5 = bf16[2,1024,512]{2,1,0:T(8,128)(2,1)} custom-call(s32[1]{0:T(128)} %bitcast.89.tab, bf16[4096,768]{1,0:T(8,128)(2,1)} %turned.3.cot, bf16[4096,768]{1,0:T(8,128)(2,1)} %turned.2.tokens, bf16[2,128,512]{2,1,0:T(8,128)(2,1)S(1)} %get-tuple-element.100.video_att.refs_0_, bf16[2,256,512]{2,1,0:T(8,128)(2,1)S(1)} %get-tuple-element.99.short_att.refs_1_, ...), custom_call_target="tpu_custom_call" | custom-call | flops 1610612736 | bytes 6815744 | tf_op jit(solution)/shard_map/term/pallas_call | solution.py:410
  144.7 3.4 %collective-permute-start.16 = (bf16[2,1024,512]{2,1,0:T(8,128)(2,1)}, bf16[2,1024,512]{2,1,0:T(8,128)(2,1)}, u32[]{:S(2)}, u32[]{:S(2)}) collective-permute-start(bf16[2,1024,512]{2,1,0:T(8,128)(2,1)} %term.5), channel_id=1, source_target_pairs={{0,64},{2,66},{4,68},{6,70},{8,12},{10,14},{12,8},{14,10},{16,80},... | collective-permute-start | bytes 6291464 | tf_op jit(solution)/shard_map/ppermute | solution.py:41
  148.1 5.4 %term.6 = bf16[2,1024,512]{2,1,0:T(8,128)(2,1)} custom-call(s32[1]{0:T(128)} %bitcast.91.tab, bf16[4096,768]{1,0:T(8,128)(2,1)} %turned.3.cot, bf16[4096,768]{1,0:T(8,128)(2,1)} %turned.2.tokens, bf16[2,128,512]{2,1,0:T(8,128)(2,1)S(1)} %get-tuple-element.100.video_att.refs_0_, bf16[2,256,512]{2,1,0:T(8,128)(2,1)S(1)} %get-tuple-element.99.short_att.refs_1_, ...), custom_call_target="tpu_custom_call" | custom-call | flops 1610612736 | bytes 6815744 | tf_op jit(solution)/shard_map/term/pallas_call | solution.py:410
  154.1 5.4 %term.7 = bf16[2,1024,512]{2,1,0:T(8,128)(2,1)} custom-call(s32[1]{0:T(128)} %bitcast.93.tab, bf16[4096,768]{1,0:T(8,128)(2,1)} %turned.3.cot, bf16[4096,768]{1,0:T(8,128)(2,1)} %turned.2.tokens, bf16[2,128,512]{2,1,0:T(8,128)(2,1)S(1)} %get-tuple-element.100.video_att.refs_0_, bf16[2,256,512]{2,1,0:T(8,128)(2,1)S(1)} %get-tuple-element.99.short_att.refs_1_, ...), custom_call_target="tpu_custom_call" | custom-call | flops 1610612736 | bytes 6815744 | tf_op jit(solution)/shard_map/term/pallas_call | solution.py:410
  159.5 2.7 %collective-permute-start.18 = (bf16[2,1024,512]{2,1,0:T(8,128)(2,1)}, bf16[2,1024,512]{2,1,0:T(8,128)(2,1)}, u32[]{:S(2)}, u32[]{:S(2)}) collective-permute-start(bf16[2,1024,512]{2,1,0:T(8,128)(2,1)} %term.7), channel_id=1, source_target_pairs={{0,96},{2,98},{4,100},{6,102},{8,14},{10,8},{12,10},{14,12},{16,11... | collective-permute-start | bytes 6291464 | tf_op jit(solution)/shard_map/ppermute | solution.py:41
  163.2 1.4 collective-permute-done.13.gb
  164.7 5.8 %key_term.1 = bf16[4,1040,256]{2,1,0:T(8,128)(2,1)} custom-call(s32[1]{0:T(128)} %bitcast.tab, bf16[4,4,4,64,768]{4,3,2,1,0:T(8,128)(2,1)} %bitcast.129, bf16[384,256]{1,0:T(8,128)(2,1)S(1)} %pad_maximum_fusion.1.ga, bf16[384,256]{1,0:T(8,128)(2,1)S(1)} %collective-permute-done.13.gb, bf16[16,256]{1,0:T(8,128)(2,1)S(1)} %maximum_maximum_fusion.tail), custom_call_target="tpu_custom_call" | custom-call | flops 1610612736 | bytes 8388608 | tf_op jit(solution)/shard_map/key_term/pallas_call | solution.py:469
  170.5 4.5 %all-to-all-start.4 = ((bf16[4,1040,256]{2,1,0:T(8,128)(2,1)}), bf16[4,1040,256]{2,1,0:T(8,128)(2,1)}, u32[]{:S(2)}, u32[]{:S(2)}) async-start(bf16[4,1040,256]{2,1,0:T(8,128)(2,1)} %key_term.1), calls=%async_computation.4 | async-start | bytes 4259840 | tf_op jit(solution)/shard_map/all_to_all | solution.py:611
  175.0 5.4 %term.4 = bf16[2,1024,512]{2,1,0:T(8,128)(2,1)} custom-call(s32[1]{0:T(128)} %bitcast.87.tab, bf16[4096,768]{1,0:T(8,128)(2,1)} %turned.3.cot, bf16[4096,768]{1,0:T(8,128)(2,1)} %turned.2.tokens, bf16[2,128,512]{2,1,0:T(8,128)(2,1)S(1)} %get-tuple-element.100.video_att.refs_0_, bf16[2,256,512]{2,1,0:T(8,128)(2,1)S(1)} %get-tuple-element.99.short_att.refs_1_, ...), custom_call_target="tpu_custom_call" | custom-call | flops 1610612736 | bytes 6815744 | tf_op jit(solution)/shard_map/term/pallas_call | solution.py:410
  180.5 9.5 %layer_out.1 = (bf16[128,8192]{1,0:T(8,128)(2,1)}, bf16[256,8192]{1,0:T(8,128)(2,1)}) custom-call(s32[1]{0:T(128)} %bitcast.1.core_ref.tab, bf16[2,128,512]{2,1,0:T(8,128)(2,1)S(1)} %get-tuple-element.100.video_att.refs_0_, bf16[2,256,512]{2,1,0:T(8,128)(2,1)S(1)} %get-tuple-element.99.short_att.refs_1_, bf16[4,8,2,64,512]{4,3,2,1,0:T(8,128)(2,1)} %all-to-all-done.1.w.mine, ...), custom_call_target="tpu_custom_call" | custom-call | flops 3221225472 | bytes 14680064 | tf_op jit(solution)/shard_map/layer_out/pallas_call | solution.py:365
  190.0 10.1 %collective-permute-done.17 = bf16[2,1024,512]{2,1,0:T(8,128)(2,1)} collective-permute-done((bf16[2,1024,512]{2,1,0:T(8,128)(2,1)}, bf16[2,1024,512]{2,1,0:T(8,128)(2,1)}, u32[]{:S(2)}, u32[]{:S(2)}) %collective-permute-start.17) | collective-permute-done | bytes 2097184 | tf_op jit(solution)/shard_map/ppermute | solution.py:41
  200.1 2.4 fusion
  203.2 2.4 fusion.1
  205.6 1.5 collective-permute-start.20
  207.0 2.4 fusion.2
  209.5 1.8 collective-permute-start.21
  211.3 1.6 add_bitcast_fusion
  213.8 1.9 slice_reduce_fusion
  216.6 2.5 %collective-permute-done.20 = bf16[2,256,512]{2,1,0:T(8,128)(2,1)S(1)} collective-permute-done((bf16[2,256,512]{2,1,0:T(8,128)(2,1)}, bf16[2,256,512]{2,1,0:T(8,128)(2,1)S(1)}, u32[]{:S(2)}, u32[]{:S(2)}) %collective-permute-start.20) | collective-permute-done | bytes 524320 | tf_op jit(solution)/shard_map/ppermute | solution.py:41
  220.3 2.3 collective-permute-start.24
  222.6 2.0 collective-permute-start.22
  224.6 9.6 %all-to-all-start.5 = ((bf16[16,80,256]{2,1,0:T(8,128)(2,1)}), bf16[16,80,256]{2,1,0:T(8,128)(2,1)S(1)}, u32[]{:S(2)}, u32[]{:S(2)}) async-start(bf16[16,80,256]{2,1,0:T(8,128)(2,1)} %pad_maximum_fusion), calls=%async_computation.5 | async-start | bytes 1310720 | tf_op jit(solution)/shard_map/all_to_all | solution.py:494
  236.2 9.1 %all-to-all-done.5 = bf16[16,80,256]{2,1,0:T(8,128)(2,1)S(1)} async-done(((bf16[16,80,256]{2,1,0:T(8,128)(2,1)}), bf16[16,80,256]{2,1,0:T(8,128)(2,1)S(1)}, u32[]{:S(2)}, u32[]{:S(2)}) %all-to-all-start.5) | async-done | bytes 655392 | tf_op jit(solution)/shard_map/all_to_all | solution.py:494
  (154 shorter events, 25.8 us)
Async XLA Ops:
  0.6 13.3 %copy-start = (bf16[1024,768]{1,0:T(8,128)(2,1)S(1)}, bf16[1024,768]{1,0:T(8,128)(2,1)}, u32[]{:S(2)}) copy-start(bf16[1024,768]{1,0:T(8,128)(2,1)} %param.10) | copy-start | bytes 4718596
  0.7 4.5 %copy-start.3 = (bf16[64,8192]{1,0:T(8,128)(2,1)S(1)}, bf16[64,8192]{1,0:T(8,128)(2,1)}, u32[]{:S(2)}) copy-start(bf16[64,8192]{1,0:T(8,128)(2,1)} %block.1) | copy-start | bytes 3145732
  5.1 15.7 %collective-permute-start.3 = (bf16[384,4096]{1,0:T(8,128)(2,1)}, bf16[384,4096]{1,0:T(8,128)(2,1)}, u32[]{:S(2)}, u32[]{:S(2)}) collective-permute-start(bf16[384,4096]{1,0:T(8,128)(2,1)} %halves.2), channel_id=1, source_target_pairs={{0,8},{2,10},{4,12},{6,14},{8,0},{10,2},{12,4},{14,6},{16,24},{18,... | collective-permute-start | bytes 9437192 | tf_op jit(solution)/shard_map/ppermute | solution.py:41
  6.9 25.3 %all-to-all-start = ((bf16[8,2,64,512]{3,2,1,0:T(8,128)(2,1)}), bf16[8,2,64,512]{3,2,1,0:T(8,128)(2,1)}, u32[]{:S(2)}, u32[]{:S(2)}) async-start(bf16[8,2,64,512]{3,2,1,0:T(8,128)(2,1)} %broadcast_in_dim.88), calls=%async_computation | async-start | bytes 2097152 | tf_op jit(solution)/shard_map/all_to_all | solution.py:520
  14.0 32.3 %collective-permute-start = (bf16[512,768]{1,0:T(8,128)(2,1)S(1)}, bf16[512,768]{1,0:T(8,128)(2,1)S(1)}, u32[]{:S(2)}, u32[]{:S(2)}) collective-permute-start(bf16[512,768]{1,0:T(8,128)(2,1)S(1)} %constant_dynamic-slice_fusion.refs_3_), channel_id=1, source_target_pairs={{0,2},{2,4},{4,6},{6,0},{8,10},{10,12},{12,14},{14,8},{16,18},{18,... | collective-permute-start | bytes 2359304 | tf_op jit(solution)/shard_map/ppermute | solution.py:41
  16.0 30.2 %collective-permute-start.1 = (bf16[512,768]{1,0:T(8,128)(2,1)S(1)}, bf16[512,768]{1,0:T(8,128)(2,1)}, u32[]{:S(2)}, u32[]{:S(2)}) collective-permute-start(bf16[512,768]{1,0:T(8,128)(2,1)S(1)} %constant_dynamic-slice_fusion.refs_3_), channel_id=1, source_target_pairs={{0,6},{2,0},{4,2},{6,4},{8,14},{10,8},{12,10},{14,12},{16,22},{18,... | collective-permute-start | bytes 2359304 | tf_op jit(solution)/shard_map/ppermute | solution.py:41
  17.3 29.2 %collective-permute-start.2 = (bf16[512,768]{1,0:T(8,128)(2,1)S(1)}, bf16[512,768]{1,0:T(8,128)(2,1)S(1)}, u32[]{:S(2)}, u32[]{:S(2)}) collective-permute-start(bf16[512,768]{1,0:T(8,128)(2,1)S(1)} %constant_dynamic-slice_fusion.refs_3_), channel_id=1, source_target_pairs={{0,17},{2,19},{4,21},{6,23},{8,25},{10,27},{12,29},{14,31},{16,1},... | collective-permute-start | bytes 2359304 | tf_op jit(solution)/shard_map/ppermute | solution.py:41
  46.5 8.3 %copy-start.13 = (bf16[512,768]{1,0:T(8,128)(2,1)}, bf16[512,768]{1,0:T(8,128)(2,1)S(1)}, u32[]{:S(2)}) copy-start(bf16[512,768]{1,0:T(8,128)(2,1)S(1)} %collective-permute-done.2.refs_6_) | copy-start | bytes 2359300
  46.5 20.4 %collective-permute-start.7 = (bf16[384,4096]{1,0:T(8,128)(2,1)}, bf16[384,4096]{1,0:T(8,128)(2,1)}, u32[]{:S(2)}, u32[]{:S(2)}) collective-permute-start(bf16[384,4096]{1,0:T(8,128)(2,1)} %halves.3), channel_id=1, source_target_pairs={{0,8},{2,10},{4,12},{6,14},{8,0},{10,2},{12,4},{14,6},{16,24},{18,... | collective-permute-start | bytes 9437192 | tf_op jit(solution)/shard_map/ppermute | solution.py:41
  46.5 29.8 %collective-permute-start.6 = (bf16[512,768]{1,0:T(8,128)(2,1)S(1)}, bf16[512,768]{1,0:T(8,128)(2,1)S(1)}, u32[]{:S(2)}, u32[]{:S(2)}) collective-permute-start(bf16[512,768]{1,0:T(8,128)(2,1)S(1)} %constant_dynamic-slice_fusion.refs_3_), channel_id=1, source_target_pairs={{0,4},{2,6},{4,0},{6,2},{8,12},{10,14},{12,8},{14,10},{16,20},{18,... | collective-permute-start | bytes 2359304 | tf_op jit(solution)/shard_map/ppermute | solution.py:41
  49.5 55.2 %all-to-all-start.1 = ((bf16[4,8,2,64,512]{4,3,2,1,0:T(8,128)(2,1)}), bf16[4,8,2,64,512]{4,3,2,1,0:T(8,128)(2,1)}, u32[]{:S(2)}, u32[]{:S(2)}) async-start(bf16[4,8,2,64,512]{4,3,2,1,0:T(8,128)(2,1)} %broadcast_in_dim.89), calls=%async_computation.1 | async-start | bytes 8388608 | tf_op jit(solution)/shard_map/all_to_all | solution.py:544
  56.1 20.3 %collective-permute-start.4 = (bf16[512,768]{1,0:T(8,128)(2,1)}, bf16[512,768]{1,0:T(8,128)(2,1)S(1)}, u32[]{:S(2)}, u32[]{:S(2)}) collective-permute-start(bf16[512,768]{1,0:T(8,128)(2,1)} %get-tuple-element.136), channel_id=1, source_target_pairs={{0,2},{2,4},{4,6},{6,0},{8,25},{10,27},{12,29},{14,31},{16,18},{18... | collective-permute-start | bytes 2359304 | tf_op jit(solution)/shard_map/ppermute | solution.py:41
  56.6 19.9 %collective-permute-start.5 = (bf16[512,768]{1,0:T(8,128)(2,1)}, bf16[512,768]{1,0:T(8,128)(2,1)}, u32[]{:S(2)}, u32[]{:S(2)}) collective-permute-start(bf16[512,768]{1,0:T(8,128)(2,1)} %get-tuple-element.135), channel_id=1, source_target_pairs={{0,6},{2,0},{4,2},{6,4},{8,25},{10,27},{12,29},{14,31},{16,22},{18... | collective-permute-start | bytes 2359304 | tf_op jit(solution)/shard_map/ppermute | solution.py:41
  66.8 9.7 %copy-start.14 = (bf16[512,768]{1,0:T(8,128)(2,1)S(1)}, bf16[512,768]{1,0:T(8,128)(2,1)}, u32[]{:S(2)}) copy-start(bf16[512,768]{1,0:T(8,128)(2,1)} %copy-done.13) | copy-start | bytes 2359300
  76.6 13.6 %collective-permute-start.8 = (bf16[512,768]{1,0:T(8,128)(2,1)S(1)}, bf16[512,768]{1,0:T(8,128)(2,1)S(1)}, u32[]{:S(2)}, u32[]{:S(2)}) collective-permute-start(bf16[512,768]{1,0:T(8,128)(2,1)S(1)} %broadcast_select_fusion), channel_id=1, source_target_pairs={{0,4},{2,6},{4,0},{6,2},{8,25},{10,27},{12,29},{14,31},{16,20},{18... | collective-permute-start | bytes 2359304 | tf_op jit(solution)/shard_map/ppermute | solution.py:41
  90.2 4.2 %copy-start.28 = (s32[3,1,256]{2,1,0:T(1,128)S(1)}, s32[3,1,256]{2,1,0:T(1,128)}, u32[]{:S(2)}) copy-start(s32[3,1,256]{2,1,0:T(1,128)} %param.16) | copy-start | bytes 9220
  90.2 4.2 %copy-start.29 = (s32[3,1,128]{2,1,0:T(1,128)S(1)}, s32[3,1,128]{2,1,0:T(1,128)}, u32[]{:S(2)}) copy-start(s32[3,1,128]{2,1,0:T(1,128)} %param.14) | copy-start | bytes 4612
  90.2 5.6 %collective-permute-start.9 = (f32[384,768]{1,0:T(8,128)}, f32[384,768]{1,0:T(8,128)S(1)}, u32[]{:S(2)}, u32[]{:S(2)}) collective-permute-start(f32[384,768]{1,0:T(8,128)} %get-tuple-element.84), channel_id=1, source_target_pairs={{0,8},{2,10},{4,12},{6,14},{8,0},{10,2},{12,4},{14,6},{16,24},{18,... | collective-permute-start | bytes 3538952 | tf_op jit(solution)/shard_map/ppermute | solution.py:41
  94.3 3.1 %collective-permute-start.10 = (f32[384,768]{1,0:T(8,128)}, f32[384,768]{1,0:T(8,128)S(1)}, u32[]{:S(2)}, u32[]{:S(2)}) collective-permute-start(f32[384,768]{1,0:T(8,128)} %get-tuple-element.87), channel_id=1, source_target_pairs={{0,8},{2,10},{4,12},{6,14},{8,0},{10,2},{12,4},{14,6},{16,24},{18,... | collective-permute-start | bytes 3538952 | tf_op jit(solution)/shard_map/ppermute | solution.py:41
  98.0 7.8 %copy-start.9 = (bf16[384,512]{1,0:T(8,128)(2,1)}, bf16[384,512]{1,0:T(8,128)(2,1)S(1)}, u32[]{:S(2)}) copy-start(bf16[384,512]{1,0:T(8,128)(2,1)S(1)} %get-tuple-element.88.queries) | copy-start | bytes 1179652
  105.7 20.2 %collective-permute-start.11 = (bf16[4,8,2,64,512]{4,3,2,1,0:T(8,128)(2,1)}, bf16[4,8,2,64,512]{4,3,2,1,0:T(8,128)(2,1)}, u32[]{:S(2)}, u32[]{:S(2)}) collective-permute-start(bf16[4,8,2,64,512]{4,3,2,1,0:T(8,128)(2,1)} %all-to-all-done.1.w.mine), channel_id=1, source_target_pairs={{0,8},{2,10},{4,12},{6,14},{8,0},{10,2},{12,4},{14,6},{16,24},{18,... | collective-permute-start | bytes 12582920 | tf_op jit(solution)/shard_map/ppermute | solution.py:41
  105.7 20.2 %all-to-all-start.2 = ((bf16[16,128,256]{2,1,0:T(8,128)(2,1)}), bf16[16,128,256]{2,1,0:T(8,128)(2,1)S(1)}, u32[]{:S(2)}, u32[]{:S(2)}) async-start(bf16[16,128,256]{2,1,0:T(8,128)(2,1)} %broadcast_in_dim.99), calls=%async_computation.2 | async-start | bytes 2097152 | tf_op jit(solution)/shard_map/all_to_all | solution.py:578
  109.4 10.1 %copy-start.16 = (f32[384,64]{1,0:T(8,128)S(1)}, f32[384,64]{1,0:T(8,128)}, u32[]{:S(2)}) copy-start(f32[384,64]{1,0:T(8,128)} %copy-done.15) | copy-start | bytes 294916
  109.4 10.1 %copy-start.18 = (f32[384,64]{1,0:T(8,128)S(1)}, f32[384,64]{1,0:T(8,128)}, u32[]{:S(2)}) copy-start(f32[384,64]{1,0:T(8,128)} %copy-done.17) | copy-start | bytes 294916
  109.4 10.1 %copy-start.21 = (f32[384,64]{1,0:T(8,128)S(1)}, f32[384,64]{1,0:T(8,128)}, u32[]{:S(2)}) copy-start(f32[384,64]{1,0:T(8,128)} %copy-done.20) | copy-start | bytes 294916
  109.4 10.2 %copy-start.26 = (s32[1,256]{1,0:T(1,128)S(1)}, s32[1,256]{1,0:T(1,128)}, u32[]{:S(2)}) copy-start(s32[1,256]{1,0:T(1,128)} %param.17) | copy-start | bytes 3076
  119.0 2.4 collective-permute-start.12
  120.3 5.7 %copy-start.11 = (bf16[384,512]{1,0:T(8,128)(2,1)S(1)}, bf16[384,512]{1,0:T(8,128)(2,1)}, u32[]{:S(2)}) copy-start(bf16[384,512]{1,0:T(8,128)(2,1)} %copy-done.9) | copy-start | bytes 1179652
  124.8 14.5 %collective-permute-start.15 = (bf16[2,256,512]{2,1,0:T(8,128)(2,1)S(1)}, bf16[2,256,512]{2,1,0:T(8,128)(2,1)S(1)}, u32[]{:S(2)}, u32[]{:S(2)}) collective-permute-start(bf16[2,256,512]{2,1,0:T(8,128)(2,1)S(1)} %get-tuple-element.99.short_att.refs_1_), channel_id=1, source_target_pairs={{0,8},{2,10},{4,12},{6,14},{8,0},{10,2},{12,4},{14,6},{16,24},{18,... | collective-permute-start | bytes 1572872 | tf_op jit(solution)/shard_map/ppermute | solution.py:41
  134.2 5.0 %collective-permute-start.14 = (bf16[2,128,512]{2,1,0:T(8,128)(2,1)S(1)}, bf16[2,128,512]{2,1,0:T(8,128)(2,1)S(1)}, u32[]{:S(2)}, u32[]{:S(2)}) collective-permute-start(bf16[2,128,512]{2,1,0:T(8,128)(2,1)S(1)} %get-tuple-element.100.video_att.refs_0_), channel_id=1, source_target_pairs={{0,8},{2,10},{4,12},{6,14},{8,0},{10,2},{12,4},{14,6},{16,24},{18,... | collective-permute-start | bytes 786440 | tf_op jit(solution)/shard_map/ppermute | solution.py:41
  134.2 28.4 %all-to-all-start.3 = ((bf16[16,128,256]{2,1,0:T(8,128)(2,1)}), bf16[16,128,256]{2,1,0:T(8,128)(2,1)S(1)}, u32[]{:S(2)}, u32[]{:S(2)}) async-start(bf16[16,128,256]{2,1,0:T(8,128)(2,1)} %bitcast.127), calls=%async_computation.3 | async-start | bytes 2097152 | tf_op jit(solution)/shard_map/all_to_all | solution.py:597
  144.7 45.4 %collective-permute-start.16 = (bf16[2,1024,512]{2,1,0:T(8,128)(2,1)}, bf16[2,1024,512]{2,1,0:T(8,128)(2,1)}, u32[]{:S(2)}, u32[]{:S(2)}) collective-permute-start(bf16[2,1024,512]{2,1,0:T(8,128)(2,1)} %term.5), channel_id=1, source_target_pairs={{0,64},{2,66},{4,68},{6,70},{8,12},{10,14},{12,8},{14,10},{16,80},... | collective-permute-start | bytes 6291464 | tf_op jit(solution)/shard_map/ppermute | solution.py:41
  153.5 46.6 %collective-permute-start.17 = (bf16[2,1024,512]{2,1,0:T(8,128)(2,1)}, bf16[2,1024,512]{2,1,0:T(8,128)(2,1)}, u32[]{:S(2)}, u32[]{:S(2)}) collective-permute-start(bf16[2,1024,512]{2,1,0:T(8,128)(2,1)} %term.6), channel_id=1, source_target_pairs={{0,32},{2,34},{4,36},{6,38},{8,10},{10,12},{12,14},{14,8},{16,48},... | collective-permute-start | bytes 6291464 | tf_op jit(solution)/shard_map/ppermute | solution.py:41
  154.1 8.1 %copy-start.19 = (f32[384,64]{1,0:T(8,128)S(1)}, f32[384,64]{1,0:T(8,128)}, u32[]{:S(2)}) copy-start(f32[384,64]{1,0:T(8,128)} %copy-done.17) | copy-start | bytes 294916
  154.1 8.1 %copy-start.22 = (f32[384,64]{1,0:T(8,128)S(1)}, f32[384,64]{1,0:T(8,128)}, u32[]{:S(2)}) copy-start(f32[384,64]{1,0:T(8,128)} %copy-done.20) | copy-start | bytes 294916
  159.5 40.6 %collective-permute-start.18 = (bf16[2,1024,512]{2,1,0:T(8,128)(2,1)}, bf16[2,1024,512]{2,1,0:T(8,128)(2,1)}, u32[]{:S(2)}, u32[]{:S(2)}) collective-permute-start(bf16[2,1024,512]{2,1,0:T(8,128)(2,1)} %term.7), channel_id=1, source_target_pairs={{0,96},{2,98},{4,100},{6,102},{8,14},{10,8},{12,10},{14,12},{16,11... | collective-permute-start | bytes 6291464 | tf_op jit(solution)/shard_map/ppermute | solution.py:41
  162.8 1.7 collective-permute-start.13
  170.5 42.4 %all-to-all-start.4 = ((bf16[4,1040,256]{2,1,0:T(8,128)(2,1)}), bf16[4,1040,256]{2,1,0:T(8,128)(2,1)}, u32[]{:S(2)}, u32[]{:S(2)}) async-start(bf16[4,1040,256]{2,1,0:T(8,128)(2,1)} %key_term.1), calls=%async_computation.4 | async-start | bytes 4259840 | tf_op jit(solution)/shard_map/all_to_all | solution.py:611
  180.5 19.7 %copy-start.12 = (bf16[2,1024,512]{2,1,0:T(8,128)(2,1)S(1)}, bf16[2,1024,512]{2,1,0:T(8,128)(2,1)}, u32[]{:S(2)}) copy-start(bf16[2,1024,512]{2,1,0:T(8,128)(2,1)} %term.4) | copy-start | bytes 6291460
  202.6 14.0 %collective-permute-start.19 = (bf16[2,256,512]{2,1,0:T(8,128)(2,1)}, bf16[2,256,512]{2,1,0:T(8,128)(2,1)S(1)}, u32[]{:S(2)}, u32[]{:S(2)}) collective-permute-start(bf16[2,256,512]{2,1,0:T(8,128)(2,1)} %fusion), channel_id=1, source_target_pairs={{0,4},{2,6},{4,0},{6,2},{8,72},{10,74},{12,76},{14,78},{16,20},{18... | collective-permute-start | bytes 1572872 | tf_op jit(solution)/shard_map/ppermute | solution.py:41
  205.6 13.5 %collective-permute-start.20 = (bf16[2,256,512]{2,1,0:T(8,128)(2,1)}, bf16[2,256,512]{2,1,0:T(8,128)(2,1)S(1)}, u32[]{:S(2)}, u32[]{:S(2)}) collective-permute-start(bf16[2,256,512]{2,1,0:T(8,128)(2,1)} %fusion.1), channel_id=1, source_target_pairs={{0,2},{2,4},{4,6},{6,0},{8,40},{10,42},{12,44},{14,46},{16,18},{18... | collective-permute-start | bytes 1572872 | tf_op jit(solution)/shard_map/ppermute | solution.py:41
  209.5 9.6 %collective-permute-start.21 = (bf16[2,256,512]{2,1,0:T(8,128)(2,1)}, bf16[2,256,512]{2,1,0:T(8,128)(2,1)S(1)}, u32[]{:S(2)}, u32[]{:S(2)}) collective-permute-start(bf16[2,256,512]{2,1,0:T(8,128)(2,1)} %fusion.2), channel_id=1, source_target_pairs={{0,6},{2,0},{4,2},{6,4},{8,104},{10,106},{12,108},{14,110},{16,22}... | collective-permute-start | bytes 1572872 | tf_op jit(solution)/shard_map/ppermute | solution.py:41
  219.1 5.5 %copy-start.25 = (bf16[2,256,512]{2,1,0:T(8,128)(2,1)}, bf16[2,256,512]{2,1,0:T(8,128)(2,1)S(1)}, u32[]{:S(2)}) copy-start(bf16[2,256,512]{2,1,0:T(8,128)(2,1)S(1)} %collective-permute-done.21) | copy-start | bytes 1572868
  220.3 14.0 %collective-permute-start.24 = (bf16[2,64,512]{2,1,0:T(8,128)(2,1)}, bf16[2,64,512]{2,1,0:T(8,128)(2,1)S(1)}, u32[]{:S(2)}, u32[]{:S(2)}) collective-permute-start(bf16[2,64,512]{2,1,0:T(8,128)(2,1)} %get-tuple-element.133), channel_id=1, source_target_pairs={{0,17},{2,19},{4,21},{6,23},{8,25},{10,27},{12,29},{14,31},{16,0},... | collective-permute-start | bytes 393224 | tf_op jit(solution)/shard_map/ppermute | solution.py:41
  222.6 11.7 %collective-permute-start.23 = (bf16[2,64,512]{2,1,0:T(8,128)(2,1)}, bf16[2,64,512]{2,1,0:T(8,128)(2,1)S(1)}, u32[]{:S(2)}, u32[]{:S(2)}) collective-permute-start(bf16[2,64,512]{2,1,0:T(8,128)(2,1)} %get-tuple-element.134), channel_id=1, source_target_pairs={{0,16},{2,18},{4,20},{6,22},{8,24},{10,26},{12,28},{14,30},{16,1},... | collective-permute-start | bytes 393224 | tf_op jit(solution)/shard_map/ppermute | solution.py:41
  222.6 24.1 %copy-start.1 = (bf16[1024,768]{1,0:T(8,128)(2,1)S(1)}, bf16[1024,768]{1,0:T(8,128)(2,1)}, u32[]{:S(2)}) copy-start(bf16[1024,768]{1,0:T(8,128)(2,1)} %param.10) | copy-start | bytes 4718596
  222.6 11.7 %collective-permute-start.22 = (bf16[2,64,512]{2,1,0:T(8,128)(2,1)}, bf16[2,64,512]{2,1,0:T(8,128)(2,1)}, u32[]{:S(2)}, u32[]{:S(2)}) collective-permute-start(bf16[2,64,512]{2,1,0:T(8,128)(2,1)} %get-tuple-element.132), channel_id=1, source_target_pairs={{0,1},{2,3},{4,5},{6,7},{8,9},{10,11},{12,13},{14,15},{16,17},{18,... | collective-permute-start | bytes 393224 | tf_op jit(solution)/shard_map/ppermute | solution.py:41
  224.6 20.7 %all-to-all-start.5 = ((bf16[16,80,256]{2,1,0:T(8,128)(2,1)}), bf16[16,80,256]{2,1,0:T(8,128)(2,1)S(1)}, u32[]{:S(2)}, u32[]{:S(2)}) async-start(bf16[16,80,256]{2,1,0:T(8,128)(2,1)} %pad_maximum_fusion), calls=%async_computation.5 | async-start | bytes 1310720 | tf_op jit(solution)/shard_map/all_to_all | solution.py:494
  (13 other events, 24.8 us)

commit v4 on v3

--- a/solution.py
+++ b/solution.py
@@ -436,12 +436,12 @@
         chunk = rows(far).astype(BF)
         *first, chunk = lax.optimization_barrier((*first, chunk))
         got.append(to_second(chunk, far))
-    *got, parts = lax.optimization_barrier((*got, parts))
+    *got, _ = lax.optimization_barrier((*got, parts))
     piece = lambda far: sum(
         (g[:, far * 64 : (far + 1) * 64].astype(F32) for g in got), rows(0)[:, far * 64 : (far + 1) * 64]
     )
     late = [to_y(piece(far).astype(BF), far) for far in (2, 1, 3)]
-    return sum((g.astype(F32) for g in late), piece(0)), parts
+    return late, piece(0)
 
 
 def tail_of(row):
@@ -610,10 +610,11 @@
     terms, video_y, short_y = lax.optimization_barrier(
         (lax.all_to_all(terms, ("yl", "yh"), 0, 0, tiled=True), video_y, short_y)
     )
-    (grad_out, grad_q), parts = scatter(
-        (place, second_place), c_turned, x_turned, results, key_parts(terms)
-    )
+    parts = key_parts(terms)
+    late, own = scatter((place, second_place), c_turned, x_turned, results, parts)
     grad_kv, bias = key_sum(parts)
+    grad_kv, bias, own, *late = lax.optimization_barrier((grad_kv, bias, own, *late))
+    grad_out, grad_q = sum((g.astype(F32) for g in late), own)
     return (
         video_y[None],
         short_y[None],

time: 249 us -> 242 us (0.972)
  waiting for transfers between devices: 45.2 us -> 38 us
    all_to_all x1, waiting for transfers between devices: 9.13 us -> 3.34 us  [key_sum(): lax.all_to_all(parts, AXES, 0, 0, tiled=True, axis_index_groups=LATE_GROUPS)]
  transfers between devices with their start and end apart: 31 -> 31, of which waited for: 14 -> 14; matrix products, arithmetic and copies ran while one was open for 10% -> 10% of each run, Pallas kernels for 39% -> 40%
where the time goes in v4:
time: 242 us; the launch traced here: 239 us
  Pallas kernels  101 us (42%)
  starting transfers between devices  68 us (28%)
  waiting for transfers between devices  38 us (16%)
  other arithmetic  18.6 us (8%)
  local copies, waits for them, and re-layouts  12.5 us (5%)
    ppermute x25, starting transfers between devices, move(): return lax.ppermute(value, AXES, pairs(target))  33.6 us
    ppermute x25, waiting for transfers between devices, move(): return lax.ppermute(value, AXES, pairs(target))  25.2 us
    pallas_call x4, Pallas kernels, term(): call(term_kernel, 'term', (4,), [((512, wide), lambda i, s: (2 * s[0] + j...  21.6 us
    pallas_call x2, Pallas kernels, turned(): call(turn_kernel, 'turned', (8,), [own(nv), own(ns), ((rows, 512), lambda...  18.8 us
    pallas_call x3, Pallas kernels, project(): call(functools.partial(project_kernel, parts=parts, added=len(before) > 0...  17.9 us
    pallas_call x1, Pallas kernels, layer_out(): call(layer_out_kernel, 'layer_out', (8,), [att(nv), att(ns), W_BLOCK, W_B...  9.55 us
    pallas_call x1, Pallas kernels, grad_attended_parts(): call(grad_attended_kernel, 'grad_attended', (8,), [own(nv), own(ns), ((ro...  9.52 us
    all_to_all x1, starting transfers between devices, key_sum(): lax.all_to_all(parts, AXES, 0, 0, tiled=True, axis_index_groups=LATE_GROUPS)  8.92 us
  transfers between devices with their start and end apart: 31, of which 14 were waited for; matrix products, arithmetic and copies ran while one was open for 10% of the time, Pallas kernels for 40%

profile of v4, /device:TPU:0, one launch (start us, length us, event | category | flops | bytes accessed | tf_op | source)
XLA Modules:
  0.0 239.1 jit_solution(1459396612800351651)
XLA Ops:
  0.7 4.4 %halves.2 = bf16[384,4096]{1,0:T(8,128)(2,1)} custom-call(s32[1]{0:T(128)S(6)} %sub.8.core_ref, bf16[128,8192]{1,0:T(8,128)(2,1)} %bitcast.136, bf16[128,8192]{1,0:T(8,128)(2,1)} %bitcast.137, bf16[256,8192]{1,0:T(8,128)(2,1)} %bitcast.130, bf16[256,8192]{1,0:T(8,128)(2,1)} %bitcast.131), custom_call_target="tpu_custom_call" | custom-call | bytes 6291456 | tf_op jit(solution)/shard_map/halves/pallas_call | solution.py:119
  6.9 7.0 %all-to-all-start = ((bf16[8,2,64,512]{3,2,1,0:T(8,128)(2,1)}), bf16[8,2,64,512]{3,2,1,0:T(8,128)(2,1)}, u32[]{:S(2)}, u32[]{:S(2)}) async-start(bf16[8,2,64,512]{3,2,1,0:T(8,128)(2,1)} %broadcast_in_dim.88), calls=%async_computation | async-start | bytes 2097152 | tf_op jit(solution)/shard_map/all_to_all | solution.py:520
  14.0 2.1 collective-permute-start
  17.3 3.3 %collective-permute-start.2 = (bf16[512,768]{1,0:T(8,128)(2,1)S(1)}, bf16[512,768]{1,0:T(8,128)(2,1)S(1)}, u32[]{:S(2)}, u32[]{:S(2)}) collective-permute-start(bf16[512,768]{1,0:T(8,128)(2,1)S(1)} %constant_dynamic-slice_fusion.refs_3_), channel_id=1, source_target_pairs={{0,17},{2,19},{4,21},{6,23},{8,25},{10,27},{12,29},{14,31},{16,1},... | collective-permute-start | bytes 2359304 | tf_op jit(solution)/shard_map/ppermute | solution.py:41
  20.7 9.4 %turned.2.tokens = bf16[4096,768]{1,0:T(8,128)(2,1)} custom-call(s32[65]{0:T(128)S(1)} %stack.331.tab, bf16[128,8192]{1,0:T(8,128)(2,1)} %bitcast.138, bf16[256,8192]{1,0:T(8,128)(2,1)} %bitcast.132, bf16[384,4096]{1,0:T(8,128)(2,1)} %collective-permute-done.3.other.refs_2_), custom_call_target="tpu_custom_call" | custom-call | bytes 12582912 | tf_op jit(solution)/shard_map/turned/pallas_call | solution.py:141
  30.2 2.0 all-to-all-done
  32.2 3.8 %broadcast_in_dim.89 = bf16[4,8,2,64,512]{4,3,2,1,0:T(8,128)(2,1)} broadcast(bf16[8,2,64,512]{3,2,1,0:T(8,128)(2,1)} %all-to-all-done), dimensions={1,2,3,4} | broadcast | bytes 5242880 | tf_op jit(solution)/shard_map/broadcast_in_dim | solution.py:542
  36.0 4.3 %halves.3 = bf16[384,4096]{1,0:T(8,128)(2,1)} custom-call(s32[1]{0:T(128)S(6)} %sub.8.core_ref, bf16[128,8192]{1,0:T(8,128)(2,1)} %bitcast.146, bf16[128,8192]{1,0:T(8,128)(2,1)} %bitcast.147, bf16[256,8192]{1,0:T(8,128)(2,1)} %bitcast.142, bf16[256,8192]{1,0:T(8,128)(2,1)} %bitcast.143), custom_call_target="tpu_custom_call" | custom-call | bytes 6291456 | tf_op jit(solution)/shard_map/halves/pallas_call | solution.py:119
  40.3 5.9 %collective-permute-done.refs_4_ = bf16[512,768]{1,0:T(8,128)(2,1)S(1)} collective-permute-done((bf16[512,768]{1,0:T(8,128)(2,1)S(1)}, bf16[512,768]{1,0:T(8,128)(2,1)S(1)}, u32[]{:S(2)}, u32[]{:S(2)}) %collective-permute-start) | collective-permute-done | bytes 786464 | tf_op jit(solution)/shard_map/ppermute | solution.py:41
  46.5 3.0 %collective-permute-start.6 = (bf16[512,768]{1,0:T(8,128)(2,1)S(1)}, bf16[512,768]{1,0:T(8,128)(2,1)S(1)}, u32[]{:S(2)}, u32[]{:S(2)}) collective-permute-start(bf16[512,768]{1,0:T(8,128)(2,1)S(1)} %constant_dynamic-slice_fusion.refs_3_), channel_id=1, source_target_pairs={{0,4},{2,6},{4,0},{6,2},{8,12},{10,14},{12,8},{14,10},{16,20},{18,... | collective-permute-start | bytes 2359304 | tf_op jit(solution)/shard_map/ppermute | solution.py:41
  49.5 5.3 %all-to-all-start.1 = ((bf16[4,8,2,64,512]{4,3,2,1,0:T(8,128)(2,1)}), bf16[4,8,2,64,512]{4,3,2,1,0:T(8,128)(2,1)}, u32[]{:S(2)}, u32[]{:S(2)}) async-start(bf16[4,8,2,64,512]{4,3,2,1,0:T(8,128)(2,1)} %broadcast_in_dim.89), calls=%async_computation.1 | async-start | bytes 8388608 | tf_op jit(solution)/shard_map/all_to_all | solution.py:544
  56.6 2.7 %collective-permute-start.5 = (bf16[512,768]{1,0:T(8,128)(2,1)}, bf16[512,768]{1,0:T(8,128)(2,1)}, u32[]{:S(2)}, u32[]{:S(2)}) collective-permute-start(bf16[512,768]{1,0:T(8,128)(2,1)} %get-tuple-element.146), channel_id=1, source_target_pairs={{0,6},{2,0},{4,2},{6,4},{8,25},{10,27},{12,29},{14,31},{16,22},{18... | collective-permute-start | bytes 2359304 | tf_op jit(solution)/shard_map/ppermute | solution.py:41
  59.4 7.4 %project.3 = (f32[384,768]{1,0:T(8,128)}, f32[384,768]{1,0:T(8,128)}) custom-call(s32[5]{0:T(128)S(1)} %stack.337.tab, bf16[128,8192]{1,0:T(8,128)(2,1)} %bitcast.139, bf16[256,8192]{1,0:T(8,128)(2,1)} %bitcast.133, bf16[384,4096]{1,0:T(8,128)(2,1)} %collective-permute-done.3.other.refs_2_, bf16[512,768]{1,0:T(8,128)(2,1)S(1)} %constant_dynamic-slice_fusion.refs_3_, ...), custom_call_target="tpu_custom_call" | custom-call | flops 2415919104 | bytes 8650752 | tf_op jit(solution)/shard_map/project/pallas_call | solution.py:194
  66.8 9.4 %turned.3.cot = bf16[4096,768]{1,0:T(8,128)(2,1)} custom-call(s32[65]{0:T(128)S(1)} %stack.331.tab, bf16[128,8192]{1,0:T(8,128)(2,1)} %bitcast.148, bf16[256,8192]{1,0:T(8,128)(2,1)} %bitcast.144, bf16[384,4096]{1,0:T(8,128)(2,1)} %collective-permute-done.7.other), custom_call_target="tpu_custom_call" | custom-call | bytes 12582912 | tf_op jit(solution)/shard_map/turned/pallas_call | solution.py:141
  76.6 2.9 %collective-permute-start.8 = (bf16[512,768]{1,0:T(8,128)(2,1)S(1)}, bf16[512,768]{1,0:T(8,128)(2,1)S(1)}, u32[]{:S(2)}, u32[]{:S(2)}) collective-permute-start(bf16[512,768]{1,0:T(8,128)(2,1)S(1)} %broadcast_select_fusion), channel_id=1, source_target_pairs={{0,4},{2,6},{4,0},{6,2},{8,25},{10,27},{12,29},{14,31},{16,20},{18... | collective-permute-start | bytes 2359304 | tf_op jit(solution)/shard_map/ppermute | solution.py:41
  79.7 7.0 %project.4 = (f32[384,768]{1,0:T(8,128)}, f32[384,768]{1,0:T(8,128)}) custom-call(s32[4]{0:T(128)S(1)} %pad_add_fusion.3.tab, bf16[128,8192]{1,0:T(8,128)(2,1)} %bitcast.140, bf16[256,8192]{1,0:T(8,128)(2,1)} %bitcast.134, bf16[384,4096]{1,0:T(8,128)(2,1)} %collective-permute-done.3.other.refs_2_, bf16[512,768]{1,0:T(8,128)(2,1)S(1)} %collective-permute-done.6.refs_3_, ...), custom_call_target="tpu_custom_call" | custom-call | flops 1811939328 | bytes 7077888 | tf_op jit(solution)/shard_map/project/pallas_call | solution.py:194
  86.6 3.6 %collective-permute-done.8.refs_3_ = bf16[512,768]{1,0:T(8,128)(2,1)S(1)} collective-permute-done((bf16[512,768]{1,0:T(8,128)(2,1)S(1)}, bf16[512,768]{1,0:T(8,128)(2,1)S(1)}, u32[]{:S(2)}, u32[]{:S(2)}) %collective-permute-start.8) | collective-permute-done | bytes 786464 | tf_op jit(solution)/shard_map/ppermute | solution.py:41
  90.9 3.5 %project.5 = (f32[384,768]{1,0:T(8,128)S(1)}, f32[384,768]{1,0:T(8,128)}) custom-call(s32[2]{0:T(128)S(1)} %pad_add_fusion.4.tab, bf16[128,8192]{1,0:T(8,128)(2,1)} %bitcast.141, bf16[256,8192]{1,0:T(8,128)(2,1)} %bitcast.135, bf16[384,4096]{1,0:T(8,128)(2,1)} %collective-permute-done.3.other.refs_2_, bf16[512,768]{1,0:T(8,128)(2,1)S(1)} %collective-permute-done.8.refs_3_), custom_call_target="tpu_custom_call" | custom-call | flops 603979776 | bytes 3932160 | tf_op jit(solution)/shard_map/project/pallas_call | solution.py:194
  95.8 1.6 collective-permute-done.10.far_got
  98.0 6.7 %all-to-all-done.1.w.mine = bf16[4,8,2,64,512]{4,3,2,1,0:T(8,128)(2,1)} async-done(((bf16[4,8,2,64,512]{4,3,2,1,0:T(8,128)(2,1)}), bf16[4,8,2,64,512]{4,3,2,1,0:T(8,128)(2,1)}, u32[]{:S(2)}, u32[]{:S(2)}) %all-to-all-start.1) | async-done | bytes 4194336 | tf_op jit(solution)/shard_map/all_to_all | solution.py:544
  105.7 3.7 %all-to-all-start.2 = ((bf16[16,128,256]{2,1,0:T(8,128)(2,1)}), bf16[16,128,256]{2,1,0:T(8,128)(2,1)S(1)}, u32[]{:S(2)}, u32[]{:S(2)}) async-start(bf16[16,128,256]{2,1,0:T(8,128)(2,1)} %broadcast_in_dim.99), calls=%async_computation.2 | async-start | bytes 2097152 | tf_op jit(solution)/shard_map/all_to_all | solution.py:578
  109.5 9.5 %grad_attended.1 = (f32[384,512]{1,0:T(8,128)S(1)}, f32[384,512]{1,0:T(8,128)S(1)}) custom-call(s32[1]{0:T(128)} %bitcast.1.core_ref.tab, bf16[128,8192]{1,0:T(8,128)(2,1)} %bitcast.149, bf16[256,8192]{1,0:T(8,128)(2,1)} %bitcast.145, bf16[384,4096]{1,0:T(8,128)(2,1)} %collective-permute-done.7.other, bf16[4,8,2,64,512]{4,3,2,1,0:T(8,128)(2,1)} %all-to-all-done.1.w.mine), custom_call_target="tpu_custom_call" | custom-call | flops 3221225472 | bytes 10485760 | tf_op jit(solution)/shard_map/grad_attended/pallas_call | solution.py:346
  122.3 2.5 %short_attention.1 = (bf16[2,256,512]{2,1,0:T(8,128)(2,1)S(1)}, bf16[256,256]{1,0:T(8,128)(2,1)S(1)}) custom-call(s32[1]{0:T(128)} %constant.347.clone.1.tab, bf16[256,512]{1,0:T(8,128)(2,1)S(1)} %slice.158.queries, bf16[256,256]{1,0:T(8,128)(2,1)S(1)} %slice.159.keys_values, s32[2,256,256]{2,1,0:T(8,128)S(1)} %pad_add_fusion.segments, ...), custom_call_target="tpu_custom_call" | custom-call | flops 335544320 | bytes 262144 | tf_op jit(solution)/shard_map/short_attention/pallas_call | solution.py:292
  128.3 5.0 %video_attention.1 = (bf16[2,128,512]{2,1,0:T(8,128)(2,1)S(1)}, bf16[2048,256]{1,0:T(8,128)(2,1)S(1)}) custom-call(s32[1]{0:T(128)} %bitcast.72.tab, bf16[384,512]{1,0:T(8,128)(2,1)S(1)} %copy-done.11, bf16[2048,256]{1,0:T(8,128)(2,1)S(1)} %bitcast.128, s32[1,8,128]{2,1,0:T(8,128)S(1)} %broadcast_in_dim.100.segments, f32[384,512]{1,0:T(8,128)S(1)} %copy-done.6, ...), custom_call_target="tpu_custom_call" | custom-call | flops 1342177280 | bytes 2097152 | tf_op jit(solution)/shard_map/video_attention/pallas_call | solution.py:292
  134.2 5.0 %all-to-all-start.3 = ((bf16[16,128,256]{2,1,0:T(8,128)(2,1)}), bf16[16,128,256]{2,1,0:T(8,128)(2,1)S(1)}, u32[]{:S(2)}, u32[]{:S(2)}) async-start(bf16[16,128,256]{2,1,0:T(8,128)(2,1)} %bitcast.127), calls=%async_computation.3 | async-start | bytes 2097152 | tf_op jit(solution)/shard_map/all_to_all | solution.py:597
  139.6 5.4 %term.5 = bf16[2,1024,512]{2,1,0:T(8,128)(2,1)} custom-call(s32[1]{0:T(128)} %bitcast.91.tab, bf16[4096,768]{1,0:T(8,128)(2,1)} %turned.3.cot, bf16[4096,768]{1,0:T(8,128)(2,1)} %turned.2.tokens, bf16[2,128,512]{2,1,0:T(8,128)(2,1)S(1)} %get-tuple-element.105.video_att.refs_0_, bf16[2,256,512]{2,1,0:T(8,128)(2,1)S(1)} %get-tuple-element.104.short_att.refs_1_, ...), custom_call_target="tpu_custom_call" | custom-call | flops 1610612736 | bytes 6815744 | tf_op jit(solution)/shard_map/term/pallas_call | solution.py:410
  145.0 3.4 %collective-permute-start.16 = (bf16[2,1024,512]{2,1,0:T(8,128)(2,1)}, bf16[2,1024,512]{2,1,0:T(8,128)(2,1)}, u32[]{:S(2)}, u32[]{:S(2)}) collective-permute-start(bf16[2,1024,512]{2,1,0:T(8,128)(2,1)} %term.5), channel_id=1, source_target_pairs={{0,64},{2,66},{4,68},{6,70},{8,12},{10,14},{12,8},{14,10},{16,80},... | collective-permute-start | bytes 6291464 | tf_op jit(solution)/shard_map/ppermute | solution.py:41
  148.4 5.4 %term.6 = bf16[2,1024,512]{2,1,0:T(8,128)(2,1)} custom-call(s32[1]{0:T(128)} %bitcast.93.tab, bf16[4096,768]{1,0:T(8,128)(2,1)} %turned.3.cot, bf16[4096,768]{1,0:T(8,128)(2,1)} %turned.2.tokens, bf16[2,128,512]{2,1,0:T(8,128)(2,1)S(1)} %get-tuple-element.105.video_att.refs_0_, bf16[2,256,512]{2,1,0:T(8,128)(2,1)S(1)} %get-tuple-element.104.short_att.refs_1_, ...), custom_call_target="tpu_custom_call" | custom-call | flops 1610612736 | bytes 6815744 | tf_op jit(solution)/shard_map/term/pallas_call | solution.py:410
  154.4 5.4 %term.7 = bf16[2,1024,512]{2,1,0:T(8,128)(2,1)} custom-call(s32[1]{0:T(128)} %bitcast.95.tab, bf16[4096,768]{1,0:T(8,128)(2,1)} %turned.3.cot, bf16[4096,768]{1,0:T(8,128)(2,1)} %turned.2.tokens, bf16[2,128,512]{2,1,0:T(8,128)(2,1)S(1)} %get-tuple-element.105.video_att.refs_0_, bf16[2,256,512]{2,1,0:T(8,128)(2,1)S(1)} %get-tuple-element.104.short_att.refs_1_, ...), custom_call_target="tpu_custom_call" | custom-call | flops 1610612736 | bytes 6815744 | tf_op jit(solution)/shard_map/term/pallas_call | solution.py:410
  159.8 2.7 %collective-permute-start.18 = (bf16[2,1024,512]{2,1,0:T(8,128)(2,1)}, bf16[2,1024,512]{2,1,0:T(8,128)(2,1)}, u32[]{:S(2)}, u32[]{:S(2)}) collective-permute-start(bf16[2,1024,512]{2,1,0:T(8,128)(2,1)} %term.7), channel_id=1, source_target_pairs={{0,96},{2,98},{4,100},{6,102},{8,14},{10,8},{12,10},{14,12},{16,11... | collective-permute-start | bytes 6291464 | tf_op jit(solution)/shard_map/ppermute | solution.py:41
  163.2 1.4 collective-permute-done.13.gb
  164.8 5.8 %key_term.1 = bf16[4,1040,256]{2,1,0:T(8,128)(2,1)} custom-call(s32[1]{0:T(128)} %bitcast.tab, bf16[4,4,4,64,768]{4,3,2,1,0:T(8,128)(2,1)} %bitcast.129, bf16[384,256]{1,0:T(8,128)(2,1)S(1)} %pad_maximum_fusion.1.ga, bf16[384,256]{1,0:T(8,128)(2,1)S(1)} %collective-permute-done.13.gb, bf16[16,256]{1,0:T(8,128)(2,1)S(1)} %maximum_maximum_fusion.tail), custom_call_target="tpu_custom_call" | custom-call | flops 1610612736 | bytes 8388608 | tf_op jit(solution)/shard_map/key_term/pallas_call | solution.py:469
  170.5 4.5 %all-to-all-start.4 = ((bf16[4,1040,256]{2,1,0:T(8,128)(2,1)}), bf16[4,1040,256]{2,1,0:T(8,128)(2,1)}, u32[]{:S(2)}, u32[]{:S(2)}) async-start(bf16[4,1040,256]{2,1,0:T(8,128)(2,1)} %key_term.1), calls=%async_computation.4 | async-start | bytes 4259840 | tf_op jit(solution)/shard_map/all_to_all | solution.py:611
  175.0 5.4 %term.4 = bf16[2,1024,512]{2,1,0:T(8,128)(2,1)} custom-call(s32[1]{0:T(128)} %bitcast.89.tab, bf16[4096,768]{1,0:T(8,128)(2,1)} %turned.3.cot, bf16[4096,768]{1,0:T(8,128)(2,1)} %turned.2.tokens, bf16[2,128,512]{2,1,0:T(8,128)(2,1)S(1)} %get-tuple-element.105.video_att.refs_0_, bf16[2,256,512]{2,1,0:T(8,128)(2,1)S(1)} %get-tuple-element.104.short_att.refs_1_, ...), custom_call_target="tpu_custom_call" | custom-call | flops 1610612736 | bytes 6815744 | tf_op jit(solution)/shard_map/term/pallas_call | solution.py:410
  180.5 9.6 %layer_out.1 = (bf16[128,8192]{1,0:T(8,128)(2,1)}, bf16[256,8192]{1,0:T(8,128)(2,1)}) custom-call(s32[1]{0:T(128)} %bitcast.1.core_ref.tab, bf16[2,128,512]{2,1,0:T(8,128)(2,1)S(1)} %get-tuple-element.105.video_att.refs_0_, bf16[2,256,512]{2,1,0:T(8,128)(2,1)S(1)} %get-tuple-element.104.short_att.refs_1_, bf16[4,8,2,64,512]{4,3,2,1,0:T(8,128)(2,1)} %all-to-all-done.1.w.mine, ...), custom_call_target="tpu_custom_call" | custom-call | flops 3221225472 | bytes 14680064 | tf_op jit(solution)/shard_map/layer_out/pallas_call | solution.py:365
  190.0 10.2 %collective-permute-done.17 = bf16[2,1024,512]{2,1,0:T(8,128)(2,1)} collective-permute-done((bf16[2,1024,512]{2,1,0:T(8,128)(2,1)}, bf16[2,1024,512]{2,1,0:T(8,128)(2,1)}, u32[]{:S(2)}, u32[]{:S(2)}) %collective-permute-start.17) | collective-permute-done | bytes 2097184 | tf_op jit(solution)/shard_map/ppermute | solution.py:41
  200.2 2.4 %fusion = bf16[2,256,512]{2,1,0:T(8,128)(2,1)} fusion(bf16[2,4,256,512]{3,2,1,0:T(8,128)(2,1)} %bitcast.96, s32[]{:T(128)S(6)} %select_n.501, bf16[2,4,256,512]{3,2,1,0:T(8,128)(2,1)} %bitcast.94, bf16[2,4,256,512]{3,2,1,0:T(8,128)(2,1)} %bitcast.92, bf16[2,4,256,512]{3,2,1,0:T(8,128)(2,1)S(1)} %bitcast.151), kind=kLoop, calls=%fused_computation.10 | loop fusion | flops 2097152 | bytes 2621444 | tf_op jit(solution)/shard_map/add | solution.py:432
  202.6 2.4 %fusion.1 = bf16[2,256,512]{2,1,0:T(8,128)(2,1)} fusion(s32[]{:T(128)S(6)} %select_n.503, bf16[2,4,256,512]{3,2,1,0:T(8,128)(2,1)S(1)} %bitcast.152, bf16[2,4,256,512]{3,2,1,0:T(8,128)(2,1)} %bitcast.92, bf16[2,4,256,512]{3,2,1,0:T(8,128)(2,1)} %bitcast.94, bf16[2,4,256,512]{3,2,1,0:T(8,128)(2,1)} %bitcast.96), kind=kLoop, calls=%fused_computation.11 | loop fusion | flops 2097152 | bytes 2621444 | tf_op jit(solution)/shard_map/add | solution.py:432
  205.0 1.6 fusion.2
  207.3 1.5 collective-permute-start.20
  208.8 1.8 collective-permute-start.21
  211.3 1.9 slice_reduce_fusion
  214.2 8.9 %all-to-all-start.5 = ((bf16[16,80,256]{2,1,0:T(8,128)(2,1)}), bf16[16,80,256]{2,1,0:T(8,128)(2,1)S(1)}, u32[]{:S(2)}, u32[]{:S(2)}) async-start(bf16[16,80,256]{2,1,0:T(8,128)(2,1)} %pad_maximum_fusion), calls=%async_computation.5 | async-start | bytes 1310720 | tf_op jit(solution)/shard_map/all_to_all | solution.py:494
  223.2 1.8 add_bitcast_fusion
  225.0 2.2 fusion.5
  227.3 2.2 collective-permute-start.22
  230.0 2.7 %collective-permute-start.24 = (bf16[2,64,512]{2,1,0:T(8,128)(2,1)}, bf16[2,64,512]{2,1,0:T(8,128)(2,1)S(1)}, u32[]{:S(2)}, u32[]{:S(2)}) collective-permute-start(bf16[2,64,512]{2,1,0:T(8,128)(2,1)} %get-tuple-element.142), channel_id=1, source_target_pairs={{0,17},{2,19},{4,21},{6,23},{8,25},{10,27},{12,29},{14,31},{16,0},... | collective-permute-start | bytes 393224 | tf_op jit(solution)/shard_map/ppermute | solution.py:41
  232.7 3.3 %all-to-all-done.5 = bf16[16,80,256]{2,1,0:T(8,128)(2,1)S(1)} async-done(((bf16[16,80,256]{2,1,0:T(8,128)(2,1)}), bf16[16,80,256]{2,1,0:T(8,128)(2,1)S(1)}, u32[]{:S(2)}, u32[]{:S(2)}) %all-to-all-start.5) | async-done | bytes 655392 | tf_op jit(solution)/shard_map/all_to_all | solution.py:494
  (148 shorter events, 25.1 us)
Async XLA Ops:
  0.6 13.3 %copy-start = (bf16[1024,768]{1,0:T(8,128)(2,1)S(1)}, bf16[1024,768]{1,0:T(8,128)(2,1)}, u32[]{:S(2)}) copy-start(bf16[1024,768]{1,0:T(8,128)(2,1)} %param.10) | copy-start | bytes 4718596
  0.7 4.5 %copy-start.3 = (bf16[64,8192]{1,0:T(8,128)(2,1)S(1)}, bf16[64,8192]{1,0:T(8,128)(2,1)}, u32[]{:S(2)}) copy-start(bf16[64,8192]{1,0:T(8,128)(2,1)} %block.1) | copy-start | bytes 3145732
  5.1 15.7 %collective-permute-start.3 = (bf16[384,4096]{1,0:T(8,128)(2,1)}, bf16[384,4096]{1,0:T(8,128)(2,1)}, u32[]{:S(2)}, u32[]{:S(2)}) collective-permute-start(bf16[384,4096]{1,0:T(8,128)(2,1)} %halves.2), channel_id=1, source_target_pairs={{0,8},{2,10},{4,12},{6,14},{8,0},{10,2},{12,4},{14,6},{16,24},{18,... | collective-permute-start | bytes 9437192 | tf_op jit(solution)/shard_map/ppermute | solution.py:41
  6.9 25.3 %all-to-all-start = ((bf16[8,2,64,512]{3,2,1,0:T(8,128)(2,1)}), bf16[8,2,64,512]{3,2,1,0:T(8,128)(2,1)}, u32[]{:S(2)}, u32[]{:S(2)}) async-start(bf16[8,2,64,512]{3,2,1,0:T(8,128)(2,1)} %broadcast_in_dim.88), calls=%async_computation | async-start | bytes 2097152 | tf_op jit(solution)/shard_map/all_to_all | solution.py:520
  14.0 32.3 %collective-permute-start = (bf16[512,768]{1,0:T(8,128)(2,1)S(1)}, bf16[512,768]{1,0:T(8,128)(2,1)S(1)}, u32[]{:S(2)}, u32[]{:S(2)}) collective-permute-start(bf16[512,768]{1,0:T(8,128)(2,1)S(1)} %constant_dynamic-slice_fusion.refs_3_), channel_id=1, source_target_pairs={{0,2},{2,4},{4,6},{6,0},{8,10},{10,12},{12,14},{14,8},{16,18},{18,... | collective-permute-start | bytes 2359304 | tf_op jit(solution)/shard_map/ppermute | solution.py:41
  16.0 30.2 %collective-permute-start.1 = (bf16[512,768]{1,0:T(8,128)(2,1)S(1)}, bf16[512,768]{1,0:T(8,128)(2,1)}, u32[]{:S(2)}, u32[]{:S(2)}) collective-permute-start(bf16[512,768]{1,0:T(8,128)(2,1)S(1)} %constant_dynamic-slice_fusion.refs_3_), channel_id=1, source_target_pairs={{0,6},{2,0},{4,2},{6,4},{8,14},{10,8},{12,10},{14,12},{16,22},{18,... | collective-permute-start | bytes 2359304 | tf_op jit(solution)/shard_map/ppermute | solution.py:41
  17.3 29.2 %collective-permute-start.2 = (bf16[512,768]{1,0:T(8,128)(2,1)S(1)}, bf16[512,768]{1,0:T(8,128)(2,1)S(1)}, u32[]{:S(2)}, u32[]{:S(2)}) collective-permute-start(bf16[512,768]{1,0:T(8,128)(2,1)S(1)} %constant_dynamic-slice_fusion.refs_3_), channel_id=1, source_target_pairs={{0,17},{2,19},{4,21},{6,23},{8,25},{10,27},{12,29},{14,31},{16,1},... | collective-permute-start | bytes 2359304 | tf_op jit(solution)/shard_map/ppermute | solution.py:41
  46.5 8.3 %copy-start.13 = (bf16[512,768]{1,0:T(8,128)(2,1)}, bf16[512,768]{1,0:T(8,128)(2,1)S(1)}, u32[]{:S(2)}) copy-start(bf16[512,768]{1,0:T(8,128)(2,1)S(1)} %collective-permute-done.2.refs_6_) | copy-start | bytes 2359300
  46.5 20.3 %collective-permute-start.7 = (bf16[384,4096]{1,0:T(8,128)(2,1)}, bf16[384,4096]{1,0:T(8,128)(2,1)}, u32[]{:S(2)}, u32[]{:S(2)}) collective-permute-start(bf16[384,4096]{1,0:T(8,128)(2,1)} %halves.3), channel_id=1, source_target_pairs={{0,8},{2,10},{4,12},{6,14},{8,0},{10,2},{12,4},{14,6},{16,24},{18,... | collective-permute-start | bytes 9437192 | tf_op jit(solution)/shard_map/ppermute | solution.py:41
  46.5 29.7 %collective-permute-start.6 = (bf16[512,768]{1,0:T(8,128)(2,1)S(1)}, bf16[512,768]{1,0:T(8,128)(2,1)S(1)}, u32[]{:S(2)}, u32[]{:S(2)}) collective-permute-start(bf16[512,768]{1,0:T(8,128)(2,1)S(1)} %constant_dynamic-slice_fusion.refs_3_), channel_id=1, source_target_pairs={{0,4},{2,6},{4,0},{6,2},{8,12},{10,14},{12,8},{14,10},{16,20},{18,... | collective-permute-start | bytes 2359304 | tf_op jit(solution)/shard_map/ppermute | solution.py:41
  49.5 55.2 %all-to-all-start.1 = ((bf16[4,8,2,64,512]{4,3,2,1,0:T(8,128)(2,1)}), bf16[4,8,2,64,512]{4,3,2,1,0:T(8,128)(2,1)}, u32[]{:S(2)}, u32[]{:S(2)}) async-start(bf16[4,8,2,64,512]{4,3,2,1,0:T(8,128)(2,1)} %broadcast_in_dim.89), calls=%async_computation.1 | async-start | bytes 8388608 | tf_op jit(solution)/shard_map/all_to_all | solution.py:544
  56.1 20.3 %collective-permute-start.4 = (bf16[512,768]{1,0:T(8,128)(2,1)}, bf16[512,768]{1,0:T(8,128)(2,1)S(1)}, u32[]{:S(2)}, u32[]{:S(2)}) collective-permute-start(bf16[512,768]{1,0:T(8,128)(2,1)} %get-tuple-element.147), channel_id=1, source_target_pairs={{0,2},{2,4},{4,6},{6,0},{8,25},{10,27},{12,29},{14,31},{16,18},{18... | collective-permute-start | bytes 2359304 | tf_op jit(solution)/shard_map/ppermute | solution.py:41
  56.6 19.9 %collective-permute-start.5 = (bf16[512,768]{1,0:T(8,128)(2,1)}, bf16[512,768]{1,0:T(8,128)(2,1)}, u32[]{:S(2)}, u32[]{:S(2)}) collective-permute-start(bf16[512,768]{1,0:T(8,128)(2,1)} %get-tuple-element.146), channel_id=1, source_target_pairs={{0,6},{2,0},{4,2},{6,4},{8,25},{10,27},{12,29},{14,31},{16,22},{18... | collective-permute-start | bytes 2359304 | tf_op jit(solution)/shard_map/ppermute | solution.py:41
  66.8 9.7 %copy-start.14 = (bf16[512,768]{1,0:T(8,128)(2,1)S(1)}, bf16[512,768]{1,0:T(8,128)(2,1)}, u32[]{:S(2)}) copy-start(bf16[512,768]{1,0:T(8,128)(2,1)} %copy-done.13) | copy-start | bytes 2359300
  76.6 13.6 %collective-permute-start.8 = (bf16[512,768]{1,0:T(8,128)(2,1)S(1)}, bf16[512,768]{1,0:T(8,128)(2,1)S(1)}, u32[]{:S(2)}, u32[]{:S(2)}) collective-permute-start(bf16[512,768]{1,0:T(8,128)(2,1)S(1)} %broadcast_select_fusion), channel_id=1, source_target_pairs={{0,4},{2,6},{4,0},{6,2},{8,25},{10,27},{12,29},{14,31},{16,20},{18... | collective-permute-start | bytes 2359304 | tf_op jit(solution)/shard_map/ppermute | solution.py:41
  90.2 4.2 %copy-start.24 = (f32[768]{0:T(1024)S(1)}, f32[768]{0:T(1024)}, u32[]{:S(2)}) copy-start(f32[768]{0:T(1024)} %param.11) | copy-start | bytes 9220
  90.2 4.2 %copy-start.25 = (s32[3,1,256]{2,1,0:T(1,128)S(1)}, s32[3,1,256]{2,1,0:T(1,128)}, u32[]{:S(2)}) copy-start(s32[3,1,256]{2,1,0:T(1,128)} %param.16) | copy-start | bytes 9220
  90.2 4.2 %copy-start.26 = (s32[3,1,128]{2,1,0:T(1,128)S(1)}, s32[3,1,128]{2,1,0:T(1,128)}, u32[]{:S(2)}) copy-start(s32[3,1,128]{2,1,0:T(1,128)} %param.14) | copy-start | bytes 4612
  90.2 5.6 %collective-permute-start.9 = (f32[384,768]{1,0:T(8,128)}, f32[384,768]{1,0:T(8,128)S(1)}, u32[]{:S(2)}, u32[]{:S(2)}) collective-permute-start(f32[384,768]{1,0:T(8,128)} %get-tuple-element.89), channel_id=1, source_target_pairs={{0,8},{2,10},{4,12},{6,14},{8,0},{10,2},{12,4},{14,6},{16,24},{18,... | collective-permute-start | bytes 3538952 | tf_op jit(solution)/shard_map/ppermute | solution.py:41
  94.3 3.1 %collective-permute-start.10 = (f32[384,768]{1,0:T(8,128)}, f32[384,768]{1,0:T(8,128)S(1)}, u32[]{:S(2)}, u32[]{:S(2)}) collective-permute-start(f32[384,768]{1,0:T(8,128)} %get-tuple-element.92), channel_id=1, source_target_pairs={{0,8},{2,10},{4,12},{6,14},{8,0},{10,2},{12,4},{14,6},{16,24},{18,... | collective-permute-start | bytes 3538952 | tf_op jit(solution)/shard_map/ppermute | solution.py:41
  98.0 7.8 %copy-start.9 = (bf16[384,512]{1,0:T(8,128)(2,1)}, bf16[384,512]{1,0:T(8,128)(2,1)S(1)}, u32[]{:S(2)}) copy-start(bf16[384,512]{1,0:T(8,128)(2,1)S(1)} %get-tuple-element.93.queries) | copy-start | bytes 1179652
  105.7 20.2 %collective-permute-start.11 = (bf16[4,8,2,64,512]{4,3,2,1,0:T(8,128)(2,1)}, bf16[4,8,2,64,512]{4,3,2,1,0:T(8,128)(2,1)}, u32[]{:S(2)}, u32[]{:S(2)}) collective-permute-start(bf16[4,8,2,64,512]{4,3,2,1,0:T(8,128)(2,1)} %all-to-all-done.1.w.mine), channel_id=1, source_target_pairs={{0,8},{2,10},{4,12},{6,14},{8,0},{10,2},{12,4},{14,6},{16,24},{18,... | collective-permute-start | bytes 12582920 | tf_op jit(solution)/shard_map/ppermute | solution.py:41
  105.7 20.2 %all-to-all-start.2 = ((bf16[16,128,256]{2,1,0:T(8,128)(2,1)}), bf16[16,128,256]{2,1,0:T(8,128)(2,1)S(1)}, u32[]{:S(2)}, u32[]{:S(2)}) async-start(bf16[16,128,256]{2,1,0:T(8,128)(2,1)} %broadcast_in_dim.99), calls=%async_computation.2 | async-start | bytes 2097152 | tf_op jit(solution)/shard_map/all_to_all | solution.py:578
  109.4 10.1 %copy-start.16 = (f32[384,64]{1,0:T(8,128)S(1)}, f32[384,64]{1,0:T(8,128)}, u32[]{:S(2)}) copy-start(f32[384,64]{1,0:T(8,128)} %copy-done.15) | copy-start | bytes 294916
  109.4 10.1 %copy-start.18 = (f32[384,64]{1,0:T(8,128)S(1)}, f32[384,64]{1,0:T(8,128)}, u32[]{:S(2)}) copy-start(f32[384,64]{1,0:T(8,128)} %copy-done.17) | copy-start | bytes 294916
  109.4 10.1 %copy-start.21 = (f32[384,64]{1,0:T(8,128)S(1)}, f32[384,64]{1,0:T(8,128)}, u32[]{:S(2)}) copy-start(f32[384,64]{1,0:T(8,128)} %copy-done.20) | copy-start | bytes 294916
  109.4 10.2 %copy-start.23 = (s32[1,256]{1,0:T(1,128)S(1)}, s32[1,256]{1,0:T(1,128)}, u32[]{:S(2)}) copy-start(s32[1,256]{1,0:T(1,128)} %param.17) | copy-start | bytes 3076
  119.0 2.4 %collective-permute-start.12 = (f32[384,512]{1,0:T(8,128)S(1)}, f32[384,512]{1,0:T(8,128)S(1)}, u32[]{:S(2)}, u32[]{:S(2)}) collective-permute-start(f32[384,512]{1,0:T(8,128)S(1)} %get-tuple-element.100), channel_id=1, source_target_pairs={{0,8},{2,10},{4,12},{6,14},{8,0},{10,2},{12,4},{14,6},{16,24},{18,... | collective-permute-start | bytes 2359304 | tf_op jit(solution)/shard_map/ppermute | solution.py:41
  120.3 5.7 %copy-start.11 = (bf16[384,512]{1,0:T(8,128)(2,1)S(1)}, bf16[384,512]{1,0:T(8,128)(2,1)}, u32[]{:S(2)}) copy-start(bf16[384,512]{1,0:T(8,128)(2,1)} %copy-done.9) | copy-start | bytes 1179652
  124.8 14.8 %collective-permute-start.15 = (bf16[2,256,512]{2,1,0:T(8,128)(2,1)S(1)}, bf16[2,256,512]{2,1,0:T(8,128)(2,1)S(1)}, u32[]{:S(2)}, u32[]{:S(2)}) collective-permute-start(bf16[2,256,512]{2,1,0:T(8,128)(2,1)S(1)} %get-tuple-element.104.short_att.refs_1_), channel_id=1, source_target_pairs={{0,8},{2,10},{4,12},{6,14},{8,0},{10,2},{12,4},{14,6},{16,24},{18,... | collective-permute-start | bytes 1572872 | tf_op jit(solution)/shard_map/ppermute | solution.py:41
  134.2 5.0 %copy-start.19 = (f32[384,64]{1,0:T(8,128)S(1)}, f32[384,64]{1,0:T(8,128)}, u32[]{:S(2)}) copy-start(f32[384,64]{1,0:T(8,128)} %copy-done.17) | copy-start | bytes 294916
  134.2 5.0 %copy-start.22 = (f32[384,64]{1,0:T(8,128)S(1)}, f32[384,64]{1,0:T(8,128)}, u32[]{:S(2)}) copy-start(f32[384,64]{1,0:T(8,128)} %copy-done.20) | copy-start | bytes 294916
  134.2 5.3 %collective-permute-start.14 = (bf16[2,128,512]{2,1,0:T(8,128)(2,1)S(1)}, bf16[2,128,512]{2,1,0:T(8,128)(2,1)S(1)}, u32[]{:S(2)}, u32[]{:S(2)}) collective-permute-start(bf16[2,128,512]{2,1,0:T(8,128)(2,1)S(1)} %get-tuple-element.105.video_att.refs_0_), channel_id=1, source_target_pairs={{0,8},{2,10},{4,12},{6,14},{8,0},{10,2},{12,4},{14,6},{16,24},{18,... | collective-permute-start | bytes 786440 | tf_op jit(solution)/shard_map/ppermute | solution.py:41
  134.2 28.4 %all-to-all-start.3 = ((bf16[16,128,256]{2,1,0:T(8,128)(2,1)}), bf16[16,128,256]{2,1,0:T(8,128)(2,1)S(1)}, u32[]{:S(2)}, u32[]{:S(2)}) async-start(bf16[16,128,256]{2,1,0:T(8,128)(2,1)} %bitcast.127), calls=%async_computation.3 | async-start | bytes 2097152 | tf_op jit(solution)/shard_map/all_to_all | solution.py:597
  145.0 45.0 %collective-permute-start.16 = (bf16[2,1024,512]{2,1,0:T(8,128)(2,1)}, bf16[2,1024,512]{2,1,0:T(8,128)(2,1)}, u32[]{:S(2)}, u32[]{:S(2)}) collective-permute-start(bf16[2,1024,512]{2,1,0:T(8,128)(2,1)} %term.5), channel_id=1, source_target_pairs={{0,64},{2,66},{4,68},{6,70},{8,12},{10,14},{12,8},{14,10},{16,80},... | collective-permute-start | bytes 6291464 | tf_op jit(solution)/shard_map/ppermute | solution.py:41
  153.8 46.4 %collective-permute-start.17 = (bf16[2,1024,512]{2,1,0:T(8,128)(2,1)}, bf16[2,1024,512]{2,1,0:T(8,128)(2,1)}, u32[]{:S(2)}, u32[]{:S(2)}) collective-permute-start(bf16[2,1024,512]{2,1,0:T(8,128)(2,1)} %term.6), channel_id=1, source_target_pairs={{0,32},{2,34},{4,36},{6,38},{8,10},{10,12},{12,14},{14,8},{16,48},... | collective-permute-start | bytes 6291464 | tf_op jit(solution)/shard_map/ppermute | solution.py:41
  159.8 40.4 %collective-permute-start.18 = (bf16[2,1024,512]{2,1,0:T(8,128)(2,1)}, bf16[2,1024,512]{2,1,0:T(8,128)(2,1)}, u32[]{:S(2)}, u32[]{:S(2)}) collective-permute-start(bf16[2,1024,512]{2,1,0:T(8,128)(2,1)} %term.7), channel_id=1, source_target_pairs={{0,96},{2,98},{4,100},{6,102},{8,14},{10,8},{12,10},{14,12},{16,11... | collective-permute-start | bytes 6291464 | tf_op jit(solution)/shard_map/ppermute | solution.py:41
  162.8 1.7 collective-permute-start.13
  170.5 40.0 %all-to-all-start.4 = ((bf16[4,1040,256]{2,1,0:T(8,128)(2,1)}), bf16[4,1040,256]{2,1,0:T(8,128)(2,1)}, u32[]{:S(2)}, u32[]{:S(2)}) async-start(bf16[4,1040,256]{2,1,0:T(8,128)(2,1)} %key_term.1), calls=%async_computation.4 | async-start | bytes 4259840 | tf_op jit(solution)/shard_map/all_to_all | solution.py:611
  180.4 19.7 %copy-start.12 = (bf16[2,1024,512]{2,1,0:T(8,128)(2,1)S(1)}, bf16[2,1024,512]{2,1,0:T(8,128)(2,1)}, u32[]{:S(2)}) copy-start(bf16[2,1024,512]{2,1,0:T(8,128)(2,1)} %term.4) | copy-start | bytes 6291460
  206.7 18.3 %collective-permute-start.19 = (bf16[2,256,512]{2,1,0:T(8,128)(2,1)}, bf16[2,256,512]{2,1,0:T(8,128)(2,1)S(1)}, u32[]{:S(2)}, u32[]{:S(2)}) collective-permute-start(bf16[2,256,512]{2,1,0:T(8,128)(2,1)} %fusion), channel_id=1, source_target_pairs={{0,4},{2,6},{4,0},{6,2},{8,72},{10,74},{12,76},{14,78},{16,20},{18... | collective-permute-start | bytes 1572872 | tf_op jit(solution)/shard_map/ppermute | solution.py:41
  207.3 17.7 %collective-permute-start.20 = (bf16[2,256,512]{2,1,0:T(8,128)(2,1)}, bf16[2,256,512]{2,1,0:T(8,128)(2,1)S(1)}, u32[]{:S(2)}, u32[]{:S(2)}) collective-permute-start(bf16[2,256,512]{2,1,0:T(8,128)(2,1)} %fusion.1), channel_id=1, source_target_pairs={{0,2},{2,4},{4,6},{6,0},{8,40},{10,42},{12,44},{14,46},{16,18},{18... | collective-permute-start | bytes 1572872 | tf_op jit(solution)/shard_map/ppermute | solution.py:41
  208.8 16.2 %collective-permute-start.21 = (bf16[2,256,512]{2,1,0:T(8,128)(2,1)S(1)}, bf16[2,256,512]{2,1,0:T(8,128)(2,1)}, u32[]{:S(2)}, u32[]{:S(2)}) collective-permute-start(bf16[2,256,512]{2,1,0:T(8,128)(2,1)S(1)} %fusion.2), channel_id=1, source_target_pairs={{0,6},{2,0},{4,2},{6,4},{8,104},{10,106},{12,108},{14,110},{16,22}... | collective-permute-start | bytes 1572872 | tf_op jit(solution)/shard_map/ppermute | solution.py:41
  214.2 21.8 %all-to-all-start.5 = ((bf16[16,80,256]{2,1,0:T(8,128)(2,1)}), bf16[16,80,256]{2,1,0:T(8,128)(2,1)S(1)}, u32[]{:S(2)}, u32[]{:S(2)}) async-start(bf16[16,80,256]{2,1,0:T(8,128)(2,1)} %pad_maximum_fusion), calls=%async_computation.5 | async-start | bytes 1310720 | tf_op jit(solution)/shard_map/all_to_all | solution.py:494
  225.0 14.1 %copy-start.1 = (bf16[1024,768]{1,0:T(8,128)(2,1)S(1)}, bf16[1024,768]{1,0:T(8,128)(2,1)}, u32[]{:S(2)}) copy-start(bf16[1024,768]{1,0:T(8,128)(2,1)} %param.10) | copy-start | bytes 4718596
  227.3 8.9 %collective-permute-start.22 = (bf16[2,64,512]{2,1,0:T(8,128)(2,1)}, bf16[2,64,512]{2,1,0:T(8,128)(2,1)S(1)}, u32[]{:S(2)}, u32[]{:S(2)}) collective-permute-start(bf16[2,64,512]{2,1,0:T(8,128)(2,1)} %get-tuple-element.144), channel_id=1, source_target_pairs={{0,1},{2,3},{4,5},{6,7},{8,9},{10,11},{12,13},{14,15},{16,17},{18,... | collective-permute-start | bytes 393224 | tf_op jit(solution)/shard_map/ppermute | solution.py:41
  229.4 7.6 %collective-permute-start.23 = (bf16[2,64,512]{2,1,0:T(8,128)(2,1)}, bf16[2,64,512]{2,1,0:T(8,128)(2,1)S(1)}, u32[]{:S(2)}, u32[]{:S(2)}) collective-permute-start(bf16[2,64,512]{2,1,0:T(8,128)(2,1)} %get-tuple-element.143), channel_id=1, source_target_pairs={{0,16},{2,18},{4,20},{6,22},{8,24},{10,26},{12,28},{14,30},{16,1},... | collective-permute-start | bytes 393224 | tf_op jit(solution)/shard_map/ppermute | solution.py:41
  230.0 7.1 %collective-permute-start.24 = (bf16[2,64,512]{2,1,0:T(8,128)(2,1)}, bf16[2,64,512]{2,1,0:T(8,128)(2,1)S(1)}, u32[]{:S(2)}, u32[]{:S(2)}) collective-permute-start(bf16[2,64,512]{2,1,0:T(8,128)(2,1)} %get-tuple-element.142), channel_id=1, source_target_pairs={{0,17},{2,19},{4,21},{6,23},{8,25},{10,27},{12,29},{14,31},{16,0},... | collective-permute-start | bytes 393224 | tf_op jit(solution)/shard_map/ppermute | solution.py:41
  (10 other events, 17.0 us)

commit v5 on v4

--- a/solution.py
+++ b/solution.py
@@ -324,7 +324,7 @@
     return ref[0, :, 0].reshape(ATT, 512)
 
 
-def grad_attended_kernel(core_ref, video, short, other, w, total_own, total_other):
+def grad_attended_kernel(core_ref, video, short, other, w, total_own, sent, total_other):
     nv = video.shape[0]
 
     @pl.when(pl.program_id(0) == 0)
@@ -336,6 +336,10 @@
     total_other[...] += jnp.dot(other[...], block, preferred_element_type=F32)
     total_own[:nv] += jnp.dot(video[...], block, preferred_element_type=F32)
     total_own[nv:] += jnp.dot(short[...], block, preferred_element_type=F32)
+
+    @pl.when(pl.program_id(0) == pl.num_programs(0) - 1)
+    def _():
+        sent[...] = total_other[...].astype(BF)
 
 
 def grad_attended_parts(core, video, short, other, w):
@@ -346,7 +350,8 @@
     return call(
         grad_attended_kernel, "grad_attended", (8,),
         [own(nv), own(ns), ((rows, 512), lambda j, s: (0, j)), W_BLOCK], [out, out],
-        [shaped((rows, ATT), F32)] * 2, core, flops=4 * rows * 4096 * 512,
+        [shaped((rows, ATT), F32), shaped((rows, ATT))], core, flops=4 * rows * 4096 * 512,
+        scratch=[pltpu.VMEM((rows, ATT), F32)],
         traffic=rows * 16384 + 4096 * 1024, limit=STREAM,
     )(video, short, other, w)
 

time: 242 us -> 241 us (level)
  no operation moved by 1% of the time
where the time goes in v5:
time: 241 us; the launch traced here: 238 us
  Pallas kernels  101 us (42%)
  starting transfers between devices  67.3 us (28%)
  waiting for transfers between devices  38.1 us (16%)
  other arithmetic  18.6 us (8%)
  local copies, waits for them, and re-layouts  12.2 us (5%)
    ppermute x25, starting transfers between devices, move(): return lax.ppermute(value, AXES, pairs(target))  33.6 us
    ppermute x25, waiting for transfers between devices, move(): return lax.ppermute(value, AXES, pairs(target))  24.6 us
    pallas_call x4, Pallas kernels, term(): call(term_kernel, 'term', (4,), [((512, wide), lambda i, s: (2 * s[0] + j...  21.6 us
    pallas_call x2, Pallas kernels, turned(): call(turn_kernel, 'turned', (8,), [own(nv), own(ns), ((rows, 512), lambda...  18.8 us
    pallas_call x3, Pallas kernels, project(): call(functools.partial(project_kernel, parts=parts, added=len(before) > 0...  17.9 us
    pallas_call x1, Pallas kernels, grad_attended_parts(): call(grad_attended_kernel, 'grad_attended', (8,), [own(nv), own(ns), ((ro...  9.55 us
    pallas_call x1, Pallas kernels, layer_out(): call(layer_out_kernel, 'layer_out', (8,), [att(nv), att(ns), W_BLOCK, W_B...  9.54 us
    all_to_all x1, starting transfers between devices, key_sum(): lax.all_to_all(parts, AXES, 0, 0, tiled=True, axis_index_groups=LATE_GROUPS)  8.91 us
  transfers between devices with their start and end apart: 31, of which 14 were waited for; matrix products, arithmetic and copies ran while one was open for 10% of the time, Pallas kernels for 40%

profile of v5, /device:TPU:0, one launch (start us, length us, event | category | flops | bytes accessed | tf_op | source)
XLA Modules:
  0.0 238.2 jit_solution(15504364816948799378)
XLA Ops:
  0.7 4.4 %halves.2 = bf16[384,4096]{1,0:T(8,128)(2,1)} custom-call(s32[1]{0:T(128)S(6)} %sub.8.core_ref, bf16[128,8192]{1,0:T(8,128)(2,1)} %bitcast.136, bf16[128,8192]{1,0:T(8,128)(2,1)} %bitcast.137, bf16[256,8192]{1,0:T(8,128)(2,1)} %bitcast.130, bf16[256,8192]{1,0:T(8,128)(2,1)} %bitcast.131), custom_call_target="tpu_custom_call" | custom-call | bytes 6291456 | tf_op jit(solution)/shard_map/halves/pallas_call | solution.py:119
  6.9 7.0 %all-to-all-start = ((bf16[8,2,64,512]{3,2,1,0:T(8,128)(2,1)}), bf16[8,2,64,512]{3,2,1,0:T(8,128)(2,1)}, u32[]{:S(2)}, u32[]{:S(2)}) async-start(bf16[8,2,64,512]{3,2,1,0:T(8,128)(2,1)} %broadcast_in_dim.88), calls=%async_computation | async-start | bytes 2097152 | tf_op jit(solution)/shard_map/all_to_all | solution.py:525
  14.0 2.1 collective-permute-start
  17.3 3.3 %collective-permute-start.2 = (bf16[512,768]{1,0:T(8,128)(2,1)S(1)}, bf16[512,768]{1,0:T(8,128)(2,1)S(1)}, u32[]{:S(2)}, u32[]{:S(2)}) collective-permute-start(bf16[512,768]{1,0:T(8,128)(2,1)S(1)} %constant_dynamic-slice_fusion.refs_3_), channel_id=1, source_target_pairs={{0,17},{2,19},{4,21},{6,23},{8,25},{10,27},{12,29},{14,31},{16,1},... | collective-permute-start | bytes 2359304 | tf_op jit(solution)/shard_map/ppermute | solution.py:41
  20.7 9.4 %turned.2.tokens = bf16[4096,768]{1,0:T(8,128)(2,1)} custom-call(s32[65]{0:T(128)S(1)} %stack.331.tab, bf16[128,8192]{1,0:T(8,128)(2,1)} %bitcast.138, bf16[256,8192]{1,0:T(8,128)(2,1)} %bitcast.132, bf16[384,4096]{1,0:T(8,128)(2,1)} %collective-permute-done.3.other.refs_2_), custom_call_target="tpu_custom_call" | custom-call | bytes 12582912 | tf_op jit(solution)/shard_map/turned/pallas_call | solution.py:141
  30.2 2.0 all-to-all-done
  32.2 3.8 %broadcast_in_dim.89 = bf16[4,8,2,64,512]{4,3,2,1,0:T(8,128)(2,1)} broadcast(bf16[8,2,64,512]{3,2,1,0:T(8,128)(2,1)} %all-to-all-done), dimensions={1,2,3,4} | broadcast | bytes 5242880 | tf_op jit(solution)/shard_map/broadcast_in_dim | solution.py:547
  36.0 4.3 %halves.3 = bf16[384,4096]{1,0:T(8,128)(2,1)} custom-call(s32[1]{0:T(128)S(6)} %sub.8.core_ref, bf16[128,8192]{1,0:T(8,128)(2,1)} %bitcast.146, bf16[128,8192]{1,0:T(8,128)(2,1)} %bitcast.147, bf16[256,8192]{1,0:T(8,128)(2,1)} %bitcast.142, bf16[256,8192]{1,0:T(8,128)(2,1)} %bitcast.143), custom_call_target="tpu_custom_call" | custom-call | bytes 6291456 | tf_op jit(solution)/shard_map/halves/pallas_call | solution.py:119
  40.3 5.9 %collective-permute-done.refs_4_ = bf16[512,768]{1,0:T(8,128)(2,1)S(1)} collective-permute-done((bf16[512,768]{1,0:T(8,128)(2,1)S(1)}, bf16[512,768]{1,0:T(8,128)(2,1)S(1)}, u32[]{:S(2)}, u32[]{:S(2)}) %collective-permute-start) | collective-permute-done | bytes 786464 | tf_op jit(solution)/shard_map/ppermute | solution.py:41
  46.5 3.0 %collective-permute-start.6 = (bf16[512,768]{1,0:T(8,128)(2,1)S(1)}, bf16[512,768]{1,0:T(8,128)(2,1)S(1)}, u32[]{:S(2)}, u32[]{:S(2)}) collective-permute-start(bf16[512,768]{1,0:T(8,128)(2,1)S(1)} %constant_dynamic-slice_fusion.refs_3_), channel_id=1, source_target_pairs={{0,4},{2,6},{4,0},{6,2},{8,12},{10,14},{12,8},{14,10},{16,20},{18,... | collective-permute-start | bytes 2359304 | tf_op jit(solution)/shard_map/ppermute | solution.py:41
  49.5 5.3 %all-to-all-start.1 = ((bf16[4,8,2,64,512]{4,3,2,1,0:T(8,128)(2,1)}), bf16[4,8,2,64,512]{4,3,2,1,0:T(8,128)(2,1)}, u32[]{:S(2)}, u32[]{:S(2)}) async-start(bf16[4,8,2,64,512]{4,3,2,1,0:T(8,128)(2,1)} %broadcast_in_dim.89), calls=%async_computation.1 | async-start | bytes 8388608 | tf_op jit(solution)/shard_map/all_to_all | solution.py:549
  56.6 2.7 %collective-permute-start.5 = (bf16[512,768]{1,0:T(8,128)(2,1)}, bf16[512,768]{1,0:T(8,128)(2,1)}, u32[]{:S(2)}, u32[]{:S(2)}) collective-permute-start(bf16[512,768]{1,0:T(8,128)(2,1)} %get-tuple-element.146), channel_id=1, source_target_pairs={{0,6},{2,0},{4,2},{6,4},{8,25},{10,27},{12,29},{14,31},{16,22},{18... | collective-permute-start | bytes 2359304 | tf_op jit(solution)/shard_map/ppermute | solution.py:41
  59.4 7.4 %project.3 = (f32[384,768]{1,0:T(8,128)}, f32[384,768]{1,0:T(8,128)}) custom-call(s32[5]{0:T(128)S(1)} %stack.337.tab, bf16[128,8192]{1,0:T(8,128)(2,1)} %bitcast.139, bf16[256,8192]{1,0:T(8,128)(2,1)} %bitcast.133, bf16[384,4096]{1,0:T(8,128)(2,1)} %collective-permute-done.3.other.refs_2_, bf16[512,768]{1,0:T(8,128)(2,1)S(1)} %constant_dynamic-slice_fusion.refs_3_, ...), custom_call_target="tpu_custom_call" | custom-call | flops 2415919104 | bytes 8650752 | tf_op jit(solution)/shard_map/project/pallas_call | solution.py:194
  66.8 9.4 %turned.3.cot = bf16[4096,768]{1,0:T(8,128)(2,1)} custom-call(s32[65]{0:T(128)S(1)} %stack.331.tab, bf16[128,8192]{1,0:T(8,128)(2,1)} %bitcast.148, bf16[256,8192]{1,0:T(8,128)(2,1)} %bitcast.144, bf16[384,4096]{1,0:T(8,128)(2,1)} %collective-permute-done.7.other), custom_call_target="tpu_custom_call" | custom-call | bytes 12582912 | tf_op jit(solution)/shard_map/turned/pallas_call | solution.py:141
  76.6 2.9 %collective-permute-start.8 = (bf16[512,768]{1,0:T(8,128)(2,1)S(1)}, bf16[512,768]{1,0:T(8,128)(2,1)S(1)}, u32[]{:S(2)}, u32[]{:S(2)}) collective-permute-start(bf16[512,768]{1,0:T(8,128)(2,1)S(1)} %broadcast_select_fusion), channel_id=1, source_target_pairs={{0,4},{2,6},{4,0},{6,2},{8,25},{10,27},{12,29},{14,31},{16,20},{18... | collective-permute-start | bytes 2359304 | tf_op jit(solution)/shard_map/ppermute | solution.py:41
  79.7 7.0 %project.4 = (f32[384,768]{1,0:T(8,128)}, f32[384,768]{1,0:T(8,128)}) custom-call(s32[4]{0:T(128)S(1)} %pad_add_fusion.3.tab, bf16[128,8192]{1,0:T(8,128)(2,1)} %bitcast.140, bf16[256,8192]{1,0:T(8,128)(2,1)} %bitcast.134, bf16[384,4096]{1,0:T(8,128)(2,1)} %collective-permute-done.3.other.refs_2_, bf16[512,768]{1,0:T(8,128)(2,1)S(1)} %collective-permute-done.6.refs_3_, ...), custom_call_target="tpu_custom_call" | custom-call | flops 1811939328 | bytes 7077888 | tf_op jit(solution)/shard_map/project/pallas_call | solution.py:194
  86.6 3.6 %collective-permute-done.8.refs_3_ = bf16[512,768]{1,0:T(8,128)(2,1)S(1)} collective-permute-done((bf16[512,768]{1,0:T(8,128)(2,1)S(1)}, bf16[512,768]{1,0:T(8,128)(2,1)S(1)}, u32[]{:S(2)}, u32[]{:S(2)}) %collective-permute-start.8) | collective-permute-done | bytes 786464 | tf_op jit(solution)/shard_map/ppermute | solution.py:41
  90.9 3.5 %project.5 = (f32[384,768]{1,0:T(8,128)S(1)}, f32[384,768]{1,0:T(8,128)}) custom-call(s32[2]{0:T(128)S(1)} %pad_add_fusion.4.tab, bf16[128,8192]{1,0:T(8,128)(2,1)} %bitcast.141, bf16[256,8192]{1,0:T(8,128)(2,1)} %bitcast.135, bf16[384,4096]{1,0:T(8,128)(2,1)} %collective-permute-done.3.other.refs_2_, bf16[512,768]{1,0:T(8,128)(2,1)S(1)} %collective-permute-done.8.refs_3_), custom_call_target="tpu_custom_call" | custom-call | flops 603979776 | bytes 3932160 | tf_op jit(solution)/shard_map/project/pallas_call | solution.py:194
  95.8 1.6 collective-permute-done.10.far_got
  98.0 6.7 %all-to-all-done.1.w.mine = bf16[4,8,2,64,512]{4,3,2,1,0:T(8,128)(2,1)} async-done(((bf16[4,8,2,64,512]{4,3,2,1,0:T(8,128)(2,1)}), bf16[4,8,2,64,512]{4,3,2,1,0:T(8,128)(2,1)}, u32[]{:S(2)}, u32[]{:S(2)}) %all-to-all-start.1) | async-done | bytes 4194336 | tf_op jit(solution)/shard_map/all_to_all | solution.py:549
  105.7 3.7 %all-to-all-start.2 = ((bf16[16,128,256]{2,1,0:T(8,128)(2,1)}), bf16[16,128,256]{2,1,0:T(8,128)(2,1)S(1)}, u32[]{:S(2)}, u32[]{:S(2)}) async-start(bf16[16,128,256]{2,1,0:T(8,128)(2,1)} %broadcast_in_dim.99), calls=%async_computation.2 | async-start | bytes 2097152 | tf_op jit(solution)/shard_map/all_to_all | solution.py:583
  109.5 9.6 %grad_attended.1 = (f32[384,512]{1,0:T(8,128)S(1)}, bf16[384,512]{1,0:T(8,128)(2,1)S(1)}) custom-call(s32[1]{0:T(128)} %bitcast.1.core_ref.tab, bf16[128,8192]{1,0:T(8,128)(2,1)} %bitcast.149, bf16[256,8192]{1,0:T(8,128)(2,1)} %bitcast.145, bf16[384,4096]{1,0:T(8,128)(2,1)} %collective-permute-done.7.other, bf16[4,8,2,64,512]{4,3,2,1,0:T(8,128)(2,1)} %all-to-all-done.1.w.mine), custom_call_target="tpu_custom_call" | custom-call | flops 3221225472 | bytes 10485760 | tf_op jit(solution)/shard_map/grad_attended/pallas_call | solution.py:350
  121.6 2.4 %short_attention.1 = (bf16[2,256,512]{2,1,0:T(8,128)(2,1)S(1)}, bf16[256,256]{1,0:T(8,128)(2,1)S(1)}) custom-call(s32[1]{0:T(128)} %constant.347.clone.1.tab, bf16[256,512]{1,0:T(8,128)(2,1)S(1)} %slice.158.queries, bf16[256,256]{1,0:T(8,128)(2,1)S(1)} %slice.159.keys_values, s32[2,256,256]{2,1,0:T(8,128)S(1)} %pad_add_fusion.segments, ...), custom_call_target="tpu_custom_call" | custom-call | flops 335544320 | bytes 262144 | tf_op jit(solution)/shard_map/short_attention/pallas_call | solution.py:292
  124.5 1.5 all-to-all-done.2
  128.1 5.0 %video_attention.1 = (bf16[2,128,512]{2,1,0:T(8,128)(2,1)S(1)}, bf16[2048,256]{1,0:T(8,128)(2,1)S(1)}) custom-call(s32[1]{0:T(128)} %bitcast.72.tab, bf16[384,512]{1,0:T(8,128)(2,1)S(1)} %copy-done.9, bf16[2048,256]{1,0:T(8,128)(2,1)S(1)} %bitcast.128, s32[1,8,128]{2,1,0:T(8,128)S(1)} %broadcast_in_dim.100.segments, f32[384,512]{1,0:T(8,128)S(1)} %copy-done.6, ...), custom_call_target="tpu_custom_call" | custom-call | flops 1342177280 | bytes 2097152 | tf_op jit(solution)/shard_map/video_attention/pallas_call | solution.py:292
  134.1 4.3 %all-to-all-start.3 = ((bf16[16,128,256]{2,1,0:T(8,128)(2,1)}), bf16[16,128,256]{2,1,0:T(8,128)(2,1)S(1)}, u32[]{:S(2)}, u32[]{:S(2)}) async-start(bf16[16,128,256]{2,1,0:T(8,128)(2,1)} %bitcast.127), calls=%async_computation.3 | async-start | bytes 2097152 | tf_op jit(solution)/shard_map/all_to_all | solution.py:602
  138.7 5.4 %term.5 = bf16[2,1024,512]{2,1,0:T(8,128)(2,1)} custom-call(s32[1]{0:T(128)} %bitcast.91.tab, bf16[4096,768]{1,0:T(8,128)(2,1)} %turned.3.cot, bf16[4096,768]{1,0:T(8,128)(2,1)} %turned.2.tokens, bf16[2,128,512]{2,1,0:T(8,128)(2,1)S(1)} %get-tuple-element.105.video_att.refs_0_, bf16[2,256,512]{2,1,0:T(8,128)(2,1)S(1)} %get-tuple-element.104.short_att.refs_1_, ...), custom_call_target="tpu_custom_call" | custom-call | flops 1610612736 | bytes 6815744 | tf_op jit(solution)/shard_map/term/pallas_call | solution.py:415
  144.1 3.4 %collective-permute-start.16 = (bf16[2,1024,512]{2,1,0:T(8,128)(2,1)}, bf16[2,1024,512]{2,1,0:T(8,128)(2,1)}, u32[]{:S(2)}, u32[]{:S(2)}) collective-permute-start(bf16[2,1024,512]{2,1,0:T(8,128)(2,1)} %term.5), channel_id=1, source_target_pairs={{0,64},{2,66},{4,68},{6,70},{8,12},{10,14},{12,8},{14,10},{16,80},... | collective-permute-start | bytes 6291464 | tf_op jit(solution)/shard_map/ppermute | solution.py:41
  147.6 5.4 %term.6 = bf16[2,1024,512]{2,1,0:T(8,128)(2,1)} custom-call(s32[1]{0:T(128)} %bitcast.93.tab, bf16[4096,768]{1,0:T(8,128)(2,1)} %turned.3.cot, bf16[4096,768]{1,0:T(8,128)(2,1)} %turned.2.tokens, bf16[2,128,512]{2,1,0:T(8,128)(2,1)S(1)} %get-tuple-element.105.video_att.refs_0_, bf16[2,256,512]{2,1,0:T(8,128)(2,1)S(1)} %get-tuple-element.104.short_att.refs_1_, ...), custom_call_target="tpu_custom_call" | custom-call | flops 1610612736 | bytes 6815744 | tf_op jit(solution)/shard_map/term/pallas_call | solution.py:415
  153.5 5.4 %term.7 = bf16[2,1024,512]{2,1,0:T(8,128)(2,1)} custom-call(s32[1]{0:T(128)} %bitcast.95.tab, bf16[4096,768]{1,0:T(8,128)(2,1)} %turned.3.cot, bf16[4096,768]{1,0:T(8,128)(2,1)} %turned.2.tokens, bf16[2,128,512]{2,1,0:T(8,128)(2,1)S(1)} %get-tuple-element.105.video_att.refs_0_, bf16[2,256,512]{2,1,0:T(8,128)(2,1)S(1)} %get-tuple-element.104.short_att.refs_1_, ...), custom_call_target="tpu_custom_call" | custom-call | flops 1610612736 | bytes 6815744 | tf_op jit(solution)/shard_map/term/pallas_call | solution.py:415
  158.9 2.7 %collective-permute-start.18 = (bf16[2,1024,512]{2,1,0:T(8,128)(2,1)}, bf16[2,1024,512]{2,1,0:T(8,128)(2,1)}, u32[]{:S(2)}, u32[]{:S(2)}) collective-permute-start(bf16[2,1024,512]{2,1,0:T(8,128)(2,1)} %term.7), channel_id=1, source_target_pairs={{0,96},{2,98},{4,100},{6,102},{8,14},{10,8},{12,10},{14,12},{16,11... | collective-permute-start | bytes 6291464 | tf_op jit(solution)/shard_map/ppermute | solution.py:41
  163.9 5.8 %key_term.1 = bf16[4,1040,256]{2,1,0:T(8,128)(2,1)} custom-call(s32[1]{0:T(128)} %bitcast.tab, bf16[4,4,4,64,768]{4,3,2,1,0:T(8,128)(2,1)} %bitcast.129, bf16[384,256]{1,0:T(8,128)(2,1)S(1)} %pad_maximum_fusion.1.ga, bf16[384,256]{1,0:T(8,128)(2,1)S(1)} %collective-permute-done.13.gb, bf16[16,256]{1,0:T(8,128)(2,1)S(1)} %maximum_maximum_fusion.tail), custom_call_target="tpu_custom_call" | custom-call | flops 1610612736 | bytes 8388608 | tf_op jit(solution)/shard_map/key_term/pallas_call | solution.py:474
  169.7 4.5 %all-to-all-start.4 = ((bf16[4,1040,256]{2,1,0:T(8,128)(2,1)}), bf16[4,1040,256]{2,1,0:T(8,128)(2,1)}, u32[]{:S(2)}, u32[]{:S(2)}) async-start(bf16[4,1040,256]{2,1,0:T(8,128)(2,1)} %key_term.1), calls=%async_computation.4 | async-start | bytes 4259840 | tf_op jit(solution)/shard_map/all_to_all | solution.py:616
  174.2 5.4 %term.4 = bf16[2,1024,512]{2,1,0:T(8,128)(2,1)} custom-call(s32[1]{0:T(128)} %bitcast.89.tab, bf16[4096,768]{1,0:T(8,128)(2,1)} %turned.3.cot, bf16[4096,768]{1,0:T(8,128)(2,1)} %turned.2.tokens, bf16[2,128,512]{2,1,0:T(8,128)(2,1)S(1)} %get-tuple-element.105.video_att.refs_0_, bf16[2,256,512]{2,1,0:T(8,128)(2,1)S(1)} %get-tuple-element.104.short_att.refs_1_, ...), custom_call_target="tpu_custom_call" | custom-call | flops 1610612736 | bytes 6815744 | tf_op jit(solution)/shard_map/term/pallas_call | solution.py:415
  179.6 9.5 %layer_out.1 = (bf16[128,8192]{1,0:T(8,128)(2,1)}, bf16[256,8192]{1,0:T(8,128)(2,1)}) custom-call(s32[1]{0:T(128)} %bitcast.1.core_ref.tab, bf16[2,128,512]{2,1,0:T(8,128)(2,1)S(1)} %get-tuple-element.105.video_att.refs_0_, bf16[2,256,512]{2,1,0:T(8,128)(2,1)S(1)} %get-tuple-element.104.short_att.refs_1_, bf16[4,8,2,64,512]{4,3,2,1,0:T(8,128)(2,1)} %all-to-all-done.1.w.mine, ...), custom_call_target="tpu_custom_call" | custom-call | flops 3221225472 | bytes 14680064 | tf_op jit(solution)/shard_map/layer_out/pallas_call | solution.py:370
  189.1 10.2 %collective-permute-done.17 = bf16[2,1024,512]{2,1,0:T(8,128)(2,1)} collective-permute-done((bf16[2,1024,512]{2,1,0:T(8,128)(2,1)}, bf16[2,1024,512]{2,1,0:T(8,128)(2,1)}, u32[]{:S(2)}, u32[]{:S(2)}) %collective-permute-start.17) | collective-permute-done | bytes 2097184 | tf_op jit(solution)/shard_map/ppermute | solution.py:41
  199.3 2.4 %fusion = bf16[2,256,512]{2,1,0:T(8,128)(2,1)} fusion(bf16[2,4,256,512]{3,2,1,0:T(8,128)(2,1)} %bitcast.96, s32[]{:T(128)S(6)} %select_n.501, bf16[2,4,256,512]{3,2,1,0:T(8,128)(2,1)} %bitcast.94, bf16[2,4,256,512]{3,2,1,0:T(8,128)(2,1)} %bitcast.92, bf16[2,4,256,512]{3,2,1,0:T(8,128)(2,1)S(1)} %bitcast.151), kind=kLoop, calls=%fused_computation.10 | loop fusion | flops 2097152 | bytes 2621444 | tf_op jit(solution)/shard_map/add | solution.py:437
  201.8 2.4 %fusion.1 = bf16[2,256,512]{2,1,0:T(8,128)(2,1)} fusion(s32[]{:T(128)S(6)} %select_n.503, bf16[2,4,256,512]{3,2,1,0:T(8,128)(2,1)S(1)} %bitcast.152, bf16[2,4,256,512]{3,2,1,0:T(8,128)(2,1)} %bitcast.92, bf16[2,4,256,512]{3,2,1,0:T(8,128)(2,1)} %bitcast.94, bf16[2,4,256,512]{3,2,1,0:T(8,128)(2,1)} %bitcast.96), kind=kLoop, calls=%fused_computation.11 | loop fusion | flops 2097152 | bytes 2621444 | tf_op jit(solution)/shard_map/add | solution.py:437
  204.2 1.6 fusion.2
  206.4 1.5 collective-permute-start.20
  207.9 1.8 collective-permute-start.21
  210.5 1.9 slice_reduce_fusion
  213.4 8.9 %all-to-all-start.5 = ((bf16[16,80,256]{2,1,0:T(8,128)(2,1)}), bf16[16,80,256]{2,1,0:T(8,128)(2,1)S(1)}, u32[]{:S(2)}, u32[]{:S(2)}) async-start(bf16[16,80,256]{2,1,0:T(8,128)(2,1)} %pad_maximum_fusion), calls=%async_computation.5 | async-start | bytes 1310720 | tf_op jit(solution)/shard_map/all_to_all | solution.py:499
  222.3 1.8 add_bitcast_fusion
  224.2 2.2 fusion.5
  226.4 2.2 collective-permute-start.22
  229.1 2.7 %collective-permute-start.24 = (bf16[2,64,512]{2,1,0:T(8,128)(2,1)}, bf16[2,64,512]{2,1,0:T(8,128)(2,1)S(1)}, u32[]{:S(2)}, u32[]{:S(2)}) collective-permute-start(bf16[2,64,512]{2,1,0:T(8,128)(2,1)} %get-tuple-element.142), channel_id=1, source_target_pairs={{0,17},{2,19},{4,21},{6,23},{8,25},{10,27},{12,29},{14,31},{16,0},... | collective-permute-start | bytes 393224 | tf_op jit(solution)/shard_map/ppermute | solution.py:41
  231.8 3.3 %all-to-all-done.5 = bf16[16,80,256]{2,1,0:T(8,128)(2,1)S(1)} async-done(((bf16[16,80,256]{2,1,0:T(8,128)(2,1)}), bf16[16,80,256]{2,1,0:T(8,128)(2,1)S(1)}, u32[]{:S(2)}, u32[]{:S(2)}) %all-to-all-start.5) | async-done | bytes 655392 | tf_op jit(solution)/shard_map/all_to_all | solution.py:499
  (148 shorter events, 25.0 us)
Async XLA Ops:
  0.6 13.3 %copy-start = (bf16[1024,768]{1,0:T(8,128)(2,1)S(1)}, bf16[1024,768]{1,0:T(8,128)(2,1)}, u32[]{:S(2)}) copy-start(bf16[1024,768]{1,0:T(8,128)(2,1)} %param.10) | copy-start | bytes 4718596
  0.7 4.5 %copy-start.3 = (bf16[64,8192]{1,0:T(8,128)(2,1)S(1)}, bf16[64,8192]{1,0:T(8,128)(2,1)}, u32[]{:S(2)}) copy-start(bf16[64,8192]{1,0:T(8,128)(2,1)} %block.1) | copy-start | bytes 3145732
  5.1 15.7 %collective-permute-start.3 = (bf16[384,4096]{1,0:T(8,128)(2,1)}, bf16[384,4096]{1,0:T(8,128)(2,1)}, u32[]{:S(2)}, u32[]{:S(2)}) collective-permute-start(bf16[384,4096]{1,0:T(8,128)(2,1)} %halves.2), channel_id=1, source_target_pairs={{0,8},{2,10},{4,12},{6,14},{8,0},{10,2},{12,4},{14,6},{16,24},{18,... | collective-permute-start | bytes 9437192 | tf_op jit(solution)/shard_map/ppermute | solution.py:41
  6.9 25.3 %all-to-all-start = ((bf16[8,2,64,512]{3,2,1,0:T(8,128)(2,1)}), bf16[8,2,64,512]{3,2,1,0:T(8,128)(2,1)}, u32[]{:S(2)}, u32[]{:S(2)}) async-start(bf16[8,2,64,512]{3,2,1,0:T(8,128)(2,1)} %broadcast_in_dim.88), calls=%async_computation | async-start | bytes 2097152 | tf_op jit(solution)/shard_map/all_to_all | solution.py:525
  14.0 32.3 %collective-permute-start = (bf16[512,768]{1,0:T(8,128)(2,1)S(1)}, bf16[512,768]{1,0:T(8,128)(2,1)S(1)}, u32[]{:S(2)}, u32[]{:S(2)}) collective-permute-start(bf16[512,768]{1,0:T(8,128)(2,1)S(1)} %constant_dynamic-slice_fusion.refs_3_), channel_id=1, source_target_pairs={{0,2},{2,4},{4,6},{6,0},{8,10},{10,12},{12,14},{14,8},{16,18},{18,... | collective-permute-start | bytes 2359304 | tf_op jit(solution)/shard_map/ppermute | solution.py:41
  16.0 30.2 %collective-permute-start.1 = (bf16[512,768]{1,0:T(8,128)(2,1)S(1)}, bf16[512,768]{1,0:T(8,128)(2,1)}, u32[]{:S(2)}, u32[]{:S(2)}) collective-permute-start(bf16[512,768]{1,0:T(8,128)(2,1)S(1)} %constant_dynamic-slice_fusion.refs_3_), channel_id=1, source_target_pairs={{0,6},{2,0},{4,2},{6,4},{8,14},{10,8},{12,10},{14,12},{16,22},{18,... | collective-permute-start | bytes 2359304 | tf_op jit(solution)/shard_map/ppermute | solution.py:41
  17.3 29.2 %collective-permute-start.2 = (bf16[512,768]{1,0:T(8,128)(2,1)S(1)}, bf16[512,768]{1,0:T(8,128)(2,1)S(1)}, u32[]{:S(2)}, u32[]{:S(2)}) collective-permute-start(bf16[512,768]{1,0:T(8,128)(2,1)S(1)} %constant_dynamic-slice_fusion.refs_3_), channel_id=1, source_target_pairs={{0,17},{2,19},{4,21},{6,23},{8,25},{10,27},{12,29},{14,31},{16,1},... | collective-permute-start | bytes 2359304 | tf_op jit(solution)/shard_map/ppermute | solution.py:41
  46.5 8.3 %copy-start.13 = (bf16[512,768]{1,0:T(8,128)(2,1)}, bf16[512,768]{1,0:T(8,128)(2,1)S(1)}, u32[]{:S(2)}) copy-start(bf16[512,768]{1,0:T(8,128)(2,1)S(1)} %collective-permute-done.2.refs_6_) | copy-start | bytes 2359300
  46.5 20.3 %collective-permute-start.7 = (bf16[384,4096]{1,0:T(8,128)(2,1)}, bf16[384,4096]{1,0:T(8,128)(2,1)}, u32[]{:S(2)}, u32[]{:S(2)}) collective-permute-start(bf16[384,4096]{1,0:T(8,128)(2,1)} %halves.3), channel_id=1, source_target_pairs={{0,8},{2,10},{4,12},{6,14},{8,0},{10,2},{12,4},{14,6},{16,24},{18,... | collective-permute-start | bytes 9437192 | tf_op jit(solution)/shard_map/ppermute | solution.py:41
  46.5 29.7 %collective-permute-start.6 = (bf16[512,768]{1,0:T(8,128)(2,1)S(1)}, bf16[512,768]{1,0:T(8,128)(2,1)S(1)}, u32[]{:S(2)}, u32[]{:S(2)}) collective-permute-start(bf16[512,768]{1,0:T(8,128)(2,1)S(1)} %constant_dynamic-slice_fusion.refs_3_), channel_id=1, source_target_pairs={{0,4},{2,6},{4,0},{6,2},{8,12},{10,14},{12,8},{14,10},{16,20},{18,... | collective-permute-start | bytes 2359304 | tf_op jit(solution)/shard_map/ppermute | solution.py:41
  49.5 55.2 %all-to-all-start.1 = ((bf16[4,8,2,64,512]{4,3,2,1,0:T(8,128)(2,1)}), bf16[4,8,2,64,512]{4,3,2,1,0:T(8,128)(2,1)}, u32[]{:S(2)}, u32[]{:S(2)}) async-start(bf16[4,8,2,64,512]{4,3,2,1,0:T(8,128)(2,1)} %broadcast_in_dim.89), calls=%async_computation.1 | async-start | bytes 8388608 | tf_op jit(solution)/shard_map/all_to_all | solution.py:549
  56.1 20.3 %collective-permute-start.4 = (bf16[512,768]{1,0:T(8,128)(2,1)}, bf16[512,768]{1,0:T(8,128)(2,1)S(1)}, u32[]{:S(2)}, u32[]{:S(2)}) collective-permute-start(bf16[512,768]{1,0:T(8,128)(2,1)} %get-tuple-element.147), channel_id=1, source_target_pairs={{0,2},{2,4},{4,6},{6,0},{8,25},{10,27},{12,29},{14,31},{16,18},{18... | collective-permute-start | bytes 2359304 | tf_op jit(solution)/shard_map/ppermute | solution.py:41
  56.6 19.9 %collective-permute-start.5 = (bf16[512,768]{1,0:T(8,128)(2,1)}, bf16[512,768]{1,0:T(8,128)(2,1)}, u32[]{:S(2)}, u32[]{:S(2)}) collective-permute-start(bf16[512,768]{1,0:T(8,128)(2,1)} %get-tuple-element.146), channel_id=1, source_target_pairs={{0,6},{2,0},{4,2},{6,4},{8,25},{10,27},{12,29},{14,31},{16,22},{18... | collective-permute-start | bytes 2359304 | tf_op jit(solution)/shard_map/ppermute | solution.py:41
  66.8 9.7 %copy-start.14 = (bf16[512,768]{1,0:T(8,128)(2,1)S(1)}, bf16[512,768]{1,0:T(8,128)(2,1)}, u32[]{:S(2)}) copy-start(bf16[512,768]{1,0:T(8,128)(2,1)} %copy-done.13) | copy-start | bytes 2359300
  76.6 13.6 %collective-permute-start.8 = (bf16[512,768]{1,0:T(8,128)(2,1)S(1)}, bf16[512,768]{1,0:T(8,128)(2,1)S(1)}, u32[]{:S(2)}, u32[]{:S(2)}) collective-permute-start(bf16[512,768]{1,0:T(8,128)(2,1)S(1)} %broadcast_select_fusion), channel_id=1, source_target_pairs={{0,4},{2,6},{4,0},{6,2},{8,25},{10,27},{12,29},{14,31},{16,20},{18... | collective-permute-start | bytes 2359304 | tf_op jit(solution)/shard_map/ppermute | solution.py:41
  90.2 4.2 %copy-start.24 = (f32[768]{0:T(1024)S(1)}, f32[768]{0:T(1024)}, u32[]{:S(2)}) copy-start(f32[768]{0:T(1024)} %param.11) | copy-start | bytes 9220
  90.2 4.2 %copy-start.25 = (s32[3,1,256]{2,1,0:T(1,128)S(1)}, s32[3,1,256]{2,1,0:T(1,128)}, u32[]{:S(2)}) copy-start(s32[3,1,256]{2,1,0:T(1,128)} %param.16) | copy-start | bytes 9220
  90.2 4.2 %copy-start.26 = (s32[3,1,128]{2,1,0:T(1,128)S(1)}, s32[3,1,128]{2,1,0:T(1,128)}, u32[]{:S(2)}) copy-start(s32[3,1,128]{2,1,0:T(1,128)} %param.14) | copy-start | bytes 4612
  90.2 5.6 %collective-permute-start.9 = (f32[384,768]{1,0:T(8,128)}, f32[384,768]{1,0:T(8,128)S(1)}, u32[]{:S(2)}, u32[]{:S(2)}) collective-permute-start(f32[384,768]{1,0:T(8,128)} %get-tuple-element.89), channel_id=1, source_target_pairs={{0,8},{2,10},{4,12},{6,14},{8,0},{10,2},{12,4},{14,6},{16,24},{18,... | collective-permute-start | bytes 3538952 | tf_op jit(solution)/shard_map/ppermute | solution.py:41
  94.3 3.1 %collective-permute-start.10 = (f32[384,768]{1,0:T(8,128)}, f32[384,768]{1,0:T(8,128)S(1)}, u32[]{:S(2)}, u32[]{:S(2)}) collective-permute-start(f32[384,768]{1,0:T(8,128)} %get-tuple-element.92), channel_id=1, source_target_pairs={{0,8},{2,10},{4,12},{6,14},{8,0},{10,2},{12,4},{14,6},{16,24},{18,... | collective-permute-start | bytes 3538952 | tf_op jit(solution)/shard_map/ppermute | solution.py:41
  98.0 7.8 %copy-start.7 = (bf16[384,512]{1,0:T(8,128)(2,1)}, bf16[384,512]{1,0:T(8,128)(2,1)S(1)}, u32[]{:S(2)}) copy-start(bf16[384,512]{1,0:T(8,128)(2,1)S(1)} %get-tuple-element.93.queries) | copy-start | bytes 1179652
  105.7 20.2 %collective-permute-start.11 = (bf16[4,8,2,64,512]{4,3,2,1,0:T(8,128)(2,1)}, bf16[4,8,2,64,512]{4,3,2,1,0:T(8,128)(2,1)}, u32[]{:S(2)}, u32[]{:S(2)}) collective-permute-start(bf16[4,8,2,64,512]{4,3,2,1,0:T(8,128)(2,1)} %all-to-all-done.1.w.mine), channel_id=1, source_target_pairs={{0,8},{2,10},{4,12},{6,14},{8,0},{10,2},{12,4},{14,6},{16,24},{18,... | collective-permute-start | bytes 12582920 | tf_op jit(solution)/shard_map/ppermute | solution.py:41
  105.7 20.2 %all-to-all-start.2 = ((bf16[16,128,256]{2,1,0:T(8,128)(2,1)}), bf16[16,128,256]{2,1,0:T(8,128)(2,1)S(1)}, u32[]{:S(2)}, u32[]{:S(2)}) async-start(bf16[16,128,256]{2,1,0:T(8,128)(2,1)} %broadcast_in_dim.99), calls=%async_computation.2 | async-start | bytes 2097152 | tf_op jit(solution)/shard_map/all_to_all | solution.py:583
  109.4 10.1 %copy-start.16 = (f32[384,64]{1,0:T(8,128)S(1)}, f32[384,64]{1,0:T(8,128)}, u32[]{:S(2)}) copy-start(f32[384,64]{1,0:T(8,128)} %copy-done.15) | copy-start | bytes 294916
  109.4 10.1 %copy-start.18 = (f32[384,64]{1,0:T(8,128)S(1)}, f32[384,64]{1,0:T(8,128)}, u32[]{:S(2)}) copy-start(f32[384,64]{1,0:T(8,128)} %copy-done.17) | copy-start | bytes 294916
  109.4 10.1 %copy-start.21 = (f32[384,64]{1,0:T(8,128)S(1)}, f32[384,64]{1,0:T(8,128)}, u32[]{:S(2)}) copy-start(f32[384,64]{1,0:T(8,128)} %copy-done.20) | copy-start | bytes 294916
  109.4 10.2 %copy-start.23 = (s32[1,256]{1,0:T(1,128)S(1)}, s32[1,256]{1,0:T(1,128)}, u32[]{:S(2)}) copy-start(s32[1,256]{1,0:T(1,128)} %param.17) | copy-start | bytes 3076
  119.0 1.8 collective-permute-start.12
  119.9 6.1 %copy-start.9 = (bf16[384,512]{1,0:T(8,128)(2,1)S(1)}, bf16[384,512]{1,0:T(8,128)(2,1)}, u32[]{:S(2)}) copy-start(bf16[384,512]{1,0:T(8,128)(2,1)} %copy-done.7) | copy-start | bytes 1179652
  124.1 14.6 %collective-permute-start.15 = (bf16[2,256,512]{2,1,0:T(8,128)(2,1)S(1)}, bf16[2,256,512]{2,1,0:T(8,128)(2,1)S(1)}, u32[]{:S(2)}, u32[]{:S(2)}) collective-permute-start(bf16[2,256,512]{2,1,0:T(8,128)(2,1)S(1)} %get-tuple-element.104.short_att.refs_1_), channel_id=1, source_target_pairs={{0,8},{2,10},{4,12},{6,14},{8,0},{10,2},{12,4},{14,6},{16,24},{18,... | collective-permute-start | bytes 1572872 | tf_op jit(solution)/shard_map/ppermute | solution.py:41
  134.1 4.3 %copy-start.19 = (f32[384,64]{1,0:T(8,128)S(1)}, f32[384,64]{1,0:T(8,128)}, u32[]{:S(2)}) copy-start(f32[384,64]{1,0:T(8,128)} %copy-done.17) | copy-start | bytes 294916
  134.1 4.3 %copy-start.22 = (f32[384,64]{1,0:T(8,128)S(1)}, f32[384,64]{1,0:T(8,128)}, u32[]{:S(2)}) copy-start(f32[384,64]{1,0:T(8,128)} %copy-done.20) | copy-start | bytes 294916
  134.1 4.6 %collective-permute-start.14 = (bf16[2,128,512]{2,1,0:T(8,128)(2,1)S(1)}, bf16[2,128,512]{2,1,0:T(8,128)(2,1)S(1)}, u32[]{:S(2)}, u32[]{:S(2)}) collective-permute-start(bf16[2,128,512]{2,1,0:T(8,128)(2,1)S(1)} %get-tuple-element.105.video_att.refs_0_), channel_id=1, source_target_pairs={{0,8},{2,10},{4,12},{6,14},{8,0},{10,2},{12,4},{14,6},{16,24},{18,... | collective-permute-start | bytes 786440 | tf_op jit(solution)/shard_map/ppermute | solution.py:41
  134.1 27.7 %all-to-all-start.3 = ((bf16[16,128,256]{2,1,0:T(8,128)(2,1)}), bf16[16,128,256]{2,1,0:T(8,128)(2,1)S(1)}, u32[]{:S(2)}, u32[]{:S(2)}) async-start(bf16[16,128,256]{2,1,0:T(8,128)(2,1)} %bitcast.127), calls=%async_computation.3 | async-start | bytes 2097152 | tf_op jit(solution)/shard_map/all_to_all | solution.py:602
  144.1 45.0 %collective-permute-start.16 = (bf16[2,1024,512]{2,1,0:T(8,128)(2,1)}, bf16[2,1024,512]{2,1,0:T(8,128)(2,1)}, u32[]{:S(2)}, u32[]{:S(2)}) collective-permute-start(bf16[2,1024,512]{2,1,0:T(8,128)(2,1)} %term.5), channel_id=1, source_target_pairs={{0,64},{2,66},{4,68},{6,70},{8,12},{10,14},{12,8},{14,10},{16,80},... | collective-permute-start | bytes 6291464 | tf_op jit(solution)/shard_map/ppermute | solution.py:41
  153.0 46.4 %collective-permute-start.17 = (bf16[2,1024,512]{2,1,0:T(8,128)(2,1)}, bf16[2,1024,512]{2,1,0:T(8,128)(2,1)}, u32[]{:S(2)}, u32[]{:S(2)}) collective-permute-start(bf16[2,1024,512]{2,1,0:T(8,128)(2,1)} %term.6), channel_id=1, source_target_pairs={{0,32},{2,34},{4,36},{6,38},{8,10},{10,12},{12,14},{14,8},{16,48},... | collective-permute-start | bytes 6291464 | tf_op jit(solution)/shard_map/ppermute | solution.py:41
  158.9 40.4 %collective-permute-start.18 = (bf16[2,1024,512]{2,1,0:T(8,128)(2,1)}, bf16[2,1024,512]{2,1,0:T(8,128)(2,1)}, u32[]{:S(2)}, u32[]{:S(2)}) collective-permute-start(bf16[2,1024,512]{2,1,0:T(8,128)(2,1)} %term.7), channel_id=1, source_target_pairs={{0,96},{2,98},{4,100},{6,102},{8,14},{10,8},{12,10},{14,12},{16,11... | collective-permute-start | bytes 6291464 | tf_op jit(solution)/shard_map/ppermute | solution.py:41
  162.0 1.7 collective-permute-start.13
  169.7 40.0 %all-to-all-start.4 = ((bf16[4,1040,256]{2,1,0:T(8,128)(2,1)}), bf16[4,1040,256]{2,1,0:T(8,128)(2,1)}, u32[]{:S(2)}, u32[]{:S(2)}) async-start(bf16[4,1040,256]{2,1,0:T(8,128)(2,1)} %key_term.1), calls=%async_computation.4 | async-start | bytes 4259840 | tf_op jit(solution)/shard_map/all_to_all | solution.py:616
  179.6 19.7 %copy-start.12 = (bf16[2,1024,512]{2,1,0:T(8,128)(2,1)S(1)}, bf16[2,1024,512]{2,1,0:T(8,128)(2,1)}, u32[]{:S(2)}) copy-start(bf16[2,1024,512]{2,1,0:T(8,128)(2,1)} %term.4) | copy-start | bytes 6291460
  205.8 18.3 %collective-permute-start.19 = (bf16[2,256,512]{2,1,0:T(8,128)(2,1)}, bf16[2,256,512]{2,1,0:T(8,128)(2,1)S(1)}, u32[]{:S(2)}, u32[]{:S(2)}) collective-permute-start(bf16[2,256,512]{2,1,0:T(8,128)(2,1)} %fusion), channel_id=1, source_target_pairs={{0,4},{2,6},{4,0},{6,2},{8,72},{10,74},{12,76},{14,78},{16,20},{18... | collective-permute-start | bytes 1572872 | tf_op jit(solution)/shard_map/ppermute | solution.py:41
  206.4 17.7 %collective-permute-start.20 = (bf16[2,256,512]{2,1,0:T(8,128)(2,1)}, bf16[2,256,512]{2,1,0:T(8,128)(2,1)S(1)}, u32[]{:S(2)}, u32[]{:S(2)}) collective-permute-start(bf16[2,256,512]{2,1,0:T(8,128)(2,1)} %fusion.1), channel_id=1, source_target_pairs={{0,2},{2,4},{4,6},{6,0},{8,40},{10,42},{12,44},{14,46},{16,18},{18... | collective-permute-start | bytes 1572872 | tf_op jit(solution)/shard_map/ppermute | solution.py:41
  207.9 16.2 %collective-permute-start.21 = (bf16[2,256,512]{2,1,0:T(8,128)(2,1)S(1)}, bf16[2,256,512]{2,1,0:T(8,128)(2,1)}, u32[]{:S(2)}, u32[]{:S(2)}) collective-permute-start(bf16[2,256,512]{2,1,0:T(8,128)(2,1)S(1)} %fusion.2), channel_id=1, source_target_pairs={{0,6},{2,0},{4,2},{6,4},{8,104},{10,106},{12,108},{14,110},{16,22}... | collective-permute-start | bytes 1572872 | tf_op jit(solution)/shard_map/ppermute | solution.py:41
  213.4 21.8 %all-to-all-start.5 = ((bf16[16,80,256]{2,1,0:T(8,128)(2,1)}), bf16[16,80,256]{2,1,0:T(8,128)(2,1)S(1)}, u32[]{:S(2)}, u32[]{:S(2)}) async-start(bf16[16,80,256]{2,1,0:T(8,128)(2,1)} %pad_maximum_fusion), calls=%async_computation.5 | async-start | bytes 1310720 | tf_op jit(solution)/shard_map/all_to_all | solution.py:499
  224.1 14.1 %copy-start.1 = (bf16[1024,768]{1,0:T(8,128)(2,1)S(1)}, bf16[1024,768]{1,0:T(8,128)(2,1)}, u32[]{:S(2)}) copy-start(bf16[1024,768]{1,0:T(8,128)(2,1)} %param.10) | copy-start | bytes 4718596
  226.4 8.9 %collective-permute-start.22 = (bf16[2,64,512]{2,1,0:T(8,128)(2,1)}, bf16[2,64,512]{2,1,0:T(8,128)(2,1)S(1)}, u32[]{:S(2)}, u32[]{:S(2)}) collective-permute-start(bf16[2,64,512]{2,1,0:T(8,128)(2,1)} %get-tuple-element.144), channel_id=1, source_target_pairs={{0,1},{2,3},{4,5},{6,7},{8,9},{10,11},{12,13},{14,15},{16,17},{18,... | collective-permute-start | bytes 393224 | tf_op jit(solution)/shard_map/ppermute | solution.py:41
  228.6 7.6 %collective-permute-start.23 = (bf16[2,64,512]{2,1,0:T(8,128)(2,1)}, bf16[2,64,512]{2,1,0:T(8,128)(2,1)S(1)}, u32[]{:S(2)}, u32[]{:S(2)}) collective-permute-start(bf16[2,64,512]{2,1,0:T(8,128)(2,1)} %get-tuple-element.143), channel_id=1, source_target_pairs={{0,16},{2,18},{4,20},{6,22},{8,24},{10,26},{12,28},{14,30},{16,1},... | collective-permute-start | bytes 393224 | tf_op jit(solution)/shard_map/ppermute | solution.py:41
  229.1 7.1 %collective-permute-start.24 = (bf16[2,64,512]{2,1,0:T(8,128)(2,1)}, bf16[2,64,512]{2,1,0:T(8,128)(2,1)S(1)}, u32[]{:S(2)}, u32[]{:S(2)}) collective-permute-start(bf16[2,64,512]{2,1,0:T(8,128)(2,1)} %get-tuple-element.142), channel_id=1, source_target_pairs={{0,17},{2,19},{4,21},{6,23},{8,25},{10,27},{12,29},{14,31},{16,0},... | collective-permute-start | bytes 393224 | tf_op jit(solution)/shard_map/ppermute | solution.py:41
  (10 other events, 16.7 us)
